TPU v7x, 32 devices: a whole 2x2x4 slice. The times are simulated.
32 devices in a mesh: rows: 8 (over y, x, core), blk: 4 (over z).
Axes of the slice: x: 2, y: 2, z: 4, core: 2. Of those that a mesh axis runs over, the one named last changes fastest.
Arguments:
- image: bfloat16 [4, 8, 96, 512], P('blk', 'rows'), may hold values from -6 to 6
- skip: bfloat16 [4, 16, 192, 512], P('blk', 'rows'), may hold values from -6 to 6
- labels: int32 [4, 16, 192], P('blk', 'rows'), may hold values from 0 to 1
- weight_map: int32 [4, 16, 192], P('blk', 'rows'), may hold values from 2 to 24
- valid: int32 [4, 16, 192], P('blk', 'rows'), may hold values from 0 to 1
- owner: int32 [320], replicated, may hold values from 0 to 319, each once
- master: float32 [4, 320, 128, 128], P('blk', 'rows'), may hold values from -0.0625 to 0.0625
- first_moment: float32 [4, 320, 128, 128], P('blk', 'rows'), may hold values from -0.0014648438 to 0.0014648438
- second_moment: float32 [4, 320, 128, 128], P('blk', 'rows'), may hold values from 8.138021e-10 to 3.2552083e-09
- left_basis: float32 [4, 320, 128, 128], P('blk', 'rows'), may hold values from -1 to 1, as said below
- right_basis: float32 [4, 320, 128, 128], P('blk', 'rows'), may hold values from -1 to 1, as said below
- left_stat: float32 [4, 320, 128, 128], P('blk', 'rows'), as said below
- right_stat: float32 [4, 320, 128, 128], P('blk', 'rows'), as said below
- norm_params: float32 [6144], replicated
- norm_first: float32 [6144], replicated, may hold values from -0.00390625 to 0.00390625
- norm_second: float32 [6144], replicated, may hold values from 8.138021e-09 to 3.2552084e-08
- head_bias: float32 [2], replicated, may hold values from -3 to 3
- bias_first: float32 [2], replicated, may hold values from -0.4375 to 0.4375
- bias_second: float32 [2], replicated, may hold values from 0.0001 to 0.0004
Outputs:
- loss_sum: float32 [], replicated
- valid_count: float32 [], replicated
- new_master: float32 [4, 320, 128, 128], P('blk', 'rows')
- new_copy: bfloat16 [4, 320, 128, 128], P('blk', 'rows')
- new_first: float32 [4, 320, 128, 128], P('blk', 'rows')
- new_second: float32 [4, 320, 128, 128], P('blk', 'rows')
- new_left: float32 [4, 320, 128, 128], P('blk', 'rows')
- new_right: float32 [4, 320, 128, 128], P('blk', 'rows')
- new_left_stat: float32 [4, 320, 128, 128], P('blk', 'rows')
- new_right_stat: float32 [4, 320, 128, 128], P('blk', 'rows')
- new_norm_first: float32 [6144], replicated
- new_norm_second: float32 [6144], replicated
- new_norm: float32 [6144], replicated
- new_bias_first: float32 [2], replicated
- new_bias_second: float32 [2], replicated
- new_bias: float32 [2], replicated
Inputs may be any that keep to these rules, and one draw needn't show every extreme that they name: `owner`: the device at index r of rows owns slots r * 40 to (r + 1) * 40 - 1; every block is in one slot. `left_basis`: each block is orthogonal. `right_basis`: each block is orthogonal. `left_stat`: each block is symmetric positive definite. `right_stat`: each block is symmetric positive definite.
All inputs are finite; a program needn't handle non-finite values.
Results may differ from a plain program's by a relative error of at most 0.0034.
The roundings to bfloat16 on the way count: a program that leaves them out, or rounds other values in their place, can miss the bound.
Values may be sent and summed in bfloat16 or wider, within the bound.
A program may use at most 320 MiB of HBM per device.

v0:
```python
from functools import reduce

import jax
import jax.numpy as jnp
from jax import lax
from jax.sharding import PartitionSpec as P

C0 = 512
C1 = 1024
GROUPS = 32
STEP = 10


beta_one = 0.9
beta_two = 0.999
beta_stat = 0.95
adam_eps = 1e-08
norm_eps = 1e-05
soap_rate = 0.008
soap_decay = 0.01
small_rate = 0.4
small_decay = 0.01
highest = lax.Precision.HIGHEST


def padded_2(block, sides, width):
    for axis, dim in sides:
        count = lax.axis_size(axis)
        forward = [(i, i + 1) for i in range(count - 1)]
        backward = [(target, source) for source, target in forward]
        low = lax.ppermute(
            lax.slice_in_dim(block, block.shape[dim] - width, None, axis=dim), axis, forward
        )
        high = lax.ppermute(lax.slice_in_dim(block, 0, width, axis=dim), axis, backward)
        block = jnp.concatenate([low, block, high], axis=dim)
    return block


def from_blocks(blocks, out_rows, taps, in_width):
    order = blocks.shape[-1]
    split = blocks.reshape(out_rows // order, taps, in_width // order, order, order)
    return split.transpose(0, 3, 1, 2, 4).reshape(out_rows, taps, in_width)


def to_blocks(weight, order):
    out_rows, taps, in_width = weight.shape
    split = weight.reshape(out_rows // order, order, taps, in_width // order, order)
    return split.transpose(0, 2, 3, 1, 4).reshape(-1, order, order)


def pad_rows(values):
    padded = padded_2(values, (("rows", 1),), 1)
    return jnp.pad(padded, ((0, 0), (0, 0), (1, 1), (0, 0)))


def tap_views(padded, height, width, flipped):
    views = []
    for row_off in range(3):
        for col_off in range(3):
            first_row = 2 - row_off if flipped else row_off
            first_col = 2 - col_off if flipped else col_off
            window = padded[:, first_row : first_row + height, first_col : first_col + width, :]
            views.append(window.reshape(-1, padded.shape[-1]))
    return views


def make_views(source, height, width, summed):
    if summed:
        return tap_views(source, height, width, False)
    return [source.reshape(-1, source.shape[-1])] * 4


def tap_products(views, piece, summed):
    terms = [
        lax.dot_general(
            views[tap],
            piece[:, tap, :],
            (((1,), (1,)), ((), ())),
            preferred_element_type=jnp.float32,
        )
        for tap in range(len(views))
    ]
    if summed:
        return reduce(lambda left, right: left + right, terms)
    return jnp.stack(terms, 1)


def forward_conv(source, shard, height, width, summed):
    views = make_views(source, height, width, summed)
    result = tap_products(views, lax.all_gather(shard, "blk", axis=0, tiled=True), summed)
    return (result, views)


def input_grad(grad_views, shard, keep):
    taps = len(grad_views)
    initial = jnp.zeros((grad_views[0].shape[0], keep), jnp.float32)
    carry = initial
    piece = lax.all_gather(shard, "blk", axis=0, tiled=True)
    for tap in range(taps):
        window = grad_views[tap]
        carry = carry + jnp.dot(window, piece[:, tap, :keep], preferred_element_type=jnp.float32)
    return carry


def weight_grad(pairs):
    parts = [
        lax.dot_general(
            grad_view, in_view, (((0,), (0,)), ((), ())), preferred_element_type=jnp.float32
        )
        for grad_view, in_view in pairs
    ]
    return lax.psum_scatter(
        jnp.stack(parts, 1).astype(jnp.bfloat16), "blk", scatter_dimension=0, tiled=True
    ).astype(jnp.float32)


def backward_conv(grad, views, shard, keep, spatial, need_input):
    chans = grad.shape[-1]
    if spatial:
        flat = grad.reshape(-1, chans)
        pairs = [(flat, view) for view in views]
        grad_views = tap_views(pad_rows(grad), grad.shape[1], grad.shape[2], True)
    else:
        grad_views = [grad[:, tap, :] for tap in range(4)]
        pairs = list(zip(grad_views, views))
    weight_part = weight_grad(pairs)
    if not need_input:
        return (weight_part, None)
    return (weight_part, input_grad(grad_views, shard, keep))


def group_forward(values, gain, shift, total_rows):
    images, height, width, chans = values.shape
    part = values.reshape(images, height, width, GROUPS, chans // GROUPS)
    first_sum = jnp.sum(part, axis=(1, 2, 4))
    second_sum = jnp.sum(part * part, axis=(1, 2, 4))
    first_sum, second_sum = lax.psum((first_sum, second_sum), "rows")
    number = total_rows * width * (chans // GROUPS)
    mean = first_sum / number
    variance = second_sum / number - mean * mean
    inv_scale = lax.rsqrt(variance + norm_eps)[:, None, None, :, None]
    zhat = ((part - mean[:, None, None, :, None]) * inv_scale).reshape(values.shape)
    normed = zhat * gain + shift
    return (normed * jax.nn.sigmoid(normed), (zhat, inv_scale, normed))


def group_backward(grad_act, saved, gain, total_rows):
    zhat, inv_scale, normed = saved
    images, height, width, chans = zhat.shape
    sigmoid_y = jax.nn.sigmoid(normed)
    grad_y = grad_act * sigmoid_y * (1.0 + normed * (1.0 - sigmoid_y))
    gain_grad = jnp.sum(grad_y * zhat, axis=(0, 1, 2))
    shift_grad = jnp.sum(grad_y, axis=(0, 1, 2))
    grad_hat = (grad_y * gain).reshape(images, height, width, GROUPS, chans // GROUPS)
    zpart = zhat.reshape(grad_hat.shape)
    grad_sum = jnp.sum(grad_hat, axis=(1, 2, 4))
    cross_sum = jnp.sum(grad_hat * zpart, axis=(1, 2, 4))
    grad_sum, cross_sum = lax.psum((grad_sum, cross_sum), "rows")
    number = total_rows * width * (chans // GROUPS)
    grad_pre = (
        grad_hat
        - (grad_sum / number)[:, None, None, :, None]
        - zpart * (cross_sum / number)[:, None, None, :, None]
    ) * inv_scale
    return (grad_pre.reshape(zhat.shape).astype(jnp.bfloat16), gain_grad, shift_grad)


def orthonormal(stat, basis):
    product = jnp.matmul(stat, basis, precision=highest)
    gram = jnp.matmul(jnp.swapaxes(product, -1, -2), product, precision=highest)
    factor = jnp.linalg.cholesky(gram)
    order = product.shape[-1]
    flat_factor = factor.reshape(-1, order, order)
    flat_product = product.reshape(-1, order, order)
    solved = jax.vmap(
        lambda lower, right: jax.scipy.linalg.solve_triangular(lower, right.T, lower=True)
    )(flat_factor, flat_product)
    return jnp.swapaxes(solved, -1, -2).reshape(product.shape)


def soap_update(grads, master, first, second, left, right, left_stat, right_stat):
    rotated = jnp.matmul(
        jnp.matmul(jnp.swapaxes(left, -1, -2), grads, precision=highest), right, precision=highest
    )
    first_new = beta_one * first + (1.0 - beta_one) * rotated
    second_new = beta_two * second + (1.0 - beta_two) * rotated * rotated
    direction = (
        first_new
        / (1.0 - beta_one**STEP)
        / (jnp.sqrt(second_new / (1.0 - beta_two**STEP)) + adam_eps)
    )
    update = jnp.matmul(
        jnp.matmul(left, direction, precision=highest),
        jnp.swapaxes(right, -1, -2),
        precision=highest,
    )
    master_new = master - soap_rate * (update + soap_decay * master)
    left_new_stat = beta_stat * left_stat + (1.0 - beta_stat) * jnp.matmul(
        grads, jnp.swapaxes(grads, -1, -2), precision=highest
    )
    right_new_stat = beta_stat * right_stat + (1.0 - beta_stat) * jnp.matmul(
        jnp.swapaxes(grads, -1, -2), grads, precision=highest
    )
    return (
        master_new,
        first_new,
        second_new,
        orthonormal(left_new_stat, left),
        orthonormal(right_new_stat, right),
        left_new_stat,
        right_new_stat,
    )


def adam_small(grads, value, first, second):
    first_new = beta_one * first + (1.0 - beta_one) * grads
    second_new = beta_two * second + (1.0 - beta_two) * grads * grads
    direction = (
        first_new
        / (1.0 - beta_one**STEP)
        / (jnp.sqrt(second_new / (1.0 - beta_two**STEP)) + adam_eps)
    )
    return (first_new, second_new, value - small_rate * (direction + small_decay * value))


def local(
    image,
    skip,
    labels,
    weight_map,
    valid,
    owner,
    master,
    first_moment,
    second_moment,
    left_basis,
    right_basis,
    left_stat,
    right_stat,
    norm_params,
    norm_first,
    norm_second,
    head_bias,
    bias_first,
    bias_second,
):
    shards = lax.axis_size("blk")
    images, low_rows, low_cols = (image.shape[0], image.shape[1], image.shape[2])
    high_rows, high_cols = (2 * low_rows, 2 * low_cols)
    total_rows = low_rows * lax.axis_size("rows")
    order = master.shape[-1]
    layers = ((C0, C1, 9), (C1, C1, 9), (C1, C0, 4), (2 * C0, C0, 9))
    copies = lax.all_gather(master.astype(jnp.bfloat16), "rows", axis=1, tiled=True)[0]
    ordered = copies[jnp.argsort(owner)]
    shard_list = []
    offset = 0
    for in_width, out_width, taps in layers:
        out_rows = out_width // shards
        number = out_rows // order * taps * (in_width // order)
        shard_list.append(from_blocks(ordered[offset : offset + number], out_rows, taps, in_width))
        offset = offset + number
    marks = (0, C1, 2 * C1, 3 * C1, 4 * C1, 4 * C1 + C0, 4 * C1 + 2 * C0)
    pieces = [norm_params[marks[index] : marks[index + 1]] for index in range(6)]
    head_low = norm_params[marks[6] :].reshape(C0, 2).astype(jnp.bfloat16)
    pre_one, views_one = forward_conv(pad_rows(image), shard_list[0], low_rows, low_cols, True)
    act_one, saved_one = group_forward(
        pre_one.reshape(images, low_rows, low_cols, C1), pieces[0], pieces[1], total_rows
    )
    pre_two, views_two = forward_conv(
        pad_rows(act_one.astype(jnp.bfloat16)), shard_list[1], low_rows, low_cols, True
    )
    act_two, saved_two = group_forward(
        pre_two.reshape(images, low_rows, low_cols, C1), pieces[2], pieces[3], total_rows
    )
    up_taps, views_up = forward_conv(
        act_two.astype(jnp.bfloat16), shard_list[2], low_rows, low_cols, False
    )
    upsampled = up_taps.reshape(images, low_rows, low_cols, 2, 2, C0).transpose(0, 1, 3, 2, 4, 5)
    upsampled = upsampled.reshape(images, high_rows, high_cols, C0).astype(jnp.bfloat16)
    joined = jnp.concatenate([upsampled, skip], -1)
    pre_three, views_three = forward_conv(
        pad_rows(joined), shard_list[3], high_rows, high_cols, True
    )
    act_three, saved_three = group_forward(
        pre_three.reshape(images, high_rows, high_cols, C0), pieces[4], pieces[5], 2 * total_rows
    )
    flat_three = act_three.astype(jnp.bfloat16).reshape(-1, C0)
    logits = jnp.dot(flat_three, head_low, preferred_element_type=jnp.float32) + head_bias
    targets = (labels.reshape(-1, 1) == jnp.arange(2)[None, :]).astype(jnp.float32)
    valid_flat = valid.reshape(-1).astype(jnp.float32)
    scales = valid_flat * weight_map.reshape(-1).astype(jnp.float32) * 0.125
    largest = jnp.max(logits, -1, keepdims=True)
    log_total = jnp.log(jnp.sum(jnp.exp(logits - largest), -1, keepdims=True)) + largest
    losses = log_total[:, 0] - jnp.sum(logits * targets, -1)
    loss_sum, valid_count = lax.psum(
        (jnp.sum(scales * losses), jnp.sum(valid_flat)), ("rows", "blk")
    )
    grad_logits = (jnp.exp(logits - log_total) - targets) * (scales / valid_count)[:, None]
    grad_head = jnp.dot(flat_three.astype(jnp.float32).T, grad_logits, precision=highest)
    grad_bias = jnp.sum(grad_logits, 0)
    grad_act = jnp.dot(grad_logits, head_low.astype(jnp.float32).T, precision=highest)
    grad_pre, gain_three, shift_three = group_backward(
        grad_act.reshape(images, high_rows, high_cols, C0), saved_three, pieces[4], 2 * total_rows
    )
    grad_four, grad_joined = backward_conv(grad_pre, views_three, shard_list[3], C0, True, True)
    grad_up = grad_joined.astype(jnp.bfloat16).reshape(images, low_rows, 2, low_cols, 2, C0)
    grad_up = grad_up.transpose(0, 1, 3, 2, 4, 5).reshape(-1, 4, C0)
    grad_three, grad_act = backward_conv(grad_up, views_up, shard_list[2], C1, False, True)
    grad_pre, gain_two, shift_two = group_backward(
        grad_act.reshape(images, low_rows, low_cols, C1), saved_two, pieces[2], total_rows
    )
    grad_two, grad_act = backward_conv(grad_pre, views_two, shard_list[1], C1, True, True)
    grad_pre, gain_one, shift_one = group_backward(
        grad_act.reshape(images, low_rows, low_cols, C1), saved_one, pieces[0], total_rows
    )
    grad_one, unused = backward_conv(grad_pre, views_one, shard_list[0], C0, True, False)
    blocks = jnp.concatenate(
        [to_blocks(grad, order) for grad in (grad_one, grad_two, grad_three, grad_four)], 0
    )
    grads = lax.psum_scatter(blocks[owner], "rows", scatter_dimension=0, tiled=True)[None]
    small = jnp.concatenate(
        [gain_one, shift_one, gain_two, shift_two, gain_three, shift_three, grad_head.reshape(-1)]
    )
    small, grad_bias = lax.psum((small, grad_bias), ("rows", "blk"))
    soap = soap_update(
        grads, master, first_moment, second_moment, left_basis, right_basis, left_stat, right_stat
    )
    norm_new = adam_small(small, norm_params, norm_first, norm_second)
    bias_new = adam_small(grad_bias, head_bias, bias_first, bias_second)
    return (
        loss_sum,
        valid_count,
        soap[0],
        soap[0].astype(jnp.bfloat16),
        soap[1],
        soap[2],
        soap[3],
        soap[4],
        soap[5],
        soap[6],
        norm_new[0],
        norm_new[1],
        norm_new[2],
        bias_new[0],
        bias_new[1],
        bias_new[2],
    )


def solution(mesh):
    placed = (
        P("blk", "rows", None, None),
        P("blk", "rows", None, None),
        P("blk", "rows", None),
        P("blk", "rows", None),
        P("blk", "rows", None),
        P(),
        P("blk", "rows", None, None),
        P("blk", "rows", None, None),
        P("blk", "rows", None, None),
        P("blk", "rows", None, None),
        P("blk", "rows", None, None),
        P("blk", "rows", None, None),
        P("blk", "rows", None, None),
        P(),
        P(),
        P(),
        P(),
        P(),
        P(),
    )
    return jax.shard_map(
        local,
        mesh=mesh,
        in_specs=placed,
        out_specs=(
            P(),
            P(),
            P("blk", "rows", None, None),
            P("blk", "rows", None, None),
            P("blk", "rows", None, None),
            P("blk", "rows", None, None),
            P("blk", "rows", None, None),
            P("blk", "rows", None, None),
            P("blk", "rows", None, None),
            P("blk", "rows", None, None),
            P(),
            P(),
            P(),
            P(),
            P(),
            P(),
        ),
        check_vma=False,
    )
```

profile of v0, /device:TPU:1, one launch (start us, length us, event | category | flops | bytes accessed | tf_op | source)
XLA Modules:
  0.0 3706.2 jit_solution(2790353739672517691)
XLA Ops:
  14.3 62.1 %all-gather.6.cloned.1.call-done = bf16[1,320,128,128]{3,2,0,1:T(8,128)(2,1)} async-done(((bf16[1,40,128,128]{3,2,0,1:T(8,128)(2,1)}), bf16[1,320,128,128]{3,2,0,1:T(8,128)(2,1)}) %all-gather.6.cloned.1.call-update) | async-done | bytes 10485776 | tf_op jit(solution)/shard_map/all_gather | solution.py:253
  76.4 14.7 gather_fusion
  138.7 132.8 %all-gather.8.cloned.1.call-done = bf16[1024,9,512]{2,0,1:T(8,128)(2,1)} async-done(((bf16[256,9,512]{2,0,1:T(8,128)(2,1)}), bf16[1024,9,512]{2,0,1:T(8,128)(2,1)}) %all-gather.8.cloned.1.call-update) | async-done | bytes 9437200 | tf_op jit(solution)/shard_map/all_gather | solution.py:90
  287.9 12.3 all-reduce.11
  312.1 281.6 %all-gather.10.cloned.1.call-done = bf16[1024,9,1024]{2,0,1:T(8,128)(2,1)} async-done(((bf16[256,9,1024]{2,0,1:T(8,128)(2,1)}), bf16[1024,9,1024]{2,0,1:T(8,128)(2,1)}) %all-gather.10.cloned.1.call-update) | async-done | bytes 18874384 | tf_op jit(solution)/shard_map/all_gather | solution.py:90
  616.1 12.2 all-reduce.10
  628.8 46.4 %all-gather.12.cloned.1.call-done = bf16[512,4,1024]{0,2,1:T(8,128)(2,1)} async-done(((bf16[128,4,1024]{0,2,1:T(8,128)(2,1)}), bf16[512,4,1024]{0,2,1:T(8,128)(2,1)}) %all-gather.12.cloned.1.call-update) | async-done | bytes 4194320 | tf_op jit(solution)/shard_map/all_gather | solution.py:90
  695.3 146.5 %all-gather.14.cloned.1.call-done = bf16[512,9,1024]{0,2,1:T(8,128)(2,1)} async-done(((bf16[128,9,1024]{0,2,1:T(8,128)(2,1)}), bf16[512,9,1024]{0,2,1:T(8,128)(2,1)}) %all-gather.14.cloned.1.call-update) | async-done | bytes 9437200 | tf_op jit(solution)/shard_map/all_gather | solution.py:90
  856.6 11.8 all-reduce.9
  875.8 38.9 %psum.119 = f32[]{:T(128)} all-reduce(f32[]{:T(128)} %get-tuple-element.106), channel_id=1, replica_groups=mesh['rows'=8,'blk'=4] {'rows','blk'}, use_global_device_ids=true, to_apply=%region_25.26 | all-reduce | flops 1 | bytes 8 | tf_op jit(solution)/shard_map/psum | solution.py:295
  923.0 12.4 all-reduce.8
  993.0 13.8 all-reduce.7
  1039.8 14.0 all-reduce.6
  1093.7 116.1 %reduce-scatter.12.cloned.1.call-done = bf16[128,9,1024]{2,0,1:T(8,128)(2,1)} async-done(((bf16[512,9,1024]{2,0,1:T(8,128)(2,1)}), bf16[128,9,1024]{2,0,1:T(8,128)(2,1)}) %reduce-scatter.12.cloned.1.call-update) | async-done | bytes 2359312 | tf_op jit(solution)/shard_map/reduce_scatter | solution.py:112
  1214.2 160.2 %reduce-scatter.6.cloned.1.call-done = bf16[256,9,512]{2,0,1:T(8,128)(2,1)} async-done(((bf16[1024,9,512]{2,0,1:T(8,128)(2,1)}), bf16[256,9,512]{2,0,1:T(8,128)(2,1)}) %reduce-scatter.6.cloned.1.call-update) | async-done | bytes 2359312 | tf_op jit(solution)/shard_map/reduce_scatter | solution.py:112
  1383.3 308.4 %reduce-scatter.8.cloned.1.call-done = bf16[256,9,1024]{2,0,1:T(8,128)(2,1)} async-done(((bf16[1024,9,1024]{2,0,1:T(8,128)(2,1)}), bf16[256,9,1024]{2,0,1:T(8,128)(2,1)}) %reduce-scatter.8.cloned.1.call-update) | async-done | bytes 4718608 | tf_op jit(solution)/shard_map/reduce_scatter | solution.py:112
  1698.0 11.0 maximum_convert_fusion
  1709.0 20.8 gather_fusion.1
  1731.6 41.4 %all-reduce.5 = (f32[]{:T(128)}, f32[6144]{0:T(1024)S(1)}, f32[2]{0:T(128)S(1)}) all-reduce(f32[]{:T(128)} %get-tuple-element.107, f32[6144]{0:T(1024)S(1)} %constant_dynamic-update-slice_fusion.3, f32[2]{0:T(128)S(1)} %copy-done.94), channel_id=1, replica_groups=mesh['rows'=8,'blk'=4] {'rows','blk'}, use_global_device_ids=true, to_apply=%region_23.24 | all-reduce | flops 6147 | bytes 49176 | tf_op jit(solution)/shard_map/psum | solution.py:295
  1774.2 93.2 %reduce-scatter.14.cloned.1.call-done = f32[40,128,128]{2,1,0:T(8,128)} async-done(((f32[320,128,128]{2,1,0:T(8,128)}), f32[40,128,128]{2,1,0:T(8,128)}) %reduce-scatter.14.cloned.1.call-update) | async-done | bytes 2621456 | tf_op jit(solution)/shard_map/reduce_scatter | solution.py:320
  1922.3 470.6 %custom-call.10 = f32[1,40,128,128]{3,2,1,0:T(8,128)} custom-call(f32[1,40,128,128]{3,2,1,0:T(8,128)} %fusion.15), custom_call_target="Cholesky" | custom-call | tf_op jit(solution)/shard_map/jit(cholesky)/cholesky | solution.py:171
  2409.1 470.6 %custom-call.8 = f32[1,40,128,128]{3,2,1,0:T(8,128)} custom-call(f32[1,40,128,128]{3,2,1,0:T(8,128)} %fusion.16), custom_call_target="Cholesky" | custom-call | tf_op jit(solution)/shard_map/jit(cholesky)/cholesky | solution.py:171
  2886.8 394.4 %custom-call.9 = f32[40,1,128,128]{2,3,1,0:T(8,128)} custom-call(f32[40,1,128,128]{3,2,1,0:T(8,128)} %get-tuple-element.164), custom_call_target="InvertDiagBlocksLowerTriangular" | custom-call | tf_op jit(solution)/shard_map/vmap(jit(_solve_triangular))/triangular_solve | solution.py:176
  3293.0 394.4 %custom-call.11 = f32[40,1,128,128]{2,3,1,0:T(8,128)} custom-call(f32[40,1,128,128]{3,2,1,0:T(8,128)} %get-tuple-element.163), custom_call_target="InvertDiagBlocksLowerTriangular" | custom-call | tf_op jit(solution)/shard_map/vmap(jit(_solve_triangular))/triangular_solve | solution.py:176
  (487 shorter events, 409.1 us)
Async XLA Ops:
  7.2 1867.3 %copy-start = (f32[1,40,128,128]{3,2,1,0:T(8,128)S(1)}, f32[1,40,128,128]{3,2,1,0:T(8,128)}, u32[]{:S(2)}) copy-start(f32[1,40,128,128]{3,2,1,0:T(8,128)} %param.32) | copy-start | bytes 7864324
  7.2 69.2 %all-gather.6.cloned.1.call-start = ((), (), s32[]{:S(2)}) async-start(), calls=%async_computation.5 | async-start | bytes 11796480 | tf_op jit(solution)/shard_map/all_gather | solution.py:253
  10.4 261.1 %all-gather.8.cloned.1.call-start = ((), (), s32[]{:S(2)}) async-start(), calls=%async_computation.6 | async-start | bytes 11796480 | tf_op jit(solution)/shard_map/all_gather | solution.py:90
  104.8 488.9 %all-gather.10.cloned.1.call-start = ((), (), s32[]{:S(2)}) async-start(), calls=%async_computation.7 | async-start | bytes 23592960 | tf_op jit(solution)/shard_map/all_gather | solution.py:90
  122.1 553.2 %all-gather.12.cloned.1.call-start = ((), (), s32[]{:S(2)}) async-start(), calls=%async_computation.8 | async-start | bytes 5242880 | tf_op jit(solution)/shard_map/all_gather | solution.py:90
  127.0 714.8 %all-gather.14.cloned.1.call-start = ((), (), s32[]{:S(2)}) async-start(), calls=%async_computation.9 | async-start | bytes 11796480 | tf_op jit(solution)/shard_map/all_gather | solution.py:90
  131.4 959.6 %reduce-scatter.10.cloned.1.call-start = ((), (), s32[]{:S(2)}) async-start(), calls=%async_computation.12 | async-start | bytes 5242880 | tf_op jit(solution)/shard_map/reduce_scatter | solution.py:112
  131.5 6.3 collective-permute-start.1
  133.7 5.0 collective-permute-start
  137.6 162.8 %copy-start.81 = (f32[1024]{0:T(1024)}, f32[1024]{0:T(1024)S(1)}, u32[]{:S(2)}) copy-start(f32[1024]{0:T(1024)S(1)} %get-tuple-element.161) | copy-start | bytes 12292
  301.3 8.9 collective-permute-start.3
  306.0 4.9 collective-permute-start.2
  310.9 287.6 %copy-start.40 = (bf16[1,1,96,1024]{3,2,1,0:T(8,128)(2,1)}, bf16[1,1,96,1024]{3,2,1,0:T(8,128)(2,1)S(1)}, u32[]{:S(2)}) copy-start(bf16[1,1,96,1024]{3,2,1,0:T(8,128)(2,1)S(1)} %collective-permute-done.2) | copy-start | bytes 589828
  312.1 298.8 %copy-start.16 = (bf16[1,3,98,1024]{3,2,1,0:T(8,128)(2,1)}, bf16[1,3,98,1024]{3,2,1,0:T(8,128)(2,1)S(1)}, u32[]{:S(2)}) copy-start(bf16[1,3,98,1024]{3,2,1,0:T(8,128)(2,1)S(1)} %select_maximum_fusion.2) | copy-start | bytes 1806340
  686.8 157.1 %collective-permute-start.5 = (bf16[1,1,192,1024]{3,2,1,0:T(8,128)(2,1)}, bf16[1,1,192,1024]{3,2,1,0:T(8,128)(2,1)}, u32[]{:S(2)}, u32[]{:S(2)}) collective-permute-start(bf16[1,1,192,1024]{3,2,1,0:T(8,128)(2,1)} %get-tuple-element.152), channel_id=1, source_target_pairs={{4,0},{8,4},{12,8},{16,12},{20,16},{24,20},{28,24},{5,1},{9,5},{13... | collective-permute-start | bytes 1179656 | tf_op jit(solution)/shard_map/ppermute | solution.py:34
  689.2 154.7 %collective-permute-start.4 = (bf16[1,1,192,1024]{3,2,1,0:T(8,128)(2,1)}, bf16[1,1,192,1024]{3,2,1,0:T(8,128)(2,1)}, u32[]{:S(2)}, u32[]{:S(2)}) collective-permute-start(bf16[1,1,192,1024]{3,2,1,0:T(8,128)(2,1)} %get-tuple-element.151), channel_id=1, source_target_pairs={{0,4},{4,8},{8,12},{12,16},{16,20},{20,24},{24,28},{1,5},{5,9},{9,... | collective-permute-start | bytes 1179656 | tf_op jit(solution)/shard_map/ppermute | solution.py:31
  937.4 7.0 collective-permute-start.7
  941.1 4.5 collective-permute-start.6
  967.1 242.7 %reduce-scatter.12.cloned.1.call-start = ((), (), s32[]{:S(2)}) async-start(), calls=%async_computation.13 | async-start | bytes 11796480 | tf_op jit(solution)/shard_map/reduce_scatter | solution.py:112
  984.2 390.2 %reduce-scatter.6.cloned.1.call-start = ((), (), s32[]{:S(2)}) async-start(), calls=%async_computation.10 | async-start | bytes 11796480 | tf_op jit(solution)/shard_map/reduce_scatter | solution.py:112
  1008.3 7.4 collective-permute-start.9
  1010.4 6.1 collective-permute-start.8
  1070.4 621.3 %reduce-scatter.8.cloned.1.call-start = ((), (), s32[]{:S(2)}) async-start(), calls=%async_computation.11 | async-start | bytes 23592960 | tf_op jit(solution)/shard_map/reduce_scatter | solution.py:112
  1090.3 777.2 %reduce-scatter.14.cloned.1.call-start = ((), (), s32[]{:S(2)}) async-start(), calls=%async_computation.14 | async-start | bytes 23592960 | tf_op jit(solution)/shard_map/reduce_scatter | solution.py:320
  (99 other events, 1737.6 us)
Sparse Core Ops, SparseCore 0:
  10.6 65.8 all-gather.5
  104.9 166.5 all-gather.7
  273.1 320.5 all-gather.9
  595.7 79.5 all-gather.11
  677.3 164.4 all-gather.13
  967.2 78.6 reduce-scatter.9
  1048.3 161.4 reduce-scatter.11
  1212.3 162.0 reduce-scatter.5
  1376.9 314.8 reduce-scatter.7
  1730.0 137.3 reduce-scatter.13
where the time goes:
time: 3720 us; the launch traced here: 3710 us
  other arithmetic  1790 us (48%)
  waiting for transfers between devices  1350 us (36%)
  matrix products  221 us (6%)
  blocking collectives  157 us (4%)
  local copies, waits for them, and re-layouts  141 us (4%)
    another operation x6, other arithmetic, orthonormal(): factor = jnp.linalg.cholesky(gram)  945 us
    another operation x4, other arithmetic, orthonormal(): jax.scipy.linalg.solve_triangular(lower, right.T, lower=True)  792 us
    all_gather x4, waiting for transfers between devices, forward_conv(): lax.all_gather(shard, 'blk', axis=0, tiled=True)  607 us
    reduce_scatter x4, waiting for transfers between devices, weight_grad(): lax.psum_scatter(jnp.stack(parts, 1).astype(jnp.bfloat16), 'blk', scatter...  585 us
    reduce_scatter x1, waiting for transfers between devices, local(): lax.psum_scatter(blocks[owner], 'rows', scatter_dimension=0, tiled=True)  93.2 us
    psum x2, blocking collectives, local(): lax.psum((jnp.sum(scales * losses), jnp.sum(valid_flat)), ('rows', 'blk'))  80.3 us
  transfers between devices with their start and end apart: 20, of which 15 were waited for; matrix products, arithmetic and copies ran while one was open for 5% of the time, Pallas kernels for 0%

commit v1 on v0

--- a/solution.py
+++ b/solution.py
@@ -3,6 +3,8 @@
 import jax
 import jax.numpy as jnp
 from jax import lax
+from jax.experimental import pallas as pl
+from jax.experimental.pallas import tpu as pltpu
 from jax.sharding import PartitionSpec as P
 
 C0 = 512
@@ -87,19 +89,16 @@
 
 def forward_conv(source, shard, height, width, summed):
     views = make_views(source, height, width, summed)
-    result = tap_products(views, lax.all_gather(shard, "blk", axis=0, tiled=True), summed)
-    return (result, views)
+    return (tap_products(views, shard, summed), views)
 
 
 def input_grad(grad_views, shard, keep):
-    taps = len(grad_views)
-    initial = jnp.zeros((grad_views[0].shape[0], keep), jnp.float32)
-    carry = initial
-    piece = lax.all_gather(shard, "blk", axis=0, tiled=True)
-    for tap in range(taps):
-        window = grad_views[tap]
-        carry = carry + jnp.dot(window, piece[:, tap, :keep], preferred_element_type=jnp.float32)
-    return carry
+    carry = jnp.zeros((grad_views[0].shape[0], keep), jnp.float32)
+    for tap in range(len(grad_views)):
+        carry = carry + jnp.dot(
+            grad_views[tap], shard[:, tap, :keep], preferred_element_type=jnp.float32
+        )
+    return lax.psum_scatter(carry, "blk", scatter_dimension=1, tiled=True)
 
 
 def weight_grad(pairs):
@@ -109,9 +108,7 @@
         )
         for grad_view, in_view in pairs
     ]
-    return lax.psum_scatter(
-        jnp.stack(parts, 1).astype(jnp.bfloat16), "blk", scatter_dimension=0, tiled=True
-    ).astype(jnp.float32)
+    return jnp.stack(parts, 1)
 
 
 def backward_conv(grad, views, shard, keep, spatial, need_input):
@@ -129,13 +126,13 @@
     return (weight_part, input_grad(grad_views, shard, keep))
 
 
-def group_forward(values, gain, shift, total_rows):
+def group_forward(values, gain, shift, total_rows, groups):
     images, height, width, chans = values.shape
-    part = values.reshape(images, height, width, GROUPS, chans // GROUPS)
+    part = values.reshape(images, height, width, groups, chans // groups)
     first_sum = jnp.sum(part, axis=(1, 2, 4))
     second_sum = jnp.sum(part * part, axis=(1, 2, 4))
     first_sum, second_sum = lax.psum((first_sum, second_sum), "rows")
-    number = total_rows * width * (chans // GROUPS)
+    number = total_rows * width * (chans // groups)
     mean = first_sum / number
     variance = second_sum / number - mean * mean
     inv_scale = lax.rsqrt(variance + norm_eps)[:, None, None, :, None]
@@ -144,19 +141,19 @@
     return (normed * jax.nn.sigmoid(normed), (zhat, inv_scale, normed))
 
 
-def group_backward(grad_act, saved, gain, total_rows):
+def group_backward(grad_act, saved, gain, total_rows, groups):
     zhat, inv_scale, normed = saved
     images, height, width, chans = zhat.shape
     sigmoid_y = jax.nn.sigmoid(normed)
     grad_y = grad_act * sigmoid_y * (1.0 + normed * (1.0 - sigmoid_y))
     gain_grad = jnp.sum(grad_y * zhat, axis=(0, 1, 2))
     shift_grad = jnp.sum(grad_y, axis=(0, 1, 2))
-    grad_hat = (grad_y * gain).reshape(images, height, width, GROUPS, chans // GROUPS)
+    grad_hat = (grad_y * gain).reshape(images, height, width, groups, chans // groups)
     zpart = zhat.reshape(grad_hat.shape)
     grad_sum = jnp.sum(grad_hat, axis=(1, 2, 4))
     cross_sum = jnp.sum(grad_hat * zpart, axis=(1, 2, 4))
     grad_sum, cross_sum = lax.psum((grad_sum, cross_sum), "rows")
-    number = total_rows * width * (chans // GROUPS)
+    number = total_rows * width * (chans // groups)
     grad_pre = (
         grad_hat
         - (grad_sum / number)[:, None, None, :, None]
@@ -165,17 +162,112 @@
     return (grad_pre.reshape(zhat.shape).astype(jnp.bfloat16), gain_grad, shift_grad)
 
 
-def orthonormal(stat, basis):
-    product = jnp.matmul(stat, basis, precision=highest)
-    gram = jnp.matmul(jnp.swapaxes(product, -1, -2), product, precision=highest)
-    factor = jnp.linalg.cholesky(gram)
-    order = product.shape[-1]
-    flat_factor = factor.reshape(-1, order, order)
-    flat_product = product.reshape(-1, order, order)
-    solved = jax.vmap(
-        lambda lower, right: jax.scipy.linalg.solve_triangular(lower, right.T, lower=True)
-    )(flat_factor, flat_product)
-    return jnp.swapaxes(solved, -1, -2).reshape(product.shape)
+LANES = 128
+
+
+def inverse_factor_kernel(stat_ref, inverse_ref, factor_ref):
+    order = stat_ref.shape[0]
+    tile = (8, LANES)
+    sub = lax.broadcasted_iota(jnp.int32, tile, 0)
+
+    def eliminate(source_ref, base, start, first, count, accs):
+        def body(group, accs):
+            top = pl.multiple_of(group * 8, 8)
+            for unit in range(8):
+                value = source_ref[top + unit, pl.ds(start, 8), :]
+                accs = tuple(
+                    accs[c]
+                    - value
+                    * jnp.broadcast_to(factor_ref[top + unit, pl.ds(base + c, 1), :], tile)
+                    for c in range(8)
+                )
+            return accs
+
+        return list(lax.fori_loop(first, count, body, tuple(accs)))
+
+    def block(kb, _):
+        base = pl.multiple_of(kb * 8, 8)
+        accs = [stat_ref[base + c, pl.ds(base, 8), :] for c in range(8)]
+        accs = eliminate(factor_ref, base, base, 0, kb, accs)
+        scale = []
+        coef = {}
+        for c in range(8):
+            scale.append(jnp.broadcast_to(lax.rsqrt(accs[c][c : c + 1, :]), tile))
+            accs[c] = accs[c] * scale[c]
+            for d in range(c + 1, 8):
+                coef[(c, d)] = jnp.broadcast_to(accs[c][d : d + 1, :], tile)
+                accs[d] = accs[d] - accs[c] * coef[(c, d)]
+        for c in range(8):
+            factor_ref[base + c, pl.ds(base, 8), :] = jnp.where(sub >= c, accs[c], 0.0)
+
+        def finish(accs, target_ref, start):
+            accs = list(accs)
+            for c in range(8):
+                for e in range(c):
+                    accs[c] = accs[c] - accs[e] * coef[(e, c)]
+                accs[c] = accs[c] * scale[c]
+                target_ref[base + c, pl.ds(start, 8), :] = accs[c]
+
+        def below(group, _):
+            start = pl.multiple_of(group * 8, 8)
+            accs = [stat_ref[base + c, pl.ds(start, 8), :] for c in range(8)]
+            finish(eliminate(factor_ref, base, start, 0, kb, accs), factor_ref, start)
+            return 0
+
+        def left(group, _):
+            start = pl.multiple_of(group * 8, 8)
+            accs = [jnp.zeros(tile, jnp.float32) for c in range(8)]
+            finish(eliminate(inverse_ref, base, start, group, kb, accs), inverse_ref, start)
+            return 0
+
+        def clear(group, _):
+            start = pl.multiple_of(group * 8, 8)
+            for c in range(8):
+                inverse_ref[base + c, pl.ds(start, 8), :] = jnp.zeros(tile, jnp.float32)
+            return 0
+
+        lax.fori_loop(kb + 1, order // 8, below, 0)
+        lax.fori_loop(0, kb, left, 0)
+        finish([jnp.where(sub == c, 1.0, 0.0) for c in range(8)], inverse_ref, base)
+        lax.fori_loop(kb + 1, order // 8, clear, 0)
+        return 0
+
+    lax.fori_loop(0, order // 8, block, 0)
+
+
+def inverse_factors(grams):
+    count, order = grams.shape[0], grams.shape[-1]
+    chunks = -(-count // LANES)
+    spare = chunks * LANES - count
+    eye = jnp.broadcast_to(jnp.eye(order, dtype=jnp.float32), (spare, order, order))
+    lanes = jnp.concatenate([grams, eye], 0).transpose(1, 2, 0)
+    block = pl.BlockSpec((order, order, LANES), lambda chunk: (0, 0, chunk))
+    result = pl.pallas_call(
+        inverse_factor_kernel,
+        grid=(chunks,),
+        out_shape=jax.ShapeDtypeStruct(lanes.shape, jnp.float32),
+        in_specs=[block],
+        out_specs=block,
+        scratch_shapes=[pltpu.VMEM((order, order, LANES), jnp.float32)],
+        compiler_params=pltpu.CompilerParams(vmem_limit_bytes=56 * 2**20),
+    )(lanes)
+    return result.transpose(2, 0, 1)[:count]
+
+
+def orthonormal(stats, bases):
+    products = [
+        jnp.matmul(stat, basis, precision=highest)[0] for stat, basis in zip(stats, bases)
+    ]
+    grams = [
+        jnp.matmul(jnp.swapaxes(product, -1, -2), product, precision=highest)
+        for product in products
+    ]
+    inverses = inverse_factors(jnp.concatenate(grams, 0))
+    count = products[0].shape[0]
+    return [
+        jnp.matmul(product, jnp.swapaxes(inverse, -1, -2), precision=highest)[None]
+        for product, inverse in zip(products, (inverses[:count], inverses[count:]))
+    ]
 
 
 def soap_update(grads, master, first, second, left, right, left_stat, right_stat):
@@ -201,12 +293,13 @@
     right_new_stat = beta_stat * right_stat + (1.0 - beta_stat) * jnp.matmul(
         jnp.swapaxes(grads, -1, -2), grads, precision=highest
     )
+    left_new, right_new = orthonormal((left_new_stat, right_new_stat), (left, right))
     return (
         master_new,
         first_new,
         second_new,
-        orthonormal(left_new_stat, left),
-        orthonormal(right_new_stat, right),
+        left_new,
+        right_new,
         left_new_stat,
         right_new_stat,
     )
@@ -245,10 +338,16 @@
     bias_second,
 ):
     shards = lax.axis_size("blk")
+    shard = lax.axis_index("blk")
+    image, skip, labels, weight_map, valid = [
+        lax.all_gather(part, "blk", axis=0, tiled=True)
+        for part in (image, skip, labels, weight_map, valid)
+    ]
     images, low_rows, low_cols = (image.shape[0], image.shape[1], image.shape[2])
     high_rows, high_cols = (2 * low_rows, 2 * low_cols)
     total_rows = low_rows * lax.axis_size("rows")
     order = master.shape[-1]
+    groups = GROUPS // shards
     layers = ((C0, C1, 9), (C1, C1, 9), (C1, C0, 4), (2 * C0, C0, 9))
     copies = lax.all_gather(master.astype(jnp.bfloat16), "rows", axis=1, tiled=True)[0]
     ordered = copies[jnp.argsort(owner)]
@@ -259,59 +358,79 @@
         number = out_rows // order * taps * (in_width // order)
         shard_list.append(from_blocks(ordered[offset : offset + number], out_rows, taps, in_width))
         offset = offset + number
-    marks = (0, C1, 2 * C1, 3 * C1, 4 * C1, 4 * C1 + C0, 4 * C1 + 2 * C0)
-    pieces = [norm_params[marks[index] : marks[index + 1]] for index in range(6)]
-    head_low = norm_params[marks[6] :].reshape(C0, 2).astype(jnp.bfloat16)
+    widths = (C1, C1, C1, C1, C0, C0)
+    pieces = []
+    offset = 0
+    for width in widths:
+        local_width = width // shards
+        pieces.append(
+            lax.dynamic_slice_in_dim(norm_params, offset + shard * local_width, local_width)
+        )
+        offset = offset + width
+    head_width = C0 // shards
+    head_low = lax.dynamic_slice_in_dim(
+        norm_params[offset:].reshape(C0, 2), shard * head_width, head_width
+    ).astype(jnp.bfloat16)
     pre_one, views_one = forward_conv(pad_rows(image), shard_list[0], low_rows, low_cols, True)
     act_one, saved_one = group_forward(
-        pre_one.reshape(images, low_rows, low_cols, C1), pieces[0], pieces[1], total_rows
-    )
-    pre_two, views_two = forward_conv(
-        pad_rows(act_one.astype(jnp.bfloat16)), shard_list[1], low_rows, low_cols, True
-    )
+        pre_one.reshape(images, low_rows, low_cols, -1), pieces[0], pieces[1], total_rows, groups
+    )
+    full_one = lax.all_gather(act_one.astype(jnp.bfloat16), "blk", axis=3, tiled=True)
+    pre_two, views_two = forward_conv(pad_rows(full_one), shard_list[1], low_rows, low_cols, True)
     act_two, saved_two = group_forward(
-        pre_two.reshape(images, low_rows, low_cols, C1), pieces[2], pieces[3], total_rows
-    )
-    up_taps, views_up = forward_conv(
-        act_two.astype(jnp.bfloat16), shard_list[2], low_rows, low_cols, False
-    )
-    upsampled = up_taps.reshape(images, low_rows, low_cols, 2, 2, C0).transpose(0, 1, 3, 2, 4, 5)
-    upsampled = upsampled.reshape(images, high_rows, high_cols, C0).astype(jnp.bfloat16)
+        pre_two.reshape(images, low_rows, low_cols, -1), pieces[2], pieces[3], total_rows, groups
+    )
+    full_two = lax.all_gather(act_two.astype(jnp.bfloat16), "blk", axis=3, tiled=True)
+    up_taps, views_up = forward_conv(full_two, shard_list[2], low_rows, low_cols, False)
+    upsampled = up_taps.astype(jnp.bfloat16)
+    upsampled = upsampled.reshape(images, low_rows, low_cols, 2, 2, -1).transpose(0, 1, 3, 2, 4, 5)
+    upsampled = upsampled.reshape(images, high_rows, high_cols, -1)
+    upsampled = lax.all_gather(upsampled, "blk", axis=3, tiled=True)
     joined = jnp.concatenate([upsampled, skip], -1)
     pre_three, views_three = forward_conv(
         pad_rows(joined), shard_list[3], high_rows, high_cols, True
     )
     act_three, saved_three = group_forward(
-        pre_three.reshape(images, high_rows, high_cols, C0), pieces[4], pieces[5], 2 * total_rows
-    )
-    flat_three = act_three.astype(jnp.bfloat16).reshape(-1, C0)
-    logits = jnp.dot(flat_three, head_low, preferred_element_type=jnp.float32) + head_bias
+        pre_three.reshape(images, high_rows, high_cols, -1),
+        pieces[4],
+        pieces[5],
+        2 * total_rows,
+        groups,
+    )
+    flat_three = act_three.astype(jnp.bfloat16).reshape(-1, head_width)
+    logits = (
+        lax.psum(jnp.dot(flat_three, head_low, preferred_element_type=jnp.float32), "blk")
+        + head_bias
+    )
     targets = (labels.reshape(-1, 1) == jnp.arange(2)[None, :]).astype(jnp.float32)
     valid_flat = valid.reshape(-1).astype(jnp.float32)
     scales = valid_flat * weight_map.reshape(-1).astype(jnp.float32) * 0.125
+    valid_count = lax.psum(jnp.sum(valid_flat), "rows")
     largest = jnp.max(logits, -1, keepdims=True)
     log_total = jnp.log(jnp.sum(jnp.exp(logits - largest), -1, keepdims=True)) + largest
     losses = log_total[:, 0] - jnp.sum(logits * targets, -1)
-    loss_sum, valid_count = lax.psum(
-        (jnp.sum(scales * losses), jnp.sum(valid_flat)), ("rows", "blk")
-    )
+    loss_part = jnp.sum(scales * losses)
     grad_logits = (jnp.exp(logits - log_total) - targets) * (scales / valid_count)[:, None]
     grad_head = jnp.dot(flat_three.astype(jnp.float32).T, grad_logits, precision=highest)
     grad_bias = jnp.sum(grad_logits, 0)
     grad_act = jnp.dot(grad_logits, head_low.astype(jnp.float32).T, precision=highest)
     grad_pre, gain_three, shift_three = group_backward(
-        grad_act.reshape(images, high_rows, high_cols, C0), saved_three, pieces[4], 2 * total_rows
+        grad_act.reshape(images, high_rows, high_cols, -1),
+        saved_three,
+        pieces[4],
+        2 * total_rows,
+        groups,
     )
     grad_four, grad_joined = backward_conv(grad_pre, views_three, shard_list[3], C0, True, True)
-    grad_up = grad_joined.astype(jnp.bfloat16).reshape(images, low_rows, 2, low_cols, 2, C0)
-    grad_up = grad_up.transpose(0, 1, 3, 2, 4, 5).reshape(-1, 4, C0)
+    grad_up = grad_joined.astype(jnp.bfloat16).reshape(images, low_rows, 2, low_cols, 2, -1)
+    grad_up = grad_up.transpose(0, 1, 3, 2, 4, 5).reshape(-1, 4, grad_up.shape[-1])
     grad_three, grad_act = backward_conv(grad_up, views_up, shard_list[2], C1, False, True)
     grad_pre, gain_two, shift_two = group_backward(
-        grad_act.reshape(images, low_rows, low_cols, C1), saved_two, pieces[2], total_rows
+        grad_act.reshape(images, low_rows, low_cols, -1), saved_two, pieces[2], total_rows, groups
     )
     grad_two, grad_act = backward_conv(grad_pre, views_two, shard_list[1], C1, True, True)
     grad_pre, gain_one, shift_one = group_backward(
-        grad_act.reshape(images, low_rows, low_cols, C1), saved_one, pieces[0], total_rows
+        grad_act.reshape(images, low_rows, low_cols, -1), saved_one, pieces[0], total_rows, groups
     )
     grad_one, unused = backward_conv(grad_pre, views_one, shard_list[0], C0, True, False)
     blocks = jnp.concatenate(
@@ -321,7 +440,14 @@
     small = jnp.concatenate(
         [gain_one, shift_one, gain_two, shift_two, gain_three, shift_three, grad_head.reshape(-1)]
     )
-    small, grad_bias = lax.psum((small, grad_bias), ("rows", "blk"))
+    small, grad_bias, loss_sum = lax.psum((small, grad_bias, loss_part), "rows")
+    spread = lax.all_gather(small, "blk", axis=0)
+    parts = []
+    offset = 0
+    for width in widths + (2 * C0,):
+        parts.append(spread[:, offset : offset + width // shards].reshape(-1))
+        offset = offset + width // shards
+    small = jnp.concatenate(parts)
     soap = soap_update(
         grads, master, first_moment, second_moment, left_basis, right_basis, left_stat, right_stat
     )

time: 3720 us -> 1140 us (0.31)
  other arithmetic: 1790 us -> 84.3 us
  waiting for transfers between devices: 1350 us -> 328 us
  local copies, waits for them, and re-layouts: 141 us -> 252 us
  matrix products: 221 us -> 156 us
  blocking collectives: 157 us -> 208 us
  Pallas kernels: 0 us -> 44.1 us
    another operation x11 -> x2, other arithmetic: 1740 us -> 1.52 us  [the longest x1 1.46 us: weight_grad(): return jnp.stack(parts, 1)]
    all_gather x4 -> x2, waiting for transfers between devices: 607 us -> 72.5 us  [the longest x1 37.1 us: local(): upsampled = lax.all_gather(upsampled, 'blk', axis=3, tiled=True)]
    reduce_scatter x4 -> x3, waiting for transfers between devices: 585 us -> 86.6 us  [input_grad(): return lax.psum_scatter(carry, 'blk', scatter_dimension=1, tiled=True)]
    all_gather x0 -> x7, blocking collectives: none -> 85 us  [the longest x4 42.2 us: local(): lax.all_gather(part, 'blk', axis=0, tiled=True)]
    pallas_call x0 -> x1, Pallas kernels: none -> 44.1 us  [inverse_factors(): pl.pallas_call(inverse_factor_kernel, grid=(chunks,), out_shape=jax.Shape...]
    psum x2 -> x3, blocking collectives: 80.3 us -> 51.5 us  [the longest x1 22.3 us: local(): small, grad_bias, loss_sum = lax.psum((small, grad_bias, loss_part), 'rows')]
  transfers between devices with their start and end apart: 20 -> 17, of which waited for: 15 -> 10; matrix products, arithmetic and copies ran while one was open for 5% -> 8% of each run, Pallas kernels for 0% -> 0%
where the time goes in v1:
time: 1140 us; the launch traced here: 1120 us
  waiting for transfers between devices  328 us (29%)
  local copies, waits for them, and re-layouts  252 us (22%)
  blocking collectives  208 us (18%)
  matrix products  156 us (14%)
  other arithmetic  84.3 us (7%)
  Pallas kernels  44.1 us (4%)
  starting transfers between devices  34.8 us (3%)
  between operations  16.6 us (1%)
    reduce_scatter x1, waiting for transfers between devices, local(): lax.psum_scatter(blocks[owner], 'rows', scatter_dimension=0, tiled=True)  125 us
    reduce_scatter x3, waiting for transfers between devices, input_grad(): return lax.psum_scatter(carry, 'blk', scatter_dimension=1, tiled=True)  86.6 us
    unnamed x279, local copies, waits for them, and re-layouts  56.1 us
    psum x3, blocking collectives, group_forward(): first_sum, second_sum = lax.psum((first_sum, second_sum), 'rows')  46 us
    pallas_call x1, Pallas kernels, inverse_factors(): pl.pallas_call(inverse_factor_kernel, grid=(chunks,), out_shape=jax.Shape...  44.1 us
    all_gather x4, blocking collectives, local(): lax.all_gather(part, 'blk', axis=0, tiled=True)  42.2 us
    all_gather x1, waiting for transfers between devices, local(): upsampled = lax.all_gather(upsampled, 'blk', axis=3, tiled=True)  37.1 us
    all_gather x1, waiting for transfers between devices, local(): lax.all_gather(part, 'blk', axis=0, tiled=True)  35.4 us
  transfers between devices with their start and end apart: 17, of which 10 were waited for; matrix products, arithmetic and copies ran while one was open for 8% of the time, Pallas kernels for 0%

profile of v1, /device:TPU:1, one launch (start us, length us, event | category | flops | bytes accessed | tf_op | source)
XLA Modules:
  0.0 1123.3 jit_solution(6982637497886136291)
XLA Ops:
  10.5 13.9 %all_gather.35 = bf16[4,1,96,512]{3,2,1,0:T(8,128)(2,1)S(1)} all-gather(bf16[1,1,96,512]{3,2,1,0:T(8,128)(2,1)S(1)} %copy-done.79), channel_id=1, replica_groups=mesh['rows'=8,'blk'=4] {'blk'}, dimensions={0}, use_global_device_ids=true | all-gather | bytes 491520 | tf_op jit(solution)/shard_map/all_gather | solution.py:343
  48.9 33.6 %all-gather.5.cloned.1.call-done = bf16[1,320,128,128]{3,2,0,1:T(8,128)(2,1)} async-done(((bf16[1,40,128,128]{3,2,0,1:T(8,128)(2,1)}), bf16[1,320,128,128]{3,2,0,1:T(8,128)(2,1)}) %all-gather.5.cloned.1.call-update) | async-done | bytes 10485776 | tf_op jit(solution)/shard_map/all_gather | solution.py:352
  82.5 14.7 %gather_fusion = bf16[320,128,128]{2,1,0:T(8,128)(2,1)} fusion(bf16[320,128,128]{2,1,0:T(8,128)(2,1)} %bitcast.1193, s32[1024]{0:T(1024)S(1)} %pad_clamp_fusion.1), kind=kCustom, calls=%fused_computation | custom fusion | bytes 20972800 | tf_op jit(solution)/shard_map/gather | solution.py:353
  124.0 12.2 %all-reduce.10 = (f32[4,8]{0,1:T(8,128)}, f32[4,8]{0,1:T(8,128)}) all-reduce(f32[4,8]{0,1:T(8,128)S(1)} %multiply_reduce_fusion.6, f32[4,8]{0,1:T(8,128)S(1)} %reduce_sum.207), channel_id=1, replica_groups=mesh['rows'=8,'blk'=4] {'rows'}, use_global_device_ids=true, to_apply=%region_4.5 | all-reduce | flops 64 | bytes 512 | tf_op jit(solution)/shard_map/psum | solution.py:134
  143.4 15.7 %all_gather.37 = bf16[4,1,96,1024]{3,2,0,1:T(8,128)(2,1)} all-gather(bf16[4,1,96,256]{3,2,0,1:T(8,128)(2,1)S(1)} %multiply_convert_fusion.6), channel_id=1, replica_groups=mesh['rows'=8,'blk'=4] {'blk'}, dimensions={3}, use_global_device_ids=true | all-gather | bytes 983040 | tf_op jit(solution)/shard_map/all_gather | solution.py:378
  207.8 13.3 %all-reduce.9 = (f32[4,8]{0,1:T(8,128)}, f32[4,8]{0,1:T(8,128)}) all-reduce(f32[4,8]{0,1:T(8,128)S(1)} %multiply_reduce_fusion.5, f32[4,8]{0,1:T(8,128)S(1)} %reduce_sum.209), channel_id=1, replica_groups=mesh['rows'=8,'blk'=4] {'rows'}, use_global_device_ids=true, to_apply=%region_8.9 | all-reduce | flops 64 | bytes 512 | tf_op jit(solution)/shard_map/psum | solution.py:134
  227.6 16.5 %all_gather.38 = bf16[4,1,96,1024]{3,2,0,1:T(8,128)(2,1)S(1)} all-gather(bf16[4,1,96,256]{3,2,0,1:T(8,128)(2,1)S(1)} %multiply_convert_fusion.5), channel_id=1, replica_groups=mesh['rows'=8,'blk'=4] {'blk'}, dimensions={3}, use_global_device_ids=true | all-gather | bytes 983040 | tf_op jit(solution)/shard_map/all_gather | solution.py:383
  249.8 37.1 %all-gather.7.cloned.1.call-done = bf16[4,2,192,512]{3,2,1,0:T(8,128)(2,1)} async-done(((bf16[4,2,192,128]{3,2,1,0:T(8,128)(2,1)}), bf16[4,2,192,512]{3,2,1,0:T(8,128)(2,1)}) %all-gather.7.cloned.1.call-update) | async-done | bytes 1572880 | tf_op jit(solution)/shard_map/all_gather | solution.py:388
  289.6 35.4 %all-gather.9.cloned.1.call-done = bf16[4,2,192,512]{3,2,1,0:T(8,128)(2,1)} async-done(((bf16[1,2,192,512]{3,2,1,0:T(8,128)(2,1)}), bf16[4,2,192,512]{3,2,1,0:T(8,128)(2,1)}) %all-gather.9.cloned.1.call-update) | async-done | bytes 1572880 | tf_op jit(solution)/shard_map/all_gather | solution.py:343
  383.7 22.4 %slice_bitcast_fusion.120 = (bf16[4,2,24,8,8,128]{5,4,3,2,1,0:T(8,128)(2,1)}, bf16[4,2,24,8,8,128]{5,4,3,2,1,0:T(8,128)(2,1)}, bf16[4,2,24,8,8,128]{5,4,3,2,1,0:...) fusion(bf16[4,4,194,1024]{3,2,1,0:T(8,128)(2,1)} %fusion.5), kind=kLoop, calls=%fused_computation.494 | loop fusion | bytes 56623104
  431.4 20.4 %all-reduce.8 = (f32[4,8]{0,1:T(8,128)}, f32[4,8]{0,1:T(8,128)}) all-reduce(f32[4,8]{0,1:T(8,128)} %get-tuple-element.21, f32[4,8]{0,1:T(8,128)} %get-tuple-element.20), channel_id=1, replica_groups=mesh['rows'=8,'blk'=4] {'rows'}, use_global_device_ids=true, to_apply=%region_12.13 | all-reduce | flops 64 | bytes 512 | tf_op jit(solution)/shard_map/psum | solution.py:134
  463.8 13.5 %psum.125 = f32[1536,2]{0,1:T(2,128)} all-reduce(f32[1536,2]{0,1:T(2,128)} %fusion.270), channel_id=1, replica_groups=mesh['rows'=8,'blk'=4] {'blk'}, use_global_device_ids=true, to_apply=%region_13.14 | all-reduce | flops 3072 | bytes 24576 | tf_op jit(solution)/shard_map/psum | solution.py:402
  482.8 15.7 %psum.127 = f32[]{:T(128)} all-reduce(f32[]{:T(128)} %get-tuple-element.34), channel_id=1, replica_groups=mesh['rows'=8,'blk'=4] {'rows'}, use_global_device_ids=true, to_apply=%region_20.21 | all-reduce | flops 1 | bytes 8 | tf_op jit(solution)/shard_map/psum | solution.py:408
  514.5 12.0 %all-reduce.7 = (f32[4,8]{0,1:T(8,128)S(1)}, f32[4,8]{0,1:T(8,128)S(1)}) all-reduce(f32[4,8]{0,1:T(8,128)S(1)} %get-tuple-element.19, f32[4,8]{0,1:T(8,128)S(1)} %get-tuple-element.18), channel_id=1, replica_groups=mesh['rows'=8,'blk'=4] {'rows'}, use_global_device_ids=true, to_apply=%region_24.25 | all-reduce | flops 64 | bytes 512 | tf_op jit(solution)/shard_map/psum | solution.py:155
  552.3 51.6 %reduce-scatter.5.cloned.1.call-done = f32[1536,128]{1,0:T(8,128)} async-done(((f32[1536,512]{1,0:T(8,128)}), f32[1536,128]{1,0:T(8,128)}) %reduce-scatter.5.cloned.1.call-update) | async-done | bytes 786448 | tf_op jit(solution)/shard_map/reduce_scatter | solution.py:101
  624.5 19.8 %reduce-scatter.7.cloned.1.call-done = f32[384,256]{1,0:T(8,128)} async-done(((f32[384,1024]{1,0:T(8,128)}), f32[384,256]{1,0:T(8,128)}) %reduce-scatter.7.cloned.1.call-update) | async-done | bytes 393232 | tf_op jit(solution)/shard_map/reduce_scatter | solution.py:101
  651.2 12.9 %all-reduce.6 = (f32[4,8]{0,1:T(8,128)S(1)}, f32[4,8]{0,1:T(8,128)}) all-reduce(f32[4,8]{0,1:T(8,128)} %get-tuple-element.27, f32[4,8]{0,1:T(8,128)} %get-tuple-element.26), channel_id=1, replica_groups=mesh['rows'=8,'blk'=4] {'rows'}, use_global_device_ids=true, to_apply=%region_30.31 | all-reduce | flops 64 | bytes 512 | tf_op jit(solution)/shard_map/psum | solution.py:155
  705.3 15.2 %reduce-scatter.9.cloned.1.call-done = f32[384,256]{1,0:T(8,128)} async-done(((f32[384,1024]{1,0:T(8,128)}), f32[384,256]{1,0:T(8,128)}) %reduce-scatter.9.cloned.1.call-update) | async-done | bytes 393232 | tf_op jit(solution)/shard_map/reduce_scatter | solution.py:101
  738.7 22.3 %all-reduce.5 = (f32[]{:T(128)}, f32[4,8]{0,1:T(8,128)S(1)}, f32[4,8]{0,1:T(8,128)S(1)}, f32[1,1536]{1,0:T(1,128)S(1)}, f32[2]{0:T(128)S(1)}) all-reduce(f32[]{:T(128)} %get-tuple-element.35, f32[4,8]{0,1:T(8,128)} %get-tuple-element.25, f32[4,8]{0,1:T(8,128)} %get-tuple-element.24, ...), channel_id=1, replica_groups=mesh['rows'=8,'blk'=4] {'rows'}, use_global_device_ids=true, to_apply=%region_18.19 | all-reduce | flops 1603 | bytes 12824 | tf_op jit(solution)/shard_map/psum | solution.py:443
  772.5 12.4 %pad_maximum_fusion = f32[320,128,128]{2,1,0:T(8,128)} fusion(f32[72,128,128]{2,1,0:T(8,128)S(1)} %bitcast.1214, f32[32,128,128]{2,1,0:T(8,128)S(1)} %bitcast.1206, f32[144,128,128]{2,1,0:T(8,128)} %bitcast.1130, f32[72,128,128]{2,1,0:T(8,128)S(1)} %bitcast.1171), kind=kLoop, calls=%fused_computation.2 | loop fusion | flops 15728640 | bytes 41943040 | tf_op jit(solution)/shard_map/concatenate | solution.py:436
  784.9 20.9 %gather_fusion.1 = f32[320,128,128]{2,1,0:T(8,128)} fusion(f32[320,128,128]{2,1,0:T(8,128)} %pad_maximum_fusion, s32[1024]{0:T(1024)S(1)} %copy-done.113), kind=kCustom, calls=%fused_computation.1 | custom fusion | bytes 41944320 | tf_op jit(solution)/shard_map/gather | solution.py:439
  817.8 125.1 %reduce-scatter.11.cloned.1.call-done = f32[40,128,128]{2,1,0:T(8,128)} async-done(((f32[320,128,128]{2,1,0:T(8,128)}), f32[40,128,128]{2,1,0:T(8,128)}) %reduce-scatter.11.cloned.1.call-update) | async-done | bytes 2621456 | tf_op jit(solution)/shard_map/reduce_scatter | solution.py:439
  1025.6 44.1 %shard_map.306 = f32[128,128,128]{2,1,0:T(8,128)} custom-call(f32[128,128,128]{2,1,0:T(8,128)} %maximum_bitcast_fusion.stat_ref), custom_call_target="tpu_custom_call" | custom-call | tf_op jit(solution)/shard_map/pallas_call | solution.py:245
  1069.7 13.8 %fusion.308 = (f32[40,128,128]{0,2,1:T(8,128)}, f32[40,128,128]{0,2,1:T(8,128)}) fusion(f32[128,128,128]{0,2,1:T(8,128)} %bitcast.1126), kind=kLoop, calls=%fused_computation.511 | loop fusion | bytes 10485760 | tf_op jit(solution)/shard_map/slice | solution.py:269
  (567 shorter events, 492.0 us)
Async XLA Ops:
  7.2 942.7 %copy-start = (f32[1,40,128,128]{3,2,1,0:T(8,128)S(1)}, f32[1,40,128,128]{3,2,1,0:T(8,128)}, u32[]{:S(2)}) copy-start(f32[1,40,128,128]{3,2,1,0:T(8,128)} %param.29) | copy-start | bytes 7864324
  7.2 75.3 %all-gather.5.cloned.1.call-start = ((), (), s32[]{:S(2)}) async-start(), calls=%async_computation.4 | async-start | bytes 11796480 | tf_op jit(solution)/shard_map/all_gather | solution.py:352
  10.4 276.4 %all-gather.7.cloned.1.call-start = ((), (), s32[]{:S(2)}) async-start(), calls=%async_computation.5 | async-start | bytes 1966080 | tf_op jit(solution)/shard_map/all_gather | solution.py:388
  24.4 90.7 %copy-start.40 = (bf16[4,1,96,512]{3,2,1,0:T(8,128)(2,1)}, bf16[4,1,96,512]{3,2,1,0:T(8,128)(2,1)S(1)}, u32[]{:S(2)}) copy-start(bf16[4,1,96,512]{3,2,1,0:T(8,128)(2,1)S(1)} %all_gather.35) | copy-start | bytes 1179652
  24.4 20.6 %collective-permute-start.1 = (bf16[4,1,96,512]{3,2,1,0:T(8,128)(2,1)S(1)}, bf16[4,1,96,512]{3,2,1,0:T(8,128)(2,1)S(1)}, u32[]{:S(2)}, u32[]{:S(2)}) collective-permute-start(bf16[4,1,96,512]{3,2,1,0:T(8,128)(2,1)S(1)} %all_gather.35), channel_id=1, source_target_pairs={{4,0},{8,4},{12,8},{16,12},{20,16},{24,20},{28,24},{5,1},{9,5},{13... | collective-permute-start | bytes 1179656 | tf_op jit(solution)/shard_map/ppermute | solution.py:36
  28.7 16.3 %collective-permute-start = (bf16[4,1,96,512]{3,2,1,0:T(8,128)(2,1)S(1)}, bf16[4,1,96,512]{3,2,1,0:T(8,128)(2,1)}, u32[]{:S(2)}, u32[]{:S(2)}) collective-permute-start(bf16[4,1,96,512]{3,2,1,0:T(8,128)(2,1)S(1)} %all_gather.35), channel_id=1, source_target_pairs={{0,4},{4,8},{8,12},{12,16},{16,20},{20,24},{24,28},{1,5},{5,9},{9,... | collective-permute-start | bytes 1179656 | tf_op jit(solution)/shard_map/ppermute | solution.py:33
  37.0 190.5 %copy-start.86 = (f32[256]{0:T(256)}, f32[256]{0:T(256)S(1)}, u32[]{:S(2)}) copy-start(f32[256]{0:T(256)S(1)} %get-tuple-element.134) | copy-start | bytes 3076
  37.0 190.5 %copy-start.100 = (f32[256]{0:T(256)}, f32[256]{0:T(256)S(1)}, u32[]{:S(2)}) copy-start(f32[256]{0:T(256)S(1)} %get-tuple-element.135) | copy-start | bytes 3076
  45.0 67.4 %copy-start.48 = (bf16[4,1,96,512]{3,2,1,0:T(8,128)(2,1)}, bf16[4,1,96,512]{3,2,1,0:T(8,128)(2,1)S(1)}, u32[]{:S(2)}) copy-start(bf16[4,1,96,512]{3,2,1,0:T(8,128)(2,1)S(1)} %collective-permute-done.1) | copy-start | bytes 1179652
  117.9 50.5 %copy-start.34 = (f32[384,256]{1,0:T(8,128)}, f32[384,256]{1,0:T(8,128)S(1)}, u32[]{:S(2)}) copy-start(f32[384,256]{1,0:T(8,128)S(1)} %fusion.165) | copy-start | bytes 1179652
  159.1 30.9 %collective-permute-start.3 = (bf16[4,1,96,1024]{3,2,0,1:T(8,128)(2,1)}, bf16[4,1,96,1024]{3,2,0,1:T(8,128)(2,1)}, u32[]{:S(2)}, u32[]{:S(2)}) collective-permute-start(bf16[4,1,96,1024]{3,2,0,1:T(8,128)(2,1)} %all_gather.37), channel_id=1, source_target_pairs={{4,0},{8,4},{12,8},{16,12},{20,16},{24,20},{28,24},{5,1},{9,5},{13... | collective-permute-start | bytes 2359304 | tf_op jit(solution)/shard_map/ppermute | solution.py:36
  166.6 23.4 %collective-permute-start.2 = (bf16[4,1,96,1024]{3,2,0,1:T(8,128)(2,1)}, bf16[4,1,96,1024]{3,2,0,1:T(8,128)(2,1)}, u32[]{:S(2)}, u32[]{:S(2)}) collective-permute-start(bf16[4,1,96,1024]{3,2,0,1:T(8,128)(2,1)} %all_gather.37), channel_id=1, source_target_pairs={{0,4},{4,8},{8,12},{12,16},{16,20},{20,24},{24,28},{1,5},{5,9},{9,... | collective-permute-start | bytes 2359304 | tf_op jit(solution)/shard_map/ppermute | solution.py:33
  249.0 76.0 %all-gather.9.cloned.1.call-start = ((), (), s32[]{:S(2)}) async-start(), calls=%async_computation.6 | async-start | bytes 1966080 | tf_op jit(solution)/shard_map/all_gather | solution.py:343
  249.8 354.1 %reduce-scatter.5.cloned.1.call-start = ((), (), s32[]{:S(2)}) async-start(), calls=%async_computation.7 | async-start | bytes 3932160 | tf_op jit(solution)/shard_map/reduce_scatter | solution.py:101
  331.7 46.1 %collective-permute-start.5 = (bf16[4,1,192,1024]{3,2,1,0:T(8,128)(2,1)}, bf16[4,1,192,1024]{3,2,1,0:T(8,128)(2,1)}, u32[]{:S(2)}, u32[]{:S(2)}) collective-permute-start(bf16[4,1,192,1024]{3,2,1,0:T(8,128)(2,1)} %get-tuple-element.84), channel_id=1, source_target_pairs={{4,0},{8,4},{12,8},{16,12},{20,16},{24,20},{28,24},{5,1},{9,5},{13... | collective-permute-start | bytes 4718600 | tf_op jit(solution)/shard_map/ppermute | solution.py:36
  334.4 43.4 %collective-permute-start.4 = (bf16[4,1,192,1024]{3,2,1,0:T(8,128)(2,1)}, bf16[4,1,192,1024]{3,2,1,0:T(8,128)(2,1)}, u32[]{:S(2)}, u32[]{:S(2)}) collective-permute-start(bf16[4,1,192,1024]{3,2,1,0:T(8,128)(2,1)} %get-tuple-element.83), channel_id=1, source_target_pairs={{0,4},{4,8},{8,12},{12,16},{16,20},{20,24},{24,28},{1,5},{5,9},{9,... | collective-permute-start | bytes 4718600 | tf_op jit(solution)/shard_map/ppermute | solution.py:33
  424.4 78.9 %copy-start.12 = (f32[1536,128]{1,0:T(8,128)}, f32[1536,128]{1,0:T(8,128)S(1)}, u32[]{:S(2)}) copy-start(f32[1536,128]{1,0:T(8,128)S(1)} %fusion.71) | copy-start | bytes 2359300
  529.0 7.0 collective-permute-start.7
  531.7 5.5 collective-permute-start.6
  544.9 99.4 %reduce-scatter.7.cloned.1.call-start = ((), (), s32[]{:S(2)}) async-start(), calls=%async_computation.8 | async-start | bytes 1966080 | tf_op jit(solution)/shard_map/reduce_scatter | solution.py:101
  609.0 111.5 %reduce-scatter.9.cloned.1.call-start = ((), (), s32[]{:S(2)}) async-start(), calls=%async_computation.9 | async-start | bytes 1966080 | tf_op jit(solution)/shard_map/reduce_scatter | solution.py:101
  670.4 10.5 collective-permute-start.9
  674.6 6.3 collective-permute-start.8
  686.9 256.0 %reduce-scatter.11.cloned.1.call-start = ((), (), s32[]{:S(2)}) async-start(), calls=%async_computation.10 | async-start | bytes 23592960 | tf_op jit(solution)/shard_map/reduce_scatter | solution.py:439
  (122 other events, 1181.6 us)
Sparse Core Ops, SparseCore 0:
  10.6 71.8 all-gather.4
  249.1 37.6 all-gather.6
  288.5 36.5 all-gather.8
  545.1 58.7 reduce-scatter.4
  609.1 35.1 reduce-scatter.6
  687.0 33.4 reduce-scatter.8
  806.0 136.8 reduce-scatter.10

commit v2 on v1

v2 whole, which is shorter than its diff:
```python
import functools

import jax
import jax.numpy as jnp
from jax import lax
from jax.experimental import pallas as pl
from jax.experimental.pallas import tpu as pltpu
from jax.sharding import PartitionSpec as P

C0 = 512
C1 = 1024
GROUPS = 32
STEP = 10


beta_one = 0.9
beta_two = 0.999
beta_stat = 0.95
adam_eps = 1e-08
norm_eps = 1e-05
soap_rate = 0.008
soap_decay = 0.01
small_rate = 0.4
small_decay = 0.01
highest = lax.Precision.HIGHEST


MESH = pl.DeviceIdType.MESH
bf16 = jnp.bfloat16
f32 = jnp.float32
TILE = 128


def dot_nt(left, right):
    return lax.dot_general(left, right, (((1,), (1,)), ((), ())), preferred_element_type=f32)


def dot_nn(left, right):
    return jnp.dot(left, right, preferred_element_type=f32)


def sigmoid(value):
    return 1.0 / (1.0 + jnp.exp(-value))


def block_layers(nb):
    result = []
    first = 0
    for in_width, out_width, taps in ((C0, C1, 9), (C1, C1, 9), (C1, C0, 4), (2 * C0, C0, 9)):
        out = out_width // nb
        result.append((out, in_width, taps, first))
        first = first + out // TILE * taps * (in_width // TILE)
    return result


def step_kernel(
    nr,
    nb,
    cols,
    copies_ref,
    place_ref,
    bias_ref,
    image_ref,
    skip_ref,
    lab_ref,
    wide_ref,
    narrow_ref,
    grad_ref,
    sums_ref,
    x_one,
    x_skip,
    x_lab,
    w_one,
    w_two,
    w_up,
    w_three,
    a_one,
    a_two,
    u_full,
    z_one,
    z_two,
    z_three,
    dy_low,
    dy_high,
    inv_one,
    inv_two,
    inv_three,
    dz_low,
    dz_high,
    shifted_low,
    shifted_high,
    turned_low,
    turned_high,
    dub,
    send_high,
    recv_high,
    send_low,
    recv_low,
    logit,
    reduce_wide,
    reduce_narrow,
    local_sem,
    line_send,
    line_recv,
    halo_send,
    halo_recv,
    red_send,
    red_recv,
    all_send,
    all_recv,
    high_send,
    high_recv,
    edge_send,
    edge_recv,
):
    r = lax.axis_index("rows")
    b = lax.axis_index("blk")
    px = nb * cols
    wide = C1 // nb
    slim = C0 // nb
    taps_high = 3 * slim
    layers = block_layers(nb)

    def remote(src, dst, send, recv, rows, blk):
        return pltpu.make_async_remote_copy(
            src_ref=src,
            dst_ref=dst,
            send_sem=send,
            recv_sem=recv,
            device_id={"rows": rows, "blk": blk},
            device_id_type=MESH,
        )

    def lanes(index, size):
        return pl.ds(pl.multiple_of(index * size, TILE), size)

    def ring(index, count):
        return lax.rem(index + count, count)

    barrier = pltpu.get_barrier_semaphore()

    def greet_rows(step, _):
        pl.semaphore_signal(
            barrier, inc=1, device_id={"rows": ring(r + step, nr), "blk": b}, device_id_type=MESH
        )
        return 0

    lax.fori_loop(1, nr, greet_rows, 0)
    for step in range(1, nb):
        pl.semaphore_signal(
            barrier, inc=1, device_id={"rows": r, "blk": ring(b + step, nb)}, device_id_type=MESH
        )
    pl.semaphore_wait(barrier, nr - 1 + nb - 1)

    class Exchange:
        def __init__(self, number, piece, up=None, down=None):
            self.number, self.piece, self.up, self.down = number, piece, up, down

        def right(self, j):
            return remote(
                self.piece(j),
                self.piece(j),
                line_send.at[self.number, j, 0],
                line_recv.at[self.number, j],
                r,
                ring(b + 1, nb),
            )

        def left(self, j):
            return remote(
                self.piece(j),
                self.piece(j),
                line_send.at[self.number, j, 1],
                line_recv.at[self.number, j],
                r,
                ring(b - 1, nb),
            )

        def higher(self, j):
            src, dst = self.up(j)
            return remote(
                src,
                dst,
                halo_send.at[self.number, j, 0],
                halo_recv.at[self.number, j, 0],
                ring(r + 1, nr),
                b,
            )

        def lower(self, j):
            src, dst = self.down(j)
            return remote(
                src,
                dst,
                halo_send.at[self.number, j, 1],
                halo_recv.at[self.number, j, 1],
                ring(r - 1, nr),
                b,
            )

        def halos(self, j):
            if self.up is None:
                return

            @pl.when(r + 1 < nr)
            def _():
                self.higher(j).start()

            @pl.when(r > 0)
            def _():
                self.lower(j).start()

        def begin(self):
            @pl.when(b + 1 < nb)
            def _():
                self.right(b).start()

            @pl.when(b > 0)
            def _():
                self.left(b).start()

            self.halos(b)

        def hop(self, k):
            @pl.when(b >= k)
            def _():
                self.right(b - k).wait_recv()

                @pl.when(b + 1 < nb)
                def _():
                    self.right(b - k).start()

                self.halos(b - k)

            @pl.when(b + k < nb)
            def _():
                self.left(b + k).wait_recv()

                @pl.when(b > 0)
                def _():
                    self.left(b + k).start()

                self.halos(b + k)

        def hops(self):
            for k in range(1, nb):
                self.hop(k)

        def finish(self):
            for k in range(nb):

                @pl.when((b >= k) & (b + 1 < nb))
                def _():
                    self.right(b - k).wait_send()

                @pl.when((b + k < nb) & (b > 0))
                def _():
                    self.left(b + k).wait_send()

            if self.up is None:
                return
            for j in range(nb):

                @pl.when(r + 1 < nr)
                def _():
                    self.higher(j).wait_send()
                    self.lower(j).wait_recv()

                @pl.when(r > 0)
                def _():
                    self.lower(j).wait_send()
                    self.higher(j).wait_recv()

    def all_reduce(number, buffer):
        def start(step, _):
            remote(
                buffer.at[r],
                buffer.at[r],
                red_send.at[number, step],
                red_recv.at[number, r],
                ring(r + step, nr),
                b,
            ).start()
            return 0

        def wait(step, _):
            source = ring(r + step, nr)
            copy = remote(
                buffer.at[source],
                buffer.at[source],
                red_send.at[number, step],
                red_recv.at[number, source],
                source,
                b,
            )
            copy.wait_recv()
            copy.wait_send()
            return 0

        lax.fori_loop(1, nr, start, 0)
        lax.fori_loop(1, nr, wait, 0)
        return lax.fori_loop(1, nr, lambda k, total: total + buffer[k], buffer[0])

    class Spread:
        def __init__(self, send, recv, source, target):
            self.send, self.recv, self.source, self.target = send, recv, source, target

        def copy(self, step):
            other = ring(b + step, nb)
            return remote(
                self.source(other),
                self.target(b),
                self.send.at[step],
                self.recv.at[b],
                r,
                other,
            )

        def begin(self):
            for step in range(1, nb):
                self.copy(step).start()

        def finish(self):
            for step in range(1, nb):
                other = ring(b + step, nb)
                remote(
                    self.source(other),
                    self.target(other),
                    self.send.at[step],
                    self.recv.at[other],
                    r,
                    other,
                ).wait_recv()
                self.copy(step).wait_send()

    position = lax.rem(lax.broadcasted_iota(jnp.int32, (px, TILE), 0), cols)

    def mask_of(value, column):
        hit = position[:, :1] == column
        return jnp.where(hit, 0.0, value)

    def shift_down(value):
        return mask_of(pltpu.roll(value, 1, 0), 0)

    def shift_up(value):
        return mask_of(pltpu.roll(value, px - 1, 0), cols - 1)

    def group_sum(value, size):
        width = value.shape[-1]
        bits = size.bit_length() - 1
        first = lax.shift_right_logical(lax.broadcasted_iota(jnp.int32, (width, width), 0), bits)
        second = lax.shift_right_logical(lax.broadcasted_iota(jnp.int32, (width, width), 1), bits)
        same = jnp.where(first == second, 1.0, 0.0).astype(f32)
        return jnp.dot(value, same, preferred_element_type=f32, precision=highest)

    def rows_of(image):
        return pl.ds(image * cols, cols)

    def norm_sums(buffer, z_ref):
        for image in range(nb):
            first = 0.0
            second = 0.0
            for part in range(z_ref.shape[0]):
                value = z_ref[part, rows_of(image), :]
                first = first + jnp.sum(value, 0, keepdims=True)
                second = second + jnp.sum(value * value, 0, keepdims=True)
            buffer[r, image : image + 1, :] = first
            buffer[r, nb + image : nb + image + 1, :] = second

    def norm_apply(total, z_ref, inv_ref, gain, shift, size, put):
        width = z_ref.shape[-1]
        number = nr * cols * z_ref.shape[0] * size
        sums = group_sum(total[: 2 * nb], size) / number
        mean = sums[:nb]
        inv = lax.rsqrt(sums[nb:] - mean * mean + norm_eps)
        inv_ref[:nb, :] = inv
        for part in range(z_ref.shape[0]):
            for image in range(nb):
                value = z_ref[part, rows_of(image), :]
                value = (value - mean[image : image + 1]) * inv[image : image + 1]
                z_ref[part, rows_of(image), :] = value
                normed = value * gain + shift
                put(part, image, (normed * sigmoid(normed)).astype(bf16))

    def back_sums(buffer, z_ref, dy_ref, gain, shift, grad_of):
        for image in range(nb):
            first = 0.0
            second = 0.0
            for part in range(z_ref.shape[0]):
                value = z_ref[part, rows_of(image), :]
                normed = value * gain + shift
                gate = sigmoid(normed)
                grad = grad_of(part, image) * gate * (1.0 + normed * (1.0 - gate))
                dy_ref[part, rows_of(image), :] = grad
                first = first + jnp.sum(grad, 0, keepdims=True)
                second = second + jnp.sum(grad * value, 0, keepdims=True)
            buffer[r, image : image + 1, :] = first
            buffer[r, nb + image : nb + image + 1, :] = second

    def back_apply(total, z_ref, dy_ref, inv_ref, gain, size, put):
        number = nr * cols * z_ref.shape[0] * size
        sums = group_sum(total[: 2 * nb] * gain, size) / number
        inv = inv_ref[:nb, :]
        for part in range(z_ref.shape[0]):
            for image in range(nb):
                one = slice(image, image + 1)
                two = slice(nb + image, nb + image + 1)
                value = dy_ref[part, rows_of(image), :] * gain - sums[one]
                value = value - z_ref[part, rows_of(image), :] * sums[two]
                put(part, image, (value * inv[one]).astype(bf16))
        shift_grad = jnp.sum(total[:nb], 0, keepdims=True)
        gain_grad = jnp.sum(total[nb : 2 * nb], 0, keepdims=True)
        return gain_grad, shift_grad

    x_one[1, b] = image_ref[...]
    x_skip[1:3, :, b] = skip_ref[...]
    x_lab[b] = lab_ref[...]
    move_image = Exchange(
        0,
        lambda j: x_one.at[1, j],
        lambda j: (x_one.at[1, j], x_one.at[0, j]),
        lambda j: (x_one.at[1, j], x_one.at[2, j]),
    )
    move_skip = Exchange(
        1,
        lambda j: x_skip.at[pl.ds(1, 2), :, j],
        lambda j: (x_skip.at[2, :, j], x_skip.at[0, :, j]),
        lambda j: (x_skip.at[1, :, j], x_skip.at[3, :, j]),
    )
    move_lab = Exchange(2, lambda j: x_lab.at[j])
    moves = (move_image, move_lab, move_skip)
    for move in moves:
        move.begin()
    stage = pltpu.make_async_copy(copies_ref, grad_ref, local_sem)
    stage.start()

    @pl.when(r == 0)
    def _():
        x_one[0] = jnp.zeros_like(x_one[0])
        x_skip[0] = jnp.zeros_like(x_skip[0])
        a_one[0] = jnp.zeros_like(a_one[0])
        u_full[0] = jnp.zeros_like(u_full[0])
        dz_low[0] = jnp.zeros_like(dz_low[0])
        dz_high[0] = jnp.zeros_like(dz_high[0])

    @pl.when(r == nr - 1)
    def _():
        x_one[2] = jnp.zeros_like(x_one[2])
        x_skip[3] = jnp.zeros_like(x_skip[3])
        a_one[2] = jnp.zeros_like(a_one[2])
        u_full[3] = jnp.zeros_like(u_full[3])
        dz_low[2] = jnp.zeros_like(dz_low[2])
        dz_high[3] = jnp.zeros_like(dz_high[3])

    stage.wait()
    for target, (out, width, taps, first) in zip((w_one, w_two, w_up, w_three), layers):
        across = width // TILE

        def arrange(n, _, target=target, out=out, taps=taps, first=first, across=across):
            ib = lax.rem(n, across)
            t = lax.rem(lax.div(n, across), taps)
            ob = lax.div(n, across * taps)
            target[
                pl.ds(pl.multiple_of(t * out + ob * TILE, TILE), TILE), lanes(ib, TILE)
            ] = grad_ref[place_ref[first + n]]
            return 0

        lax.fori_loop(0, out // TILE * taps * across, arrange, 0)
    for k in range(1, nb):
        for move in moves:
            move.hop(k)
    for move in moves:
        move.finish()

    gain_one, shift_one = wide_ref[0:1, :], wide_ref[1:2, :]
    gain_two, shift_two = wide_ref[2:3, :], wide_ref[3:4, :]
    gain_three, shift_three = narrow_ref[0:1, :], narrow_ref[1:2, :]
    size_low, size_high = C1 // GROUPS, C0 // GROUPS

    def conv_low(z_ref, weight, source):
        def tap(dx):
            total = 0.0
            for dy in range(3):
                first = (3 * dy + dx) * wide
                total = total + dot_nt(source(dy), weight[first : first + wide, :])
            return total

        z_ref[0] = tap(1)
        z_ref[0] += shift_down(tap(0))
        z_ref[0] += shift_up(tap(2))

    conv_low(z_one, w_one, lambda dy: x_one[dy].reshape(px, C0))
    reduce_one, reduce_two = reduce_wide.at[0], reduce_wide.at[1]
    norm_sums(reduce_one, z_one)
    count = 0.0
    for image in range(nb):
        for part in range(4):
            count = count + jnp.sum(x_lab[image, part, 2:3, :], 1, keepdims=True)
    reduce_one[r, 2 * nb : 2 * nb + 1, :] = jnp.broadcast_to(count, (1, wide))
    total = all_reduce(0, reduce_one)
    count = total[2 * nb : 2 * nb + 1, :1]

    def put_one(part, image, value):
        a_one[1, rows_of(image), lanes(b, wide)] = value

    norm_apply(total, z_one, inv_one, gain_one, shift_one, size_low, put_one)
    move = Exchange(
        3,
        lambda j: a_one.at[1, :, lanes(j, wide)],
        lambda j: (a_one.at[1, :, lanes(j, wide)], a_one.at[0, :, lanes(j, wide)]),
        lambda j: (a_one.at[1, :, lanes(j, wide)], a_one.at[2, :, lanes(j, wide)]),
    )
    move.begin()
    move.hops()
    move.finish()
    conv_low(z_two, w_two, lambda dy: a_one[dy])
    norm_sums(reduce_two, z_two)
    total = all_reduce(1, reduce_two)

    def put_two(part, image, value):
        a_two[rows_of(image), lanes(b, wide)] = value

    norm_apply(total, z_two, inv_two, gain_two, shift_two, size_low, put_two)
    move = Exchange(4, lambda j: a_two.at[:, lanes(j, wide)])
    move.begin()
    move.hops()
    move.finish()
    for part in range(4):
        u_full[1 + part // 2, part % 2, :, lanes(b, slim)] = dot_nt(
            a_two[...], w_up[part * slim : (part + 1) * slim, :]
        ).astype(bf16)
    move = Exchange(
        5,
        lambda j: u_full.at[pl.ds(1, 2), :, :, lanes(j, slim)],
        lambda j: (u_full.at[2, :, :, lanes(j, slim)], u_full.at[0, :, :, lanes(j, slim)]),
        lambda j: (u_full.at[1, :, :, lanes(j, slim)], u_full.at[3, :, :, lanes(j, slim)]),
    )
    move.begin()
    move.hops()
    move.finish()
    for e in range(2):
        found = []
        for f in range(2):
            total = 0.0
            for dy in range(3):
                weight = w_three[dy * taps_high : (dy + 1) * taps_high, :]
                total = total + dot_nt(u_full[e + dy, f], weight[:, :C0])
                total = total + dot_nt(x_skip[e + dy, f].reshape(px, C0), weight[:, C0:])
            found.append(total)
        even, odd = found
        z_three[2 * e] = (
            even[:, slim : 2 * slim] + shift_down(odd[:, :slim]) + odd[:, 2 * slim :]
        )
        z_three[2 * e + 1] = (
            odd[:, slim : 2 * slim] + even[:, :slim] + shift_up(even[:, 2 * slim :])
        )
    reduce_three, reduce_four = reduce_narrow.at[0], reduce_narrow.at[1]
    norm_sums(reduce_three, z_three)
    total = all_reduce(2, reduce_three)
    a_three = send_high

    def put_three(part, image, value):
        a_three[part, 0, rows_of(image), :] = value

    norm_apply(total, z_three, inv_three, gain_three, shift_three, size_high, put_three)
    head_low = narrow_ref[8:16, :].astype(bf16)
    head = head_low.astype(f32)
    for part in range(4):
        for image in range(nb):
            logit[b, part * nb + image] = dot_nt(
                head_low, a_three[part, 0, rows_of(image), :]
            )
    spread = Spread(all_send.at[0], all_recv.at[0], lambda other: logit.at[b], lambda j: logit.at[j])
    spread.begin()
    spread.finish()
    loss = jnp.zeros((1, cols), f32)
    bias_grad = [jnp.zeros((1, cols), f32), jnp.zeros((1, cols), f32)]
    head_grad = jnp.zeros((8, slim), f32)
    level = lax.broadcasted_iota(jnp.int32, (8, cols), 0)

    def head_of(part, image):
        tile = logit[0, part * nb + image]
        for j in range(1, nb):
            tile = tile + logit[j, part * nb + image]
        first = tile[0:1, :] + bias_ref[0]
        second = tile[1:2, :] + bias_ref[1]
        scale = x_lab[image, part, 0:1, :]
        label = x_lab[image, part, 1:2, :]
        largest = jnp.maximum(first, second)
        log_total = jnp.log(jnp.exp(first - largest) + jnp.exp(second - largest)) + largest
        picked = first * (1.0 - label) + second * label
        unit = scale / count
        return (
            scale * (log_total - picked),
            (jnp.exp(first - log_total) - (1.0 - label)) * unit,
            (jnp.exp(second - log_total) - label) * unit,
        )

    for part in range(4):
        for image in range(nb):
            cost, first, second = head_of(part, image)
            loss = loss + cost
            bias_grad = [bias_grad[0] + first, bias_grad[1] + second]
            tile = jnp.where(level == 0, first, jnp.where(level == 1, second, 0.0))
            logit[0, part * nb + image] = tile
            head_grad = head_grad + jnp.dot(
                tile,
                a_three[part, 0, rows_of(image), :].astype(f32),
                preferred_element_type=f32,
                precision=highest,
            )

    def grad_three(part, image):
        return lax.dot_general(
            logit[0, part * nb + image],
            head,
            (((0,), (0,)), ((), ())),
            preferred_element_type=f32,
            precision=highest,
        )

    reduce_four[r, 2 * nb : 2 * nb + 8, :] = head_grad
    for row, value in enumerate([loss] + bias_grad):
        reduce_four[r, 2 * nb + 2 + row : 2 * nb + 3 + row, :] = jnp.broadcast_to(
            jnp.sum(value, 1, keepdims=True), (1, slim)
        )
    back_sums(reduce_four, z_three, dy_high, gain_three, shift_three, grad_three)
    total = all_reduce(3, reduce_four)

    def put_high(part, image, value):
        dz_high[1 + part // 2, part % 2, rows_of(image), :] = value

    gain_grad, shift_grad = back_apply(
        total, z_three, dy_high, inv_three, gain_three, size_high, put_high
    )
    sums_ref[b] = jnp.zeros_like(sums_ref[b])
    sums_ref[b, 4:5, :slim] = gain_grad
    sums_ref[b, 4:5, slim : 2 * slim] = shift_grad
    sums_ref[b, 5:6, :slim] = total[2 * nb : 2 * nb + 1]
    sums_ref[b, 5:6, slim : 2 * slim] = total[2 * nb + 1 : 2 * nb + 2]
    for row in range(3):
        sums_ref[b, 6 + row : 7 + row, :slim] = total[2 * nb + 2 + row : 2 * nb + 3 + row]
    sums_ref[b, 9:10, :] = jnp.broadcast_to(count, (1, wide))

    def edges(number, source_up, target_up, source_down, target_down):
        def higher():
            return remote(
                source_up,
                target_up,
                edge_send.at[number, 0],
                edge_recv.at[number, 0],
                ring(r + 1, nr),
                b,
            )

        def lower():
            return remote(
                source_down,
                target_down,
                edge_send.at[number, 1],
                edge_recv.at[number, 1],
                ring(r - 1, nr),
                b,
            )

        def begin():
            @pl.when(r + 1 < nr)
            def _():
                higher().start()

            @pl.when(r > 0)
            def _():
                lower().start()

        def finish():
            @pl.when(r + 1 < nr)
            def _():
                higher().wait_send()
                lower().wait_recv()

            @pl.when(r > 0)
            def _():
                lower().wait_send()
                higher().wait_recv()

        return begin, finish

    def widen_high(row):
        even, odd = dz_high[row, 0], dz_high[row, 1]
        shifted_high[row, 0, :, :slim] = odd
        shifted_high[row, 0, :, slim : 2 * slim] = even
        shifted_high[row, 0, :, 2 * slim :] = shift_down(odd.astype(f32)).astype(bf16)
        shifted_high[row, 1, :, :slim] = shift_up(even.astype(f32)).astype(bf16)
        shifted_high[row, 1, :, slim : 2 * slim] = odd
        shifted_high[row, 1, :, 2 * slim :] = even

    begin, finish = edges(0, dz_high.at[2], dz_high.at[0], dz_high.at[1], dz_high.at[3])
    begin()
    widen_high(1)
    widen_high(2)
    finish()
    widen_high(0)
    widen_high(3)
    spreads = []
    own_high = []
    for part in range(4):
        e, f = part // 2, part % 2
        total = 0.0
        for dy in range(3):
            total = total + dot_nn(
                shifted_high[e + 2 - dy, f], w_three[dy * taps_high : (dy + 1) * taps_high, :C0]
            )
        for j in range(nb):
            send_high[part, j] = total[:, j * slim : (j + 1) * slim].astype(bf16)

            @pl.when(b == j)
            def _():
                dy_high[part] = total[:, j * slim : (j + 1) * slim]

        spread = Spread(
            high_send.at[part],
            high_recv.at[part],
            lambda other, part=part: send_high.at[part, other],
            lambda j, part=part: recv_high.at[part, j],
        )
        spread.begin()
        spreads.append(spread)

    def put_grad(first, across, value, rows, start):
        for row, number in rows:
            for k in range(value.shape[1] // TILE):
                grad_ref[first + number * across + start + k] = value[
                    row : row + TILE, k * TILE : (k + 1) * TILE
                ].astype(bf16)

    out, width, taps, first = layers[3]
    for e in range(2):
        for f in range(2):
            turned_high[e, :, f * px : (f + 1) * px] = shifted_high[1 + e, f].T
    for dy in range(3):
        rows = [(dx * slim, 3 * dy + dx) for dx in range(3)]
        for half, source in enumerate((u_full, x_skip)):
            total = 0.0
            for e in range(2):
                for f in range(2):
                    value = source[e + dy, f].reshape(px, C0)
                    total = total + dot_nn(turned_high[e, :, f * px : (f + 1) * px], value)
            put_grad(first, width // TILE, total, rows, half * (C0 // TILE))
    for part in range(4):
        spreads[part].finish()
        total = dy_high[part]
        for step in range(1, nb):
            total = total + recv_high[part, ring(b + step, nb)].astype(f32)
        dub[:, part * slim : (part + 1) * slim] = total.astype(bf16)

    def input_low(number, product):
        for j in range(nb):
            total = product(j)
            send_low[j] = total.astype(bf16)

            @pl.when(b == j)
            def _():
                dy_low[0] = total

        spread = Spread(
            all_send.at[number],
            all_recv.at[number],
            lambda other: send_low.at[other],
            lambda j: recv_low.at[number - 1, j],
        )
        spread.begin()

        def finish():
            spread.finish()
            total = dy_low[0]
            for step in range(1, nb):
                total = total + recv_low[number - 1, ring(b + step, nb)].astype(f32)
            dy_low[0] = total

        return finish

    finish_sum = input_low(
        1, lambda j: dot_nn(dub[...], w_up[:, j * wide : (j + 1) * wide])
    )
    out, width, taps, first = layers[2]
    turned_low[: 4 * slim, :] = dub[...].T
    for j in range(nb):
        total = dot_nn(turned_low[: 4 * slim, :], a_two[:, j * wide : (j + 1) * wide])
        rows = [(part * slim, part) for part in range(4)]
        put_grad(first, width // TILE, total, rows, j * (wide // TILE))
    finish_sum()

    def back_low(number, z_ref, inv_ref, gain, shift):
        def grad_of(part, image):
            return dy_low[0, rows_of(image), :]

        buffer = reduce_wide.at[number - 2]
        back_sums(buffer, z_ref, dy_low, gain, shift, grad_of)
        total = all_reduce(number, buffer)

        def put(part, image, value):
            dz_low[1, rows_of(image), :] = value

        return back_apply(total, z_ref, dy_low, inv_ref, gain, size_low, put)

    def widen_low(row):
        value = dz_low[row]
        wider = value.astype(f32)
        shifted_low[row, :, :wide] = shift_up(wider).astype(bf16)
        shifted_low[row, :, wide : 2 * wide] = value
        shifted_low[row, :, 2 * wide :] = shift_down(wider).astype(bf16)

    def weight_low(number, source):
        out, width, taps, first = layers[number]
        turned_low[...] = shifted_low[1].T
        chunk = 2 * TILE
        for dy in range(3):
            rows = []
            for dx in range(3):
                for ob in range(wide // TILE):
                    rows.append((dx * wide + ob * TILE, ob * taps + 3 * dy + dx))
            for j in range(width // chunk):
                total = dot_nn(turned_low[...], source(dy, j * chunk, chunk))
                put_grad(first, width // TILE, total, rows, j * (chunk // TILE))

    gain_grad, shift_grad = back_low(4, z_two, inv_two, gain_two, shift_two)
    sums_ref[b, 2:3, :] = gain_grad
    sums_ref[b, 3:4, :] = shift_grad
    begin, finish = edges(1, dz_low.at[1], dz_low.at[0], dz_low.at[1], dz_low.at[2])
    begin()
    widen_low(1)
    finish()
    widen_low(0)
    widen_low(2)

    def product_two(j):
        total = 0.0
        for dy in range(3):
            total = total + dot_nn(
                shifted_low[2 - dy],
                w_two[3 * dy * wide : 3 * (dy + 1) * wide, j * wide : (j + 1) * wide],
            )
        return total

    finish_sum = input_low(2, product_two)
    weight_low(1, lambda dy, start, size: a_one[dy, :, start : start + size])
    finish_sum()
    gain_grad, shift_grad = back_low(5, z_one, inv_one, gain_one, shift_one)
    sums_ref[b, 0:1, :] = gain_grad
    sums_ref[b, 1:2, :] = shift_grad
    spread = Spread(
        all_send.at[3], all_recv.at[3], lambda other: sums_ref.at[b], lambda j: sums_ref.at[j]
    )
    spread.begin()
    widen_low(1)
    weight_low(0, lambda dy, start, size: x_one[dy].reshape(px, C0)[:, start : start + size])
    spread.finish()


def run_step(copies, place, bias, image, skip, lab, wide_rows, narrow_rows):
    nr, nb = lax.axis_size("rows"), lax.axis_size("blk")
    cols = image.shape[0]
    px = nb * cols
    wide, slim = C1 // nb, C0 // nb
    vmem = pl.BlockSpec(memory_space=pltpu.VMEM)
    smem = pl.BlockSpec(memory_space=pltpu.SMEM)
    dma = pltpu.SemaphoreType.DMA
    scratch = [
        pltpu.VMEM((3, nb, cols, C0), bf16),
        pltpu.VMEM((4, 2, nb, cols, C0), bf16),
        pltpu.VMEM((nb, 4, 8, cols), f32),
        pltpu.VMEM((9 * wide, C0), bf16),
        pltpu.VMEM((9 * wide, C1), bf16),
        pltpu.VMEM((4 * slim, C1), bf16),
        pltpu.VMEM((9 * slim, 2 * C0), bf16),
        pltpu.VMEM((3, px, C1), bf16),
        pltpu.VMEM((px, C1), bf16),
        pltpu.VMEM((4, 2, px, C0), bf16),
        pltpu.VMEM((1, px, wide), f32),
        pltpu.VMEM((1, px, wide), f32),
        pltpu.VMEM((4, px, slim), f32),
        pltpu.VMEM((1, px, wide), f32),
        pltpu.VMEM((4, px, slim), f32),
        pltpu.VMEM((8, wide), f32),
        pltpu.VMEM((8, wide), f32),
        pltpu.VMEM((8, slim), f32),
        pltpu.VMEM((3, px, wide), bf16),
        pltpu.VMEM((4, 2, px, slim), bf16),
        pltpu.VMEM((3, px, 3 * wide), bf16),
        pltpu.VMEM((4, 2, px, 3 * slim), bf16),
        pltpu.VMEM((3 * wide, px), bf16),
        pltpu.VMEM((2, 3 * slim, 2 * px), bf16),
        pltpu.VMEM((px, 4 * slim), bf16),
        pltpu.VMEM((4, nb, px, slim), bf16),
        pltpu.VMEM((4, nb, px, slim), bf16),
        pltpu.VMEM((nb, px, wide), bf16),
        pltpu.VMEM((2, nb, px, wide), bf16),
        pltpu.VMEM((nb, 4 * nb, 8, cols), f32),
        pltpu.VMEM((4, nr, 2 * nb + 8, wide), f32),
        pltpu.VMEM((2, nr, 2 * nb + 8, slim), f32),
        dma(()),
        dma((6, nb, 2)),
        dma((6, nb)),
        dma((6, nb, 2)),
        dma((6, nb, 2)),
        dma((6, nr)),
        dma((6, nr)),
        dma((4, nb)),
        dma((4, nb)),
        dma((4, nb)),
        dma((4, nb)),
        dma((2, 2)),
        dma((2, 2)),
    ]
    return pl.pallas_call(
        functools.partial(step_kernel, nr, nb, cols),
        out_shape=(
            jax.ShapeDtypeStruct(copies.shape, bf16),
            jax.ShapeDtypeStruct((nb, 16, wide), f32),
        ),
        in_specs=[pl.BlockSpec(memory_space=pl.ANY), smem, smem, vmem, vmem, vmem, vmem, vmem],
        out_specs=(vmem, vmem),
        scratch_shapes=scratch,
        compiler_params=pltpu.CompilerParams(
            collective_id=0, has_side_effects=True, vmem_limit_bytes=60 * 2**20
        ),
    )(copies, place, bias, image, skip, lab, wide_rows, narrow_rows)


LANES = 128


def inverse_factor_kernel(stat_ref, inverse_ref, factor_ref):
    order = stat_ref.shape[0]
    tile = (8, LANES)
    sub = lax.broadcasted_iota(jnp.int32, tile, 0)

    def eliminate(source_ref, base, start, first, count, accs):
        def body(group, accs):
            top = pl.multiple_of(group * 8, 8)
            for unit in range(8):
                value = source_ref[top + unit, pl.ds(start, 8), :]
                accs = tuple(
                    accs[c]
                    - value
                    * jnp.broadcast_to(factor_ref[top + unit, pl.ds(base + c, 1), :], tile)
                    for c in range(8)
                )
            return accs

        return list(lax.fori_loop(first, count, body, tuple(accs)))

    def block(kb, _):
        base = pl.multiple_of(kb * 8, 8)
        accs = [stat_ref[base + c, pl.ds(base, 8), :] for c in range(8)]
        accs = eliminate(factor_ref, base, base, 0, kb, accs)
        scale = []
        coef = {}
        for c in range(8):
            scale.append(jnp.broadcast_to(lax.rsqrt(accs[c][c : c + 1, :]), tile))
            accs[c] = accs[c] * scale[c]
            for d in range(c + 1, 8):
                coef[(c, d)] = jnp.broadcast_to(accs[c][d : d + 1, :], tile)
                accs[d] = accs[d] - accs[c] * coef[(c, d)]
        for c in range(8):
            factor_ref[base + c, pl.ds(base, 8), :] = jnp.where(sub >= c, accs[c], 0.0)

        def finish(accs, target_ref, start):
            accs = list(accs)
            for c in range(8):
                for e in range(c):
                    accs[c] = accs[c] - accs[e] * coef[(e, c)]
                accs[c] = accs[c] * scale[c]
                target_ref[base + c, pl.ds(start, 8), :] = accs[c]

        def below(group, _):
            start = pl.multiple_of(group * 8, 8)
            accs = [stat_ref[base + c, pl.ds(start, 8), :] for c in range(8)]
            finish(eliminate(factor_ref, base, start, 0, kb, accs), factor_ref, start)
            return 0

        def left(group, _):
            start = pl.multiple_of(group * 8, 8)
            accs = [jnp.zeros(tile, jnp.float32) for c in range(8)]
            finish(eliminate(inverse_ref, base, start, group, kb, accs), inverse_ref, start)
            return 0

        def clear(group, _):
            start = pl.multiple_of(group * 8, 8)
            for c in range(8):
                inverse_ref[base + c, pl.ds(start, 8), :] = jnp.zeros(tile, jnp.float32)
            return 0

        lax.fori_loop(kb + 1, order // 8, below, 0)
        lax.fori_loop(0, kb, left, 0)
        finish([jnp.where(sub == c, 1.0, 0.0) for c in range(8)], inverse_ref, base)
        lax.fori_loop(kb + 1, order // 8, clear, 0)
        return 0

    lax.fori_loop(0, order // 8, block, 0)


def inverse_factors(grams):
    count, order = grams.shape[0], grams.shape[-1]
    chunks = -(-count // LANES)
    spare = chunks * LANES - count
    eye = jnp.broadcast_to(jnp.eye(order, dtype=jnp.float32), (spare, order, order))
    lanes = jnp.concatenate([grams, eye], 0).transpose(1, 2, 0)
    block = pl.BlockSpec((order, order, LANES), lambda chunk: (0, 0, chunk))
    result = pl.pallas_call(
        inverse_factor_kernel,
        grid=(chunks,),
        out_shape=jax.ShapeDtypeStruct(lanes.shape, jnp.float32),
        in_specs=[block],
        out_specs=block,
        scratch_shapes=[pltpu.VMEM((order, order, LANES), jnp.float32)],
        compiler_params=pltpu.CompilerParams(vmem_limit_bytes=56 * 2**20),
    )(lanes)
    return result.transpose(2, 0, 1)[:count]


def orthonormal(stats, bases):
    products = [
        jnp.matmul(stat, basis, precision=highest)[0] for stat, basis in zip(stats, bases)
    ]
    grams = [
        jnp.matmul(jnp.swapaxes(product, -1, -2), product, precision=highest)
        for product in products
    ]
    inverses = inverse_factors(jnp.concatenate(grams, 0))
    count = products[0].shape[0]
    return [
        jnp.matmul(product, jnp.swapaxes(inverse, -1, -2), precision=highest)[None]
        for product, inverse in zip(products, (inverses[:count], inverses[count:]))
    ]


def soap_update(grads, master, first, second, left, right, left_stat, right_stat):
    rotated = jnp.matmul(
        jnp.matmul(jnp.swapaxes(left, -1, -2), grads, precision=highest), right, precision=highest
    )
    first_new = beta_one * first + (1.0 - beta_one) * rotated
    second_new = beta_two * second + (1.0 - beta_two) * rotated * rotated
    direction = (
        first_new
        / (1.0 - beta_one**STEP)
        / (jnp.sqrt(second_new / (1.0 - beta_two**STEP)) + adam_eps)
    )
    update = jnp.matmul(
        jnp.matmul(left, direction, precision=highest),
        jnp.swapaxes(right, -1, -2),
        precision=highest,
    )
    master_new = master - soap_rate * (update + soap_decay * master)
    left_new_stat = beta_stat * left_stat + (1.0 - beta_stat) * jnp.matmul(
        grads, jnp.swapaxes(grads, -1, -2), precision=highest
    )
    right_new_stat = beta_stat * right_stat + (1.0 - beta_stat) * jnp.matmul(
        jnp.swapaxes(grads, -1, -2), grads, precision=highest
    )
    left_new, right_new = orthonormal((left_new_stat, right_new_stat), (left, right))
    return (
        master_new,
        first_new,
        second_new,
        left_new,
        right_new,
        left_new_stat,
        right_new_stat,
    )


def adam_small(grads, value, first, second):
    first_new = beta_one * first + (1.0 - beta_one) * grads
    second_new = beta_two * second + (1.0 - beta_two) * grads * grads
    direction = (
        first_new
        / (1.0 - beta_one**STEP)
        / (jnp.sqrt(second_new / (1.0 - beta_two**STEP)) + adam_eps)
    )
    return (first_new, second_new, value - small_rate * (direction + small_decay * value))


def local(
    image,
    skip,
    labels,
    weight_map,
    valid,
    owner,
    master,
    first_moment,
    second_moment,
    left_basis,
    right_basis,
    left_stat,
    right_stat,
    norm_params,
    norm_first,
    norm_second,
    head_bias,
    bias_first,
    bias_second,
):
    shards = lax.axis_size("blk")
    shard = lax.axis_index("blk")
    cols = image.shape[2]
    copies = lax.all_gather(master.astype(bf16), "rows", axis=1, tiled=True)[0]
    slots = jnp.arange(owner.shape[0])
    place = jnp.sum(jnp.where(owner[None, :] == slots[:, None], slots[None, :], 0), 1)
    widths = (C1, C1, C1, C1, C0, C0)
    rows = []
    offset = 0
    for width in widths:
        part = width // shards
        rows.append(lax.dynamic_slice_in_dim(norm_params, offset + shard * part, part))
        offset = offset + width
    heads = norm_params[offset:].reshape(C0, 2)
    part = C0 // shards
    heads = lax.dynamic_slice_in_dim(heads, shard * part, part).T
    wide_rows = jnp.pad(jnp.stack(rows[:4]), ((0, 4), (0, 0)))
    narrow_rows = jnp.concatenate(
        [jnp.pad(jnp.stack(rows[4:]), ((0, 6), (0, 0))), jnp.pad(heads, ((0, 6), (0, 0)))]
    )
    valid_float = valid.astype(f32)
    scales = valid_float * weight_map.astype(f32) * 0.125
    lab = jnp.stack([scales, labels.astype(f32), valid_float]).reshape(3, 2, cols, 2)
    lab = lab.transpose(1, 3, 0, 2).reshape(4, 3, cols)
    lab = jnp.pad(lab, ((0, 0), (0, 5), (0, 0)))
    skip = skip.reshape(2, cols, 2, C0).transpose(0, 2, 1, 3)
    blocks, sums = run_step(
        copies, place.astype(jnp.int32), head_bias, image[0, 0], skip, lab, wide_rows, narrow_rows
    )
    grads = lax.psum_scatter(
        blocks[owner].astype(f32), "rows", scatter_dimension=0, tiled=True
    )[None]
    loss_sum, valid_count = sums[0, 6, 0], sums[0, 9, 0]
    grad_bias = sums[0, 7:9, 0]
    grad_head = jnp.stack([sums[:, 5, :part].reshape(-1), sums[:, 5, part : 2 * part].reshape(-1)], 1)
    small = jnp.concatenate(
        [sums[:, row].reshape(-1) for row in range(4)]
        + [
            sums[:, 4, :part].reshape(-1),
            sums[:, 4, part : 2 * part].reshape(-1),
            grad_head.reshape(-1),
        ]
    )
    soap = soap_update(
        grads, master, first_moment, second_moment, left_basis, right_basis, left_stat, right_stat
    )
    norm_new = adam_small(small, norm_params, norm_first, norm_second)
    bias_new = adam_small(grad_bias, head_bias, bias_first, bias_second)
    return (
        loss_sum,
        valid_count,
        soap[0],
        soap[0].astype(jnp.bfloat16),
        soap[1],
        soap[2],
        soap[3],
        soap[4],
        soap[5],
        soap[6],
        norm_new[0],
        norm_new[1],
        norm_new[2],
        bias_new[0],
        bias_new[1],
        bias_new[2],
    )


def solution(mesh):
    placed = (
        P("blk", "rows", None, None),
        P("blk", "rows", None, None),
        P("blk", "rows", None),
        P("blk", "rows", None),
        P("blk", "rows", None),
        P(),
        P("blk", "rows", None, None),
        P("blk", "rows", None, None),
        P("blk", "rows", None, None),
        P("blk", "rows", None, None),
        P("blk", "rows", None, None),
        P("blk", "rows", None, None),
        P("blk", "rows", None, None),
        P(),
        P(),
        P(),
        P(),
        P(),
        P(),
    )
    return jax.shard_map(
        local,
        mesh=mesh,
        in_specs=placed,
        out_specs=(
            P(),
            P(),
            P("blk", "rows", None, None),
            P("blk", "rows", None, None),
            P("blk", "rows", None, None),
            P("blk", "rows", None, None),
            P("blk", "rows", None, None),
            P("blk", "rows", None, None),
            P("blk", "rows", None, None),
            P("blk", "rows", None, None),
            P(),
            P(),
            P(),
            P(),
            P(),
            P(),
        ),
        check_vma=False,
    )
```

time: 1140 us -> 678 us (0.59)
  Pallas kernels: 44.1 us -> 295 us
  blocking collectives: 208 us -> 0 us
  local copies, waits for them, and re-layouts: 252 us -> 68.2 us
  waiting for transfers between devices: 328 us -> 189 us
  matrix products: 156 us -> 75 us
  other arithmetic: 84.3 us -> 29.2 us
  starting transfers between devices: 34.8 us -> 0.08 us
    pallas_call x0 -> x1, Pallas kernels: none -> 250 us  [run_step(): pl.pallas_call(functools.partial(step_kernel, nr, nb, cols), out_shape=(j...]
    psum x8 -> x0, blocking collectives: 122 us -> none  [the longest x3 46 us: group_forward(): first_sum, second_sum = lax.psum((first_sum, second_sum), 'rows')]
    all_gather x7 -> x0, blocking collectives: 85 us -> none  [the longest x4 42.2 us: local(): lax.all_gather(part, 'blk', axis=0, tiled=True)]
    reduce_scatter x4 -> x1, waiting for transfers between devices: 212 us -> 128 us  [local(): lax.psum_scatter(blocks[owner].astype(f32), 'rows', scatter_dimension=0,...]
    dot_general x87 -> x0, matrix products: 81.8 us -> none  [the longest x31 31.6 us: tap_products(): lax.dot_general(views[tap], piece[:, tap, :], (((1,), (1,)), ((), ())), p...]
    unnamed x279 -> x58, local copies, waits for them, and re-layouts: 56.1 us -> 4.67 us
    all_gather x3 -> x1, waiting for transfers between devices: 106 us -> 60.8 us  [local(): copies = lax.all_gather(master.astype(bf16), 'rows', axis=1, tiled=True)[0]]
    ppermute x10 -> x0, starting transfers between devices: 34.3 us -> none  [the longest x5 21.3 us: padded_2(): lax.ppermute(lax.slice_in_dim(block, 0, width, axis=dim), axis, backward)]
  transfers between devices with their start and end apart: 17 -> 2, of which waited for: 10 -> 2; matrix products, arithmetic and copies ran while one was open for 8% -> 2% of each run, Pallas kernels for 0% -> 0%
where the time goes in v2:
time: 678 us; the launch traced here: 671 us
  Pallas kernels  295 us (44%)
  waiting for transfers between devices  189 us (28%)
  matrix products  75 us (11%)
  local copies, waits for them, and re-layouts  68.2 us (10%)
  other arithmetic  29.2 us (4%)
  between operations  15 us (2%)
    pallas_call x1, Pallas kernels, run_step(): pl.pallas_call(functools.partial(step_kernel, nr, nb, cols), out_shape=(j...  250 us
    reduce_scatter x1, waiting for transfers between devices, local(): lax.psum_scatter(blocks[owner].astype(f32), 'rows', scatter_dimension=0,...  128 us
    all_gather x1, waiting for transfers between devices, local(): copies = lax.all_gather(master.astype(bf16), 'rows', axis=1, tiled=True)[0]  60.8 us
    pallas_call x1, Pallas kernels, inverse_factors(): pl.pallas_call(inverse_factor_kernel, grid=(chunks,), out_shape=jax.Shape...  44.1 us
    slice x2, local copies, waits for them, and re-layouts, orthonormal(): inverses[count:]  19.8 us
    dot_general x2, matrix products, orthonormal(): jnp.matmul(product, jnp.swapaxes(inverse, -1, -2), precision=highest)[None]  19.3 us
    gather x1, local copies, waits for them, and re-layouts, local(): blocks[owner].astype(f32)  14.9 us
    convert_element_type x1, other arithmetic, local(): blocks[owner].astype(f32)  13.7 us
  transfers between devices with their start and end apart: 2, of which 2 were waited for; matrix products, arithmetic and copies ran while one was open for 2% of the time, Pallas kernels for 0%

profile of v2, /device:TPU:1, one launch (start us, length us, event | category | flops | bytes accessed | tf_op | source)
XLA Modules:
  0.0 671.2 jit_solution(11698760891280341003)
XLA Ops:
  7.3 3.2 bitcast_convert_fusion
  15.6 60.8 %all-gather.2.cloned.1.call-done = bf16[1,320,128,128]{3,2,0,1:T(8,128)(2,1)} async-done(((bf16[1,40,128,128]{3,2,0,1:T(8,128)(2,1)}), bf16[1,320,128,128]{3,2,0,1:T(8,128)(2,1)}) %all-gather.2.cloned.1.call-update) | async-done | bytes 10485776 | tf_op jit(solution)/shard_map/all_gather | solution.py:1108
  76.4 250.5 %shard_map.306 = (bf16[320,128,128]{2,1,0:T(8,128)(2,1)}, f32[4,16,256]{2,1,0:T(8,128)}) custom-call(bf16[320,128,128]{2,1,0:T(8,128)(2,1)} %bitcast.117, s32[320]{0:T(512)} %select_reduce_fusion.place_ref, f32[2]{0:T(128)} %bias_ref.1, bf16[96,512]{1,0:T(8,128)(2,1)} %bitcast.120, bf16[2,2,96,512]{3,2,1,0:T(8,128)(2,1)} %bitcast.118, ...), custom_call_target="tpu_custom_call" | custom-call | tf_op jit(solution)/shard_map/pallas_call | solution.py:915
  326.9 14.9 %gather_fusion = bf16[320,128,128]{2,1,0:T(8,128)(2,1)} fusion(bf16[320,128,128]{2,1,0:T(8,128)(2,1)} %get-tuple-element.19, s32[1024]{0:T(1024)S(1)} %pad_clamp_fusion), kind=kCustom, calls=%fused_computation | custom fusion | bytes 20972800 | tf_op jit(solution)/shard_map/gather | solution.py:1135
  341.8 13.7 %convert_element_type.32 = f32[320,128,128]{2,1,0:T(8,128)} convert(bf16[320,128,128]{2,1,0:T(8,128)(2,1)} %gather_fusion) | non-fusion elementwise | flops 5242880 | bytes 31457280 | tf_op jit(solution)/shard_map/convert_element_type | solution.py:1135
  361.0 128.4 %reduce-scatter.2.cloned.1.call-done = f32[40,128,128]{2,1,0:T(8,128)} async-done(((f32[320,128,128]{2,1,0:T(8,128)}), f32[40,128,128]{2,1,0:T(8,128)}) %reduce-scatter.2.cloned.1.call-update) | async-done | bytes 2621456 | tf_op jit(solution)/shard_map/reduce_scatter | solution.py:1134
  489.4 9.0 %bitcast_add_fusion.1 = f32[1,40,128,128]{3,2,1,0:T(8,128)S(1)} fusion(f32[1,40,128,128]{3,2,1,0:T(8,128)} %param.30, f32[40,128,128]{2,1,0:T(8,128)} %reduce-scatter.2.cloned.1.call-done), kind=kOutput, calls=%fused_computation.18 | convolution fusion | flops 1008599040 | bytes 7864320 | tf_op jit(solution)/shard_map/dot_general | solution.py:1055
  502.9 6.4 fusion.50
  509.4 6.5 copy.103
  515.9 7.8 %bitcast_add_fusion = f32[1,40,128,128]{3,2,1,0:T(8,128)S(1)} fusion(f32[1,40,128,128]{3,2,1,0:T(8,128)} %param.31, f32[40,128,128]{2,1,0:T(8,128)} %reduce-scatter.2.cloned.1.call-done), kind=kOutput, calls=%fused_computation.15 | convolution fusion | flops 1008599040 | bytes 7864320 | tf_op jit(solution)/shard_map/dot_general | solution.py:1058
  523.7 3.0 fusion.10
  528.2 6.0 fusion.51
  534.3 6.6 copy.104
  544.3 9.1 %maximum_bitcast_fusion.stat_ref = f32[128,128,128]{2,1,0:T(8,128)} fusion(f32[48,128,128]{0,2,1:T(8,128)S(1)} %broadcast_in_dim.41, f32[40,128,128]{0,2,1:T(8,128)S(1)} %copy-done.4, f32[40,128,128]{0,2,1:T(8,128)} %copy.103), kind=kLoop, calls=%fused_computation.1 | loop fusion | flops 4194304 | bytes 16777216 | tf_op jit(solution)/shard_map/transpose | solution.py:1008
  553.4 44.1 %shard_map.307 = f32[128,128,128]{2,1,0:T(8,128)} custom-call(f32[128,128,128]{2,1,0:T(8,128)} %maximum_bitcast_fusion.stat_ref), custom_call_target="tpu_custom_call" | custom-call | tf_op jit(solution)/shard_map/pallas_call | solution.py:1010
  597.4 13.3 %fusion.45 = (f32[40,128,128]{0,2,1:T(8,128)}, f32[40,128,128]{0,2,1:T(8,128)}) fusion(f32[128,128,128]{0,2,1:T(8,128)} %bitcast.116), kind=kLoop, calls=%fused_computation.83 | loop fusion | bytes 10485760 | tf_op jit(solution)/shard_map/slice | solution.py:1034
  610.7 6.6 copy.106
  617.3 9.6 %convolution_bitcast_fusion = f32[1,40,128,128]{3,2,1,0:T(8,128)} fusion(f32[40,128,128]{2,1,0:T(8,128)} %copy-done.3, f32[40,128,128]{2,1,0:T(8,128)} %copy.106), kind=kOutput, calls=%fused_computation.36 | convolution fusion | flops 1006632960 | bytes 7864320 | tf_op jit(solution)/shard_map/dot_general | solution.py:1033
  626.9 6.8 %copy.105 = f32[40,128,128]{2,1,0:T(8,128)} copy(f32[40,128,128]{0,2,1:T(8,128)} %get-tuple-element.27) | data formatting | bytes 5242880 | tf_op jit(solution)/shard_map/slice | solution.py:1034
  633.7 9.7 %convolution_bitcast_fusion.1 = f32[1,40,128,128]{3,2,1,0:T(8,128)} fusion(f32[40,128,128]{2,1,0:T(8,128)} %copy-done.2, f32[40,128,128]{2,1,0:T(8,128)} %copy.105), kind=kOutput, calls=%fused_computation.37 | convolution fusion | flops 1006632960 | bytes 7864320 | tf_op jit(solution)/shard_map/dot_general | solution.py:1033
  643.4 4.5 fusion.8
  647.9 3.8 bitcast_add_fusion.3
  651.8 4.5 fusion.17
  656.3 7.6 %fusion.49 = (bf16[1,40,128,128]{3,2,1,0:T(8,128)(2,1)}, f32[1,40,128,128]{3,2,1,0:T(8,128)}) fusion(f32[1,40,128,128]{3,2,1,0:T(8,128)S(1)} %copy-done.9, f32[40,128,128]{1,2,0:T(8,128)S(1)} %fusion.17, f32[1,40,128,128]{3,2,1,0:T(8,128)S(1)} %copy-done), kind=kOutput, calls=%fused_computation.87 | convolution fusion | flops 1009909760 | bytes 11796480 | tf_op jit(solution)/shard_map/dot_general | solution.py:1049
  (100 shorter events, 19.9 us)
Async XLA Ops:
  7.2 516.5 %copy-start = (f32[1,40,128,128]{3,2,1,0:T(8,128)S(1)}, f32[1,40,128,128]{3,2,1,0:T(8,128)}, u32[]{:S(2)}) copy-start(f32[1,40,128,128]{3,2,1,0:T(8,128)} %param.29) | copy-start | bytes 7864324
  7.2 3.4 slice-start
  7.2 3.7 copy-start.14
  7.2 69.2 %all-gather.2.cloned.1.call-start = ((), (), s32[]{:S(2)}) async-start(), calls=%async_computation.1 | async-start | bytes 11796480 | tf_op jit(solution)/shard_map/all_gather | solution.py:1108
  10.5 1.9 copy-start.22
  10.5 3.0 copy-start.15
  10.5 3.1 copy-start.19
  10.5 478.9 %reduce-scatter.2.cloned.1.call-start = ((), (), s32[]{:S(2)}) async-start(), calls=%async_computation.2 | async-start | bytes 23592960 | tf_op jit(solution)/shard_map/reduce_scatter | solution.py:1134
  355.5 4.3 copy-start.20
  355.5 4.3 copy-start.23
  355.5 4.3 copy-start.24
  355.5 4.8 copy-start.16
  355.5 4.8 copy-start.17
  489.4 9.0 %copy-start.7 = (f32[1,40,128,128]{3,2,1,0:T(8,128)S(1)}, f32[1,40,128,128]{3,2,1,0:T(8,128)}, u32[]{:S(2)}) copy-start(f32[1,40,128,128]{3,2,1,0:T(8,128)} %param.28) | copy-start | bytes 7864324
  498.4 3.0 copy-start.5
  523.7 3.0 copy-start.6
  540.9 3.4 copy-start.4
  633.6 9.7 %copy-start.1 = (f32[40,128,128]{2,1,0:T(8,128)S(1)}, f32[40,128,128]{2,1,0:T(8,128)}, u32[]{:S(2)}) copy-start(f32[40,128,128]{2,1,0:T(8,128)} %reduce-scatter.2.cloned.1.call-done) | copy-start | bytes 7864324
  633.6 9.7 %copy-start.8 = (f32[1,40,128,128]{3,2,1,0:T(8,128)S(1)}, f32[1,40,128,128]{3,2,1,0:T(8,128)}, u32[]{:S(2)}) copy-start(f32[1,40,128,128]{3,2,1,0:T(8,128)} %param.28) | copy-start | bytes 7864324
  643.4 4.5 copy-start.10
  643.4 4.5 copy-start.11
  651.7 4.6 copy-start.12
  651.8 4.6 copy-start.13
  651.8 4.6 copy-start.9
  (4 other events, 6.3 us)
Sparse Core Ops, SparseCore 0:
  10.6 65.7 all-gather.1
  355.6 133.7 reduce-scatter.1

commit v3 on v2

--- a/solution.py
+++ b/solution.py
@@ -1000,74 +1000,320 @@
     lax.fori_loop(0, order // 8, block, 0)
 
 
-def inverse_factors(grams):
-    count, order = grams.shape[0], grams.shape[-1]
-    chunks = -(-count // LANES)
-    spare = chunks * LANES - count
-    eye = jnp.broadcast_to(jnp.eye(order, dtype=jnp.float32), (spare, order, order))
-    lanes = jnp.concatenate([grams, eye], 0).transpose(1, 2, 0)
-    block = pl.BlockSpec((order, order, LANES), lambda chunk: (0, 0, chunk))
-    result = pl.pallas_call(
-        inverse_factor_kernel,
-        grid=(chunks,),
-        out_shape=jax.ShapeDtypeStruct(lanes.shape, jnp.float32),
-        in_specs=[block],
-        out_specs=block,
-        scratch_shapes=[pltpu.VMEM((order, order, LANES), jnp.float32)],
-        compiler_params=pltpu.CompilerParams(vmem_limit_bytes=56 * 2**20),
-    )(lanes)
-    return result.transpose(2, 0, 1)[:count]
-
-
-def orthonormal(stats, bases):
-    products = [
-        jnp.matmul(stat, basis, precision=highest)[0] for stat, basis in zip(stats, bases)
+def product(left, right, left_dim, right_dim):
+    return lax.dot_general(
+        left,
+        right,
+        (((left_dim,), (right_dim,)), ((), ())),
+        preferred_element_type=f32,
+        precision=highest,
+    )
+
+
+def soap_block(index, grad, ins, outs):
+    master_ref, first_ref, second_ref, left_ref, right_ref, left_stat_ref, right_stat_ref = ins
+    left, right = left_ref[index], right_ref[index]
+    rotated = product(product(left, grad, 0, 0), right, 1, 0)
+    first = beta_one * first_ref[index] + (1.0 - beta_one) * rotated
+    second = beta_two * second_ref[index] + (1.0 - beta_two) * rotated * rotated
+    direction = (
+        first
+        / (1.0 - beta_one**STEP)
+        / (jnp.sqrt(second / (1.0 - beta_two**STEP)) + adam_eps)
+    )
+    update = product(product(left, direction, 1, 0), right, 1, 1)
+    master = master_ref[index]
+    master = master - soap_rate * (update + soap_decay * master)
+    values = [master, master.astype(bf16), first, second]
+    moved = []
+    for stat_ref, basis, dim in ((left_stat_ref, left, 1), (right_stat_ref, right, 0)):
+        stat = beta_stat * stat_ref[index] + (1.0 - beta_stat) * product(grad, grad, dim, dim)
+        values.append(stat)
+        moved.append(product(stat, basis, 1, 0))
+    values = values + moved + [product(value, value, 0, 0) for value in moved]
+    for ref, value in zip(outs, values):
+        ref[index] = value
+
+
+def collect_kernel(nr, size, *refs):
+    (owner_ref, grad_ref), refs = refs[:2], refs[2:]
+    ins, refs = refs[:7], refs[7:]
+    outs, refs = refs[:10], refs[10:]
+    (
+        out_a,
+        in_a,
+        out_b,
+        in_b,
+        total,
+        in_buffer,
+        out_buffer,
+        copy_buffer,
+        a_send,
+        a_recv,
+        b_send,
+        b_recv,
+        in_sem,
+        out_sem,
+    ) = refs
+    r = lax.axis_index("rows")
+    b = lax.axis_index("blk")
+    core = lax.rem(r, 2)
+    chip = lax.div(r, 2)
+    chips = nr // 2
+    mate = r + 1 - 2 * core
+    count = ins[0].shape[0]
+    chunks = count // size
+
+    def device(chip, core):
+        return {"rows": 2 * chip + core, "blk": b}
+
+    barrier = pltpu.get_barrier_semaphore()
+    pl.semaphore_signal(
+        barrier, inc=1, device_id={"rows": mate, "blk": b}, device_id_type=MESH
+    )
+
+    def greet(step, _):
+        pl.semaphore_signal(
+            barrier,
+            inc=1,
+            device_id=device(lax.rem(chip + step, chips), core),
+            device_id_type=MESH,
+        )
+        return 0
+
+    lax.fori_loop(1, chips, greet, 0)
+    pl.semaphore_wait(barrier, chips)
+
+    def loads(chunk):
+        return [
+            pltpu.make_async_copy(
+                ref.at[pl.ds(chunk * size, size)],
+                in_buffer.at[chunk % 2, number],
+                in_sem.at[chunk % 2, number],
+            )
+            for number, ref in enumerate(ins)
+        ]
+
+    def stores(chunk):
+        copies = []
+        for number, ref in enumerate(outs):
+            source = (
+                copy_buffer.at[chunk % 2]
+                if number == 1
+                else out_buffer.at[chunk % 2, number - (number > 1)]
+            )
+            copies.append(
+                pltpu.make_async_copy(
+                    source, ref.at[pl.ds(chunk * size, size)], out_sem.at[chunk % 2, number]
+                )
+            )
+        return copies
+
+    def mine(to_chip, to_core, chunk, index):
+        return grad_ref[owner_ref[(2 * to_chip + to_core) * count + chunk * size + index]]
+
+    def send_a(chunk):
+        return pltpu.make_async_remote_copy(
+            src_ref=out_a.at[chunk],
+            dst_ref=in_a.at[chunk],
+            send_sem=a_send.at[chunk],
+            recv_sem=a_recv.at[chunk],
+            device_id={"rows": mate, "blk": b},
+            device_id_type=MESH,
+        )
+
+    def send_b(chunk, step):
+        other = lax.rem(chip + step, chips)
+        return pltpu.make_async_remote_copy(
+            src_ref=out_b.at[chunk, other],
+            dst_ref=in_b.at[chunk, chip],
+            send_sem=b_send.at[chunk, step],
+            recv_sem=b_recv.at[chunk, chip],
+            device_id=device(other, core),
+            device_id_type=MESH,
+        )
+
+    for copy in loads(0):
+        copy.start()
+    for chunk in range(chunks):
+
+        def fill(n, _, chunk=chunk):
+            to_chip, index = lax.div(n, size), lax.rem(n, size)
+            out_a[chunk, to_chip, index] = mine(to_chip, 1 - core, chunk, index)
+            return 0
+
+        lax.fori_loop(0, chips * size, fill, 0)
+        send_a(chunk).start()
+    for chunk in range(chunks):
+        send_a(chunk).wait_recv()
+
+        def join(step, _, chunk=chunk):
+            other = lax.rem(chip + step, chips)
+
+            def each(index, _):
+                value = mine(other, core, chunk, index).astype(f32)
+                value = value + in_a[chunk, other, index].astype(f32)
+                out_b[chunk, other, index] = value.astype(bf16)
+                return 0
+
+            lax.fori_loop(0, size, each, 0)
+            send_b(chunk, step).start()
+            return 0
+
+        lax.fori_loop(1, chips, join, 0)
+
+        def keep(index, _, chunk=chunk):
+            value = mine(chip, core, chunk, index).astype(f32)
+            total[chunk, index] = value + in_a[chunk, chip, index].astype(f32)
+            return 0
+
+        lax.fori_loop(0, size, keep, 0)
+    for chunk in range(chunks):
+        if chunk + 1 < chunks:
+            for copy in loads(chunk + 1):
+                copy.start()
+        for copy in loads(chunk):
+            copy.wait()
+        if chunk >= 2:
+            for copy in stores(chunk - 2):
+                copy.wait()
+
+        def arrive(step, _, chunk=chunk):
+            other = lax.rem(chip + step, chips)
+            pltpu.make_async_remote_copy(
+                src_ref=out_b.at[chunk, other],
+                dst_ref=in_b.at[chunk, other],
+                send_sem=b_send.at[chunk, step],
+                recv_sem=b_recv.at[chunk, other],
+                device_id=device(other, core),
+                device_id_type=MESH,
+            ).wait_recv()
+            return 0
+
+        lax.fori_loop(1, chips, arrive, 0)
+        slot = chunk % 2
+        chunk_ins = [in_buffer.at[slot, number] for number in range(7)]
+        chunk_outs = [out_buffer.at[slot, number] for number in range(9)]
+        chunk_outs.insert(1, copy_buffer.at[slot])
+
+        def work(index, _, chunk=chunk, chunk_ins=chunk_ins, chunk_outs=chunk_outs):
+            grad = lax.fori_loop(
+                1,
+                chips,
+                lambda step, value: value
+                + in_b[chunk, lax.rem(chip + step, chips), index].astype(f32),
+                total[chunk, index],
+            )
+            soap_block(index, grad, chunk_ins, chunk_outs)
+            return 0
+
+        lax.fori_loop(0, size, work, 0, unroll=2 if size % 2 == 0 else 1)
+        for copy in stores(chunk):
+            copy.start()
+    for chunk in range(chunks):
+        send_a(chunk).wait_send()
+        lax.fori_loop(
+            1, chips, lambda step, _, chunk=chunk: (send_b(chunk, step).wait_send(), 0)[1], 0
+        )
+        if chunk >= chunks - 2:
+            for copy in stores(chunk):
+                copy.wait()
+
+
+def basis_kernel(
+    left_gram_ref, right_gram_ref, left_ref, right_ref, new_left_ref, new_right_ref, stat_ref,
+    inverse_ref, factor_ref
+):
+    order = left_gram_ref.shape[1]
+    count = left_gram_ref.shape[0] // order
+    spare = LANES - 2 * count
+
+    def enter(row, _):
+        rows = pl.ds(row, count, stride=order)
+        values = [left_gram_ref[rows, :], right_gram_ref[rows, :]]
+        if spare:
+            column = lax.broadcasted_iota(jnp.int32, (spare, order), 1)
+            values.append(jnp.where(column == row, 1.0, 0.0))
+        stat_ref[row] = jnp.concatenate(values, 0).T
+        return 0
+
+    lax.fori_loop(0, order, enter, 0)
+    inverse_factor_kernel(stat_ref, inverse_ref, factor_ref)
+
+    def leave(row, _):
+        rows = pl.ds(row, count, stride=order)
+        value = inverse_ref[row].T
+        new_left_ref[rows, :] = value[:count]
+        new_right_ref[rows, :] = value[count : 2 * count]
+        return 0
+
+    lax.fori_loop(0, order, leave, 0)
+
+    def solve(index, _):
+        rows = pl.ds(pl.multiple_of(index * order, order), order)
+        new_left_ref[rows, :] = product(left_ref[rows, :], new_left_ref[rows, :], 1, 1)
+        new_right_ref[rows, :] = product(right_ref[rows, :], new_right_ref[rows, :], 1, 1)
+        return 0
+
+    lax.fori_loop(0, count, solve, 0, unroll=2 if count % 2 == 0 else 1)
+
+
+def soap_update(blocks, owner, states):
+    nr = lax.axis_size("rows")
+    count, order = states[0].shape[0], states[0].shape[-1]
+    size = 8 if count % 8 == 0 else count
+    chunks = count // size
+    anywhere = pl.BlockSpec(memory_space=pl.ANY)
+    vmem = pl.BlockSpec(memory_space=pltpu.VMEM)
+    shape = jax.ShapeDtypeStruct(states[0].shape, f32)
+    dma = pltpu.SemaphoreType.DMA
+    square = (order, order)
+    results = pl.pallas_call(
+        functools.partial(collect_kernel, nr, size),
+        out_shape=(shape, jax.ShapeDtypeStruct(shape.shape, bf16)) + (shape,) * 8,
+        in_specs=[pl.BlockSpec(memory_space=pltpu.SMEM), vmem] + [anywhere] * 7,
+        out_specs=[anywhere] * 10,
+        scratch_shapes=[
+            pltpu.VMEM((chunks, nr // 2, size) + square, bf16),
+            pltpu.VMEM((chunks, nr // 2, size) + square, bf16),
+            pltpu.VMEM((chunks, nr // 2, size) + square, bf16),
+            pltpu.VMEM((chunks, nr // 2, size) + square, bf16),
+            pltpu.VMEM((chunks, size) + square, f32),
+            pltpu.VMEM((2, 7, size) + square, f32),
+            pltpu.VMEM((2, 9, size) + square, f32),
+            pltpu.VMEM((2, size) + square, bf16),
+            dma((chunks,)),
+            dma((chunks,)),
+            dma((chunks, nr // 2)),
+            dma((chunks, nr // 2)),
+            dma((2, 7)),
+            dma((2, 10)),
+        ],
+        compiler_params=pltpu.CompilerParams(
+            collective_id=1, has_side_effects=True, vmem_limit_bytes=60 * 2**20
+        ),
+    )(owner, blocks, *states)
+    new_master, new_copy, new_first, new_second, new_left_stat, new_right_stat = results[:6]
+    lanes = pltpu.VMEM((order, order, LANES), f32)
+    flat = [value.reshape(count * order, order) for value in results[8:] + results[6:8]]
+    new_left, new_right = pl.pallas_call(
+        basis_kernel,
+        out_shape=(jax.ShapeDtypeStruct(flat[0].shape, f32),) * 2,
+        in_specs=[vmem] * 4,
+        out_specs=(vmem, vmem),
+        scratch_shapes=[lanes, lanes, lanes],
+        compiler_params=pltpu.CompilerParams(vmem_limit_bytes=60 * 2**20),
+    )(*flat)
+    return [
+        new_master,
+        new_copy,
+        new_first,
+        new_second,
+        new_left.reshape(shape.shape),
+        new_right.reshape(shape.shape),
+        new_left_stat,
+        new_right_stat,
     ]
-    grams = [
-        jnp.matmul(jnp.swapaxes(product, -1, -2), product, precision=highest)
-        for product in products
-    ]
-    inverses = inverse_factors(jnp.concatenate(grams, 0))
-    count = products[0].shape[0]
-    return [
-        jnp.matmul(product, jnp.swapaxes(inverse, -1, -2), precision=highest)[None]
-        for product, inverse in zip(products, (inverses[:count], inverses[count:]))
-    ]
-
-
-def soap_update(grads, master, first, second, left, right, left_stat, right_stat):
-    rotated = jnp.matmul(
-        jnp.matmul(jnp.swapaxes(left, -1, -2), grads, precision=highest), right, precision=highest
-    )
-    first_new = beta_one * first + (1.0 - beta_one) * rotated
-    second_new = beta_two * second + (1.0 - beta_two) * rotated * rotated
-    direction = (
-        first_new
-        / (1.0 - beta_one**STEP)
-        / (jnp.sqrt(second_new / (1.0 - beta_two**STEP)) + adam_eps)
-    )
-    update = jnp.matmul(
-        jnp.matmul(left, direction, precision=highest),
-        jnp.swapaxes(right, -1, -2),
-        precision=highest,
-    )
-    master_new = master - soap_rate * (update + soap_decay * master)
-    left_new_stat = beta_stat * left_stat + (1.0 - beta_stat) * jnp.matmul(
-        grads, jnp.swapaxes(grads, -1, -2), precision=highest
-    )
-    right_new_stat = beta_stat * right_stat + (1.0 - beta_stat) * jnp.matmul(
-        jnp.swapaxes(grads, -1, -2), grads, precision=highest
-    )
-    left_new, right_new = orthonormal((left_new_stat, right_new_stat), (left, right))
-    return (
-        master_new,
-        first_new,
-        second_new,
-        left_new,
-        right_new,
-        left_new_stat,
-        right_new_stat,
-    )
 
 
 def adam_small(grads, value, first, second):
@@ -1131,9 +1377,6 @@
     blocks, sums = run_step(
         copies, place.astype(jnp.int32), head_bias, image[0, 0], skip, lab, wide_rows, narrow_rows
     )
-    grads = lax.psum_scatter(
-        blocks[owner].astype(f32), "rows", scatter_dimension=0, tiled=True
-    )[None]
     loss_sum, valid_count = sums[0, 6, 0], sums[0, 9, 0]
     grad_bias = sums[0, 7:9, 0]
     grad_head = jnp.stack([sums[:, 5, :part].reshape(-1), sums[:, 5, part : 2 * part].reshape(-1)], 1)
@@ -1145,22 +1388,30 @@
             grad_head.reshape(-1),
         ]
     )
-    soap = soap_update(
-        grads, master, first_moment, second_moment, left_basis, right_basis, left_stat, right_stat
-    )
+    states = (
+        master,
+        first_moment,
+        second_moment,
+        left_basis,
+        right_basis,
+        left_stat,
+        right_stat,
+    )
+    soap = soap_update(blocks, owner, [state[0] for state in states])
+    soap = [value[None] for value in soap]
     norm_new = adam_small(small, norm_params, norm_first, norm_second)
     bias_new = adam_small(grad_bias, head_bias, bias_first, bias_second)
     return (
         loss_sum,
         valid_count,
         soap[0],
-        soap[0].astype(jnp.bfloat16),
         soap[1],
         soap[2],
         soap[3],
         soap[4],
         soap[5],
         soap[6],
+        soap[7],
         norm_new[0],
         norm_new[1],
         norm_new[2],

time: 678 us -> 544 us (0.80)
  Pallas kernels: 295 us -> 441 us
  waiting for transfers between devices: 189 us -> 60.9 us
  matrix products: 75 us -> 0 us
  local copies, waits for them, and re-layouts: 68.2 us -> 21.2 us
  other arithmetic: 29.2 us -> 6.21 us
    pallas_call x1 -> x2, Pallas kernels: 44.1 us -> 178 us  [the longest x1 91.5 us: soap_update(): pl.pallas_call(functools.partial(collect_kernel, nr, size), out_shape=(sh...]
    reduce_scatter x1 -> x0, waiting for transfers between devices: 128 us -> none  [local(): lax.psum_scatter(blocks[owner].astype(f32), 'rows', scatter_dimension=0,...]
    dot_general x12 -> x0, matrix products: 75 us -> none  [the longest x2 19.3 us: orthonormal(): jnp.matmul(product, jnp.swapaxes(inverse, -1, -2), precision=highest)[None]]
    slice x3 -> x0, local copies, waits for them, and re-layouts: 26.6 us -> none  [the longest x2 19.8 us: orthonormal(): inverses[count:]]
    gather x1 -> x0, local copies, waits for them, and re-layouts: 14.9 us -> none  [local(): blocks[owner].astype(f32)]
    convert_element_type x2 -> x0, other arithmetic: 13.7 us -> none  [the longest x1 13.7 us: local(): blocks[owner].astype(f32)]
    dot_general x2 -> x0, local copies, waits for them, and re-layouts: 13.1 us -> none  [orthonormal(): jnp.matmul(jnp.swapaxes(product, -1, -2), product, precision=highest)]
    pallas_call x1, Pallas kernels: 250 us -> 262 us  [run_step(): pl.pallas_call(functools.partial(step_kernel, nr, nb, cols), out_shape=(j...]
  transfers between devices with their start and end apart: 2 -> 1, of which waited for: 2 -> 1; matrix products, arithmetic and copies ran while one was open for 2% -> 1% of each run, Pallas kernels for 0% -> 0%
where the time goes in v3:
time: 544 us
  Pallas kernels  441 us (81%)
  waiting for transfers between devices  60.9 us (11%)
  local copies, waits for them, and re-layouts  21.2 us (4%)
  between operations  14.5 us (3%)
  other arithmetic  6.21 us (1%)
    pallas_call x1, Pallas kernels, run_step(): pl.pallas_call(functools.partial(step_kernel, nr, nb, cols), out_shape=(j...  262 us
    pallas_call x1, Pallas kernels, soap_update(): pl.pallas_call(functools.partial(collect_kernel, nr, size), out_shape=(sh...  91.5 us
    pallas_call x1, Pallas kernels, soap_update(): pl.pallas_call(basis_kernel, out_shape=(jax.ShapeDtypeStruct(flat[0].shap...  87 us
    all_gather x1, waiting for transfers between devices, local(): copies = lax.all_gather(master.astype(bf16), 'rows', axis=1, tiled=True)[0]  60.9 us
    unnamed x48, local copies, waits for them, and re-layouts  14.6 us
  transfers between devices with their start and end apart: 1, of which 1 were waited for; matrix products, arithmetic and copies ran while one was open for 1% of the time, Pallas kernels for 0%

profile of v3, /device:TPU:1, one launch (start us, length us, event | category | flops | bytes accessed | tf_op | source)
XLA Modules:
  0.0 543.7 jit_solution(13685888322998791873)
XLA Ops:
  7.3 3.0 bitcast_convert_fusion
  10.8 0.8 copy.64
  12.6 0.6 pad.15.lab_ref
  14.6 0.7 select_reduce_fusion.place_ref
  15.4 60.9 %all-gather.2.cloned.1.call-done = bf16[1,320,128,128]{3,2,0,1:T(8,128)(2,1)} async-done(((bf16[1,40,128,128]{3,2,0,1:T(8,128)(2,1)}), bf16[1,320,128,128]{3,2,0,1:T(8,128)(2,1)}) %all-gather.2.cloned.1.call-update) | async-done | bytes 10485776 | tf_op jit(solution)/shard_map/all_gather | solution.py:1354
  76.3 262.3 %shard_map.306 = (bf16[320,128,128]{2,1,0:T(8,128)(2,1)}, f32[4,16,256]{2,1,0:T(8,128)}) custom-call(bf16[320,128,128]{2,1,0:T(8,128)(2,1)} %bitcast.52, s32[320]{0:T(512)} %select_reduce_fusion.place_ref, f32[2]{0:T(128)} %bias_ref.1, bf16[96,512]{1,0:T(8,128)(2,1)} %bitcast.71, bf16[2,2,96,512]{3,2,1,0:T(8,128)(2,1)} %bitcast.68, ...), custom_call_target="tpu_custom_call" | custom-call | tf_op jit(solution)/shard_map/pallas_call | solution.py:915
  338.6 1.2 fusion.5
  339.8 1.0 fusion.4
  340.8 0.8 slice_bitcast_fusion.1
  341.6 0.8 slice_reduce_fusion
  342.5 91.5 %shard_map.307 = (f32[40,128,128]{2,1,0:T(8,128)}, bf16[40,128,128]{2,1,0:T(8,128)(2,1)}, f32[40,128,128]{2,1,0:T(8,128)}, f32[40,128,128]{2,1,0:T(8,128)}, f32[...) custom-call(s32[320]{0:T(512)} %refs_0_.1, ...), custom_call_target="tpu_custom_call" | custom-call | tf_op jit(solution)/shard_map/pallas_call | solution.py:1271
  434.4 0.6 multiply_subtract_fusion
  435.6 87.0 %shard_map.308 = (f32[5120,128]{1,0:T(8,128)}, f32[5120,128]{1,0:T(8,128)}) custom-call(f32[5120,128]{1,0:T(8,128)} %bitcast.61, f32[5120,128]{1,0:T(8,128)} %bitcast.62, f32[5120,128]{1,0:T(8,128)} %bitcast.59, f32[5120,128]{1,0:T(8,128)} %bitcast.60), custom_call_target="tpu_custom_call" | custom-call | tf_op jit(solution)/shard_map/pallas_call | solution.py:1299
  522.6 1.5 copy.77
  524.1 0.8 copy-done.5
  524.8 1.1 copy.78
  525.9 1.2 copy-done.3
  527.0 1.5 copy.79
  528.5 1.2 copy-done.2
  529.7 1.5 copy.80
  531.2 1.2 copy-done.1
  532.4 1.5 copy.81
  533.9 1.2 copy-done
  535.1 1.5 copy.82
  (64 shorter events, 3.8 us)
Async XLA Ops:
  7.2 3.2 copy-start.6
  7.2 4.4 copy-start.11
  7.2 4.6 copy-start.14
  7.2 69.1 %all-gather.2.cloned.1.call-start = ((), (), s32[]{:S(2)}) async-start(), calls=%async_computation | async-start | bytes 11796480 | tf_op jit(solution)/shard_map/all_gather | solution.py:1354
  10.3 1.7 copy-start.13
  10.3 2.0 slice-start
  10.3 2.9 copy-start.7
  10.3 4.3 copy-start.10
  342.4 91.9 %copy-start.8 = (f32[6144]{0:T(1024)S(1)}, f32[6144]{0:T(1024)}, u32[]{:S(2)}) copy-start(f32[6144]{0:T(1024)} %param.34) | copy-start | bytes 73732
  342.4 91.9 %copy-start.9 = (f32[6144]{0:T(1024)S(1)}, f32[6144]{0:T(1024)}, u32[]{:S(2)}) copy-start(f32[6144]{0:T(1024)} %param.33) | copy-start | bytes 73732
  342.4 92.6 %copy-start.12 = (f32[2]{0:T(128)S(1)}, f32[2]{0:T(128)}, u32[]{:S(2)}) copy-start(f32[2]{0:T(128)} %bias_ref.1) | copy-start | bytes 28
  342.5 92.6 %copy-start.15 = (f32[2]{0:T(128)S(1)}, f32[2]{0:T(128)}, u32[]{:S(2)}) copy-start(f32[2]{0:T(128)} %param.37) | copy-start | bytes 28
  342.5 92.6 %copy-start.16 = (f32[2]{0:T(128)S(1)}, f32[2]{0:T(128)}, u32[]{:S(2)}) copy-start(f32[2]{0:T(128)} %param.36) | copy-start | bytes 28
  435.6 87.0 %copy-start.4 = (f32[40,128,128]{2,1,0:T(8,128)S(1)}, f32[40,128,128]{2,1,0:T(8,128)}, u32[]{:S(2)}) copy-start(f32[40,128,128]{2,1,0:T(8,128)} %get-tuple-element.32) | copy-start | bytes 7864324
  522.6 2.3 copy-start.5
  524.8 2.2 copy-start.3
  527.0 2.7 copy-start.2
  529.7 2.7 copy-start.1
  532.4 2.7 copy-start
Sparse Core Ops, SparseCore 0:
  10.5 65.7 all-gather.1

commit v4 on v3

--- a/solution.py
+++ b/solution.py
@@ -57,7 +57,7 @@
     nr,
     nb,
     cols,
-    copies_ref,
+    master_ref,
     place_ref,
     bias_ref,
     image_ref,
@@ -99,7 +99,8 @@
     logit,
     reduce_wide,
     reduce_narrow,
-    local_sem,
+    gather_send,
+    gather_recv,
     line_send,
     line_recv,
     halo_send,
@@ -271,7 +272,7 @@
                     self.lower(j).wait_send()
                     self.higher(j).wait_recv()
 
-    def all_reduce(number, buffer):
+    def reduce_start(number, buffer):
         def start(step, _):
             remote(
                 buffer.at[r],
@@ -283,6 +284,9 @@
             ).start()
             return 0
 
+        lax.fori_loop(1, nr, start, 0)
+
+    def reduce_finish(number, buffer):
         def wait(step, _):
             source = ring(r + step, nr)
             copy = remote(
@@ -297,9 +301,12 @@
             copy.wait_send()
             return 0
 
-        lax.fori_loop(1, nr, start, 0)
         lax.fori_loop(1, nr, wait, 0)
         return lax.fori_loop(1, nr, lambda k, total: total + buffer[k], buffer[0])
+
+    def all_reduce(number, buffer):
+        reduce_start(number, buffer)
+        return reduce_finish(number, buffer)
 
     class Spread:
         def __init__(self, send, recv, source, target):
@@ -332,6 +339,124 @@
                     other,
                 ).wait_recv()
                 self.copy(step).wait_send()
+
+    class Gather:
+        def __init__(self):
+            self.size = master_ref.shape[0]
+            self.chips = nr // 2
+            self.core = lax.rem(r, 2)
+            self.chip = lax.div(r, 2)
+            self.mate = r + 1 - 2 * self.core
+            self.square = self.chips == 4 and self.size % 2 == 0
+            self.halves = 2 if self.square else 1
+
+        def piece(self, row, half):
+            part = self.size // self.halves
+            return grad_ref.at[pl.ds(row * self.size + half * part, part)]
+
+        def move(self, kind, target, row, half):
+            return remote(
+                self.piece(row, half),
+                self.piece(row, half),
+                gather_send.at[kind, row, half],
+                gather_recv.at[row, half],
+                target,
+                b,
+            )
+
+        def direct(self, target):
+            return remote(
+                self.piece(r, 0),
+                self.piece(r, 0),
+                gather_send.at[0, target, 0],
+                gather_recv.at[r, 0],
+                target,
+                b,
+            )
+
+        def beside(self, step):
+            return 2 * lax.rem(self.chip + step, self.chips) + self.core
+
+        def other(self, bit):
+            away = self.chip + bit - 2 * bit * lax.rem(lax.div(self.chip, bit), 2)
+            return 2 * away + self.core
+
+        def begin(self):
+            def cast(index, _):
+                grad_ref[r * self.size + index] = master_ref[index].astype(bf16)
+                return 0
+
+            lax.fori_loop(0, self.size, cast, 0)
+            if self.square:
+                for half in range(2):
+                    self.move(2, self.mate, r, half).start()
+                    self.move(0, self.other(1), r, 1 - half).start()
+                    self.move(1, self.other(2), r, half).start()
+            else:
+                self.move(2, self.mate, r, 0).start()
+
+                def send(step, _):
+                    self.direct(self.beside(step)).start()
+                    return 0
+
+                lax.fori_loop(1, self.chips, send, 0)
+
+        def arrived(self, row, half):
+            self.move(2, self.mate, row, half).wait_recv()
+
+        def hand(self, row, half):
+            self.arrived(row, half)
+            self.move(2, self.mate, row, half).start()
+
+        def forward(self, moves):
+            image, lab, skip = moves
+            for k in range(1, nb):
+                image.hop(k)
+                lab.hop(k)
+            if self.square:
+                x, y = self.other(1), self.other(2)
+                corner = 2 * (3 - self.chip) + self.core
+                self.hand(y, 0)
+                self.move(0, x, y, 0).start()
+                self.hand(x, 1)
+                self.move(1, y, x, 1).start()
+                skip.hop(1)
+                self.hand(x, 0)
+                self.hand(y, 1)
+                for k in range(2, nb):
+                    skip.hop(k)
+                self.hand(corner, 0)
+                self.hand(corner, 1)
+                rows = (r, x, y, corner)
+                for half in range(2):
+                    for row in rows:
+                        self.arrived(row + 1 - 2 * self.core, half)
+                for half in range(2):
+                    for row in rows:
+                        self.move(2, self.mate, row, half).wait_send()
+                    self.move(0, x, r, half).wait_send()
+                    self.move(1, y, r, half).wait_send()
+                self.move(0, x, y, 0).wait_send()
+                self.move(1, y, x, 1).wait_send()
+            else:
+
+                def pass_on(step, _):
+                    self.hand(self.beside(step), 0)
+                    return 0
+
+                def close(step, _):
+                    row = self.beside(step)
+                    self.arrived(row + 1 - 2 * self.core, 0)
+                    self.move(2, self.mate, row, 0).wait_send()
+                    self.direct(row).wait_send()
+                    return 0
+
+                lax.fori_loop(1, self.chips, pass_on, 0)
+                for k in range(1, nb):
+                    skip.hop(k)
+                self.arrived(self.mate, 0)
+                self.move(2, self.mate, r, 0).wait_send()
+                lax.fori_loop(1, self.chips, close, 0)
 
     position = lax.rem(lax.broadcasted_iota(jnp.int32, (px, TILE), 0), cols)
 
@@ -412,6 +537,8 @@
         gain_grad = jnp.sum(total[nb : 2 * nb], 0, keepdims=True)
         return gain_grad, shift_grad
 
+    gather = Gather()
+    gather.begin()
     x_one[1, b] = image_ref[...]
     x_skip[1:3, :, b] = skip_ref[...]
     x_lab[b] = lab_ref[...]
@@ -431,9 +558,6 @@
     moves = (move_image, move_lab, move_skip)
     for move in moves:
         move.begin()
-    stage = pltpu.make_async_copy(copies_ref, grad_ref, local_sem)
-    stage.start()
-
     @pl.when(r == 0)
     def _():
         x_one[0] = jnp.zeros_like(x_one[0])
@@ -452,11 +576,15 @@
         dz_low[2] = jnp.zeros_like(dz_low[2])
         dz_high[3] = jnp.zeros_like(dz_high[3])
 
-    stage.wait()
-    for target, (out, width, taps, first) in zip((w_one, w_two, w_up, w_three), layers):
+    gather.forward(moves)
+    for move in moves:
+        move.finish()
+
+    def arrange(number, target):
+        out, width, taps, first = layers[number]
         across = width // TILE
 
-        def arrange(n, _, target=target, out=out, taps=taps, first=first, across=across):
+        def body(n, _):
             ib = lax.rem(n, across)
             t = lax.rem(lax.div(n, across), taps)
             ob = lax.div(n, across * taps)
@@ -465,27 +593,26 @@
             ] = grad_ref[place_ref[first + n]]
             return 0
 
-        lax.fori_loop(0, out // TILE * taps * across, arrange, 0)
-    for k in range(1, nb):
-        for move in moves:
-            move.hop(k)
-    for move in moves:
-        move.finish()
-
+        lax.fori_loop(0, out // TILE * taps * across, body, 0)
+
+    arrange(0, w_one)
     gain_one, shift_one = wide_ref[0:1, :], wide_ref[1:2, :]
     gain_two, shift_two = wide_ref[2:3, :], wide_ref[3:4, :]
     gain_three, shift_three = narrow_ref[0:1, :], narrow_ref[1:2, :]
     size_low, size_high = C1 // GROUPS, C0 // GROUPS
 
-    def conv_low(z_ref, weight, source):
+    def conv_low(z_ref, weight, source, lines=(0, 1, 2), more=False):
         def tap(dx):
             total = 0.0
-            for dy in range(3):
+            for dy in lines:
                 first = (3 * dy + dx) * wide
                 total = total + dot_nt(source(dy), weight[first : first + wide, :])
             return total
 
-        z_ref[0] = tap(1)
+        if more:
+            z_ref[0] += tap(1)
+        else:
+            z_ref[0] = tap(1)
         z_ref[0] += shift_down(tap(0))
         z_ref[0] += shift_up(tap(2))
 
@@ -497,7 +624,9 @@
         for part in range(4):
             count = count + jnp.sum(x_lab[image, part, 2:3, :], 1, keepdims=True)
     reduce_one[r, 2 * nb : 2 * nb + 1, :] = jnp.broadcast_to(count, (1, wide))
-    total = all_reduce(0, reduce_one)
+    reduce_start(0, reduce_one)
+    arrange(1, w_two)
+    total = reduce_finish(0, reduce_one)
     count = total[2 * nb : 2 * nb + 1, :1]
 
     def put_one(part, image, value):
@@ -511,9 +640,14 @@
         lambda j: (a_one.at[1, :, lanes(j, wide)], a_one.at[2, :, lanes(j, wide)]),
     )
     move.begin()
-    move.hops()
+    move.hop(1)
+    arrange(2, w_up)
+    for k in range(2, nb):
+        move.hop(k)
+    arrange(3, w_three)
+    conv_low(z_two, w_two, lambda dy: a_one[dy], (1,))
     move.finish()
-    conv_low(z_two, w_two, lambda dy: a_one[dy])
+    conv_low(z_two, w_two, lambda dy: a_one[dy], (0, 2), True)
     norm_sums(reduce_two, z_two)
     total = all_reduce(1, reduce_two)
 
@@ -535,25 +669,36 @@
         lambda j: (u_full.at[2, :, :, lanes(j, slim)], u_full.at[0, :, :, lanes(j, slim)]),
         lambda j: (u_full.at[1, :, :, lanes(j, slim)], u_full.at[3, :, :, lanes(j, slim)]),
     )
+    def conv_high(product, more):
+        for e in range(2):
+            even, odd = product(e, 0), product(e, 1)
+            first = even[:, slim : 2 * slim] + shift_down(odd[:, :slim]) + odd[:, 2 * slim :]
+            second = odd[:, slim : 2 * slim] + even[:, :slim] + shift_up(even[:, 2 * slim :])
+            if more:
+                z_three[2 * e] += first
+                z_three[2 * e + 1] += second
+            else:
+                z_three[2 * e] = first
+                z_three[2 * e + 1] = second
+
+    def high_product(source, start, lines):
+        def product(e, f):
+            total = 0.0
+            for dy in lines[e]:
+                weight = w_three[dy * taps_high : (dy + 1) * taps_high, start : start + C0]
+                total = total + dot_nt(source[e + dy, f].reshape(px, C0), weight)
+            return total
+
+        return product
+
+    every = ((0, 1, 2), (0, 1, 2))
+    inner, outer = ((1, 2), (0, 1)), ((0,), (2,))
     move.begin()
+    conv_high(high_product(x_skip, C0, every), False)
     move.hops()
+    conv_high(high_product(u_full, 0, inner), True)
     move.finish()
-    for e in range(2):
-        found = []
-        for f in range(2):
-            total = 0.0
-            for dy in range(3):
-                weight = w_three[dy * taps_high : (dy + 1) * taps_high, :]
-                total = total + dot_nt(u_full[e + dy, f], weight[:, :C0])
-                total = total + dot_nt(x_skip[e + dy, f].reshape(px, C0), weight[:, C0:])
-            found.append(total)
-        even, odd = found
-        z_three[2 * e] = (
-            even[:, slim : 2 * slim] + shift_down(odd[:, :slim]) + odd[:, 2 * slim :]
-        )
-        z_three[2 * e + 1] = (
-            odd[:, slim : 2 * slim] + even[:, :slim] + shift_up(even[:, 2 * slim :])
-        )
+    conv_high(high_product(u_full, 0, outer), True)
     reduce_three, reduce_four = reduce_narrow.at[0], reduce_narrow.at[1]
     norm_sums(reduce_three, z_three)
     total = all_reduce(2, reduce_three)
@@ -857,7 +1002,7 @@
     spread.finish()
 
 
-def run_step(copies, place, bias, image, skip, lab, wide_rows, narrow_rows):
+def run_step(master, place, bias, image, skip, lab, wide_rows, narrow_rows):
     nr, nb = lax.axis_size("rows"), lax.axis_size("blk")
     cols = image.shape[0]
     px = nb * cols
@@ -898,7 +1043,8 @@
         pltpu.VMEM((nb, 4 * nb, 8, cols), f32),
         pltpu.VMEM((4, nr, 2 * nb + 8, wide), f32),
         pltpu.VMEM((2, nr, 2 * nb + 8, slim), f32),
-        dma(()),
+        dma((3, nr, 2)),
+        dma((nr, 2)),
         dma((6, nb, 2)),
         dma((6, nb)),
         dma((6, nb, 2)),
@@ -915,124 +1061,107 @@
     return pl.pallas_call(
         functools.partial(step_kernel, nr, nb, cols),
         out_shape=(
-            jax.ShapeDtypeStruct(copies.shape, bf16),
+            jax.ShapeDtypeStruct((place.shape[0],) + master.shape[1:], bf16),
             jax.ShapeDtypeStruct((nb, 16, wide), f32),
         ),
-        in_specs=[pl.BlockSpec(memory_space=pl.ANY), smem, smem, vmem, vmem, vmem, vmem, vmem],
+        in_specs=[vmem, smem, smem, vmem, vmem, vmem, vmem, vmem],
         out_specs=(vmem, vmem),
         scratch_shapes=scratch,
         compiler_params=pltpu.CompilerParams(
             collective_id=0, has_side_effects=True, vmem_limit_bytes=60 * 2**20
         ),
-    )(copies, place, bias, image, skip, lab, wide_rows, narrow_rows)
-
-
-LANES = 128
-
-
-def inverse_factor_kernel(stat_ref, inverse_ref, factor_ref):
-    order = stat_ref.shape[0]
-    tile = (8, LANES)
-    sub = lax.broadcasted_iota(jnp.int32, tile, 0)
-
-    def eliminate(source_ref, base, start, first, count, accs):
-        def body(group, accs):
-            top = pl.multiple_of(group * 8, 8)
-            for unit in range(8):
-                value = source_ref[top + unit, pl.ds(start, 8), :]
-                accs = tuple(
-                    accs[c]
-                    - value
-                    * jnp.broadcast_to(factor_ref[top + unit, pl.ds(base + c, 1), :], tile)
-                    for c in range(8)
-                )
-            return accs
-
-        return list(lax.fori_loop(first, count, body, tuple(accs)))
-
-    def block(kb, _):
-        base = pl.multiple_of(kb * 8, 8)
-        accs = [stat_ref[base + c, pl.ds(base, 8), :] for c in range(8)]
-        accs = eliminate(factor_ref, base, base, 0, kb, accs)
-        scale = []
-        coef = {}
-        for c in range(8):
-            scale.append(jnp.broadcast_to(lax.rsqrt(accs[c][c : c + 1, :]), tile))
-            accs[c] = accs[c] * scale[c]
-            for d in range(c + 1, 8):
-                coef[(c, d)] = jnp.broadcast_to(accs[c][d : d + 1, :], tile)
-                accs[d] = accs[d] - accs[c] * coef[(c, d)]
-        for c in range(8):
-            factor_ref[base + c, pl.ds(base, 8), :] = jnp.where(sub >= c, accs[c], 0.0)
-
-        def finish(accs, target_ref, start):
-            accs = list(accs)
-            for c in range(8):
-                for e in range(c):
-                    accs[c] = accs[c] - accs[e] * coef[(e, c)]
-                accs[c] = accs[c] * scale[c]
-                target_ref[base + c, pl.ds(start, 8), :] = accs[c]
-
-        def below(group, _):
-            start = pl.multiple_of(group * 8, 8)
-            accs = [stat_ref[base + c, pl.ds(start, 8), :] for c in range(8)]
-            finish(eliminate(factor_ref, base, start, 0, kb, accs), factor_ref, start)
-            return 0
-
-        def left(group, _):
-            start = pl.multiple_of(group * 8, 8)
-            accs = [jnp.zeros(tile, jnp.float32) for c in range(8)]
-            finish(eliminate(inverse_ref, base, start, group, kb, accs), inverse_ref, start)
-            return 0
-
-        def clear(group, _):
-            start = pl.multiple_of(group * 8, 8)
-            for c in range(8):
-                inverse_ref[base + c, pl.ds(start, 8), :] = jnp.zeros(tile, jnp.float32)
-            return 0
-
-        lax.fori_loop(kb + 1, order // 8, below, 0)
-        lax.fori_loop(0, kb, left, 0)
-        finish([jnp.where(sub == c, 1.0, 0.0) for c in range(8)], inverse_ref, base)
-        lax.fori_loop(kb + 1, order // 8, clear, 0)
-        return 0
-
-    lax.fori_loop(0, order // 8, block, 0)
-
-
-def product(left, right, left_dim, right_dim):
+    )(master, place, bias, image, skip, lab, wide_rows, narrow_rows)
+
+
+def split(value):
+    high = value.astype(bf16)
+    return high, (value - high.astype(f32)).astype(bf16)
+
+
+def product_three(left, right, right_dim):
+    (a, b), (c, d) = left, right
     return lax.dot_general(
-        left,
-        right,
-        (((left_dim,), (right_dim,)), ((), ())),
+        jnp.concatenate([a, a, b], 1),
+        jnp.concatenate([c, d, c], right_dim),
+        (((1,), (right_dim,)), ((), ())),
         preferred_element_type=f32,
-        precision=highest,
-    )
-
-
-def soap_block(index, grad, ins, outs):
+    )
+
+
+def square_six(value):
+    high = value.astype(bf16)
+    rest = value - high.astype(f32)
+    middle = rest.astype(bf16)
+    low = (rest - middle.astype(f32)).astype(bf16)
+    return lax.dot_general(
+        jnp.concatenate([high, high, middle, high, middle, low], 1),
+        jnp.concatenate([high, middle, high, low, middle, high], 1),
+        (((1,), (1,)), ((), ())),
+        preferred_element_type=f32,
+    )
+
+
+def soap_blocks(indices, grads, ins, outs):
+    def every(function, *lists):
+        return [function(*items) for items in zip(*lists)]
+
+    def load(ref):
+        return [ref[index] for index in indices]
+
+    def store(ref, values):
+        for index, value in zip(indices, values):
+            ref[index] = value
+
     master_ref, first_ref, second_ref, left_ref, right_ref, left_stat_ref, right_stat_ref = ins
-    left, right = left_ref[index], right_ref[index]
-    rotated = product(product(left, grad, 0, 0), right, 1, 0)
-    first = beta_one * first_ref[index] + (1.0 - beta_one) * rotated
-    second = beta_two * second_ref[index] + (1.0 - beta_two) * rotated * rotated
-    direction = (
-        first
-        / (1.0 - beta_one**STEP)
-        / (jnp.sqrt(second / (1.0 - beta_two**STEP)) + adam_eps)
-    )
-    update = product(product(left, direction, 1, 0), right, 1, 1)
-    master = master_ref[index]
-    master = master - soap_rate * (update + soap_decay * master)
-    values = [master, master.astype(bf16), first, second]
-    moved = []
-    for stat_ref, basis, dim in ((left_stat_ref, left, 1), (right_stat_ref, right, 0)):
-        stat = beta_stat * stat_ref[index] + (1.0 - beta_stat) * product(grad, grad, dim, dim)
-        values.append(stat)
-        moved.append(product(stat, basis, 1, 0))
-    values = values + moved + [product(value, value, 0, 0) for value in moved]
-    for ref, value in zip(outs, values):
-        ref[index] = value
+    left = load(left_ref)
+    sides, bases = every(split, grads), every(split, load(right_ref))
+    lefts, turned = every(split, left), every(lambda grad: split(grad.T), grads)
+
+    def three(dim):
+        return lambda one, two: product_three(one, two, dim)
+
+    half = every(three(0), every(lambda value: split(value.T), left), sides)
+    left_outer = every(three(1), sides, sides)
+    rotated = every(three(0), every(split, half), bases)
+    right_outer = every(three(1), turned, turned)
+    first = every(
+        lambda old, new: beta_one * old + (1.0 - beta_one) * new, load(first_ref), rotated
+    )
+    second = every(
+        lambda old, new: beta_two * old + (1.0 - beta_two) * new * new, load(second_ref), rotated
+    )
+    store(outs[2], first)
+    store(outs[3], second)
+    direction = every(
+        lambda one, two: one
+        * (1.0 / (1.0 - beta_one**STEP))
+        / (jnp.sqrt(two * (1.0 / (1.0 - beta_two**STEP))) + adam_eps),
+        first,
+        second,
+    )
+    half = every(three(0), lefts, every(split, direction))
+    stats = []
+    for ref, target, outer in (
+        (left_stat_ref, outs[4], left_outer),
+        (right_stat_ref, outs[5], right_outer),
+    ):
+        stat = every(
+            lambda old, new: beta_stat * old + (1.0 - beta_stat) * new, load(ref), outer
+        )
+        store(target, stat)
+        stats.append(every(split, stat))
+    moved = every(three(0), stats[0], lefts)
+    update = every(three(1), every(split, half), bases)
+    moved_right = every(three(0), stats[1], bases)
+    master = every(
+        lambda old, new: old - soap_rate * (new + soap_decay * old), load(master_ref), update
+    )
+    store(outs[0], master)
+    store(outs[1], every(lambda value: value.astype(bf16), master))
+    store(outs[6], moved)
+    store(outs[7], moved_right)
+    store(outs[8], every(lambda value: square_six(value.T), moved))
+    store(outs[9], every(lambda value: square_six(value.T), moved_right))
 
 
 def collect_kernel(nr, size, *refs):
@@ -1196,18 +1325,18 @@
         chunk_outs = [out_buffer.at[slot, number] for number in range(9)]
         chunk_outs.insert(1, copy_buffer.at[slot])
 
-        def work(index, _, chunk=chunk, chunk_ins=chunk_ins, chunk_outs=chunk_outs):
-            grad = lax.fori_loop(
-                1,
-                chips,
-                lambda step, value: value
-                + in_b[chunk, lax.rem(chip + step, chips), index].astype(f32),
-                total[chunk, index],
-            )
-            soap_block(index, grad, chunk_ins, chunk_outs)
-            return 0
-
-        lax.fori_loop(0, size, work, 0, unroll=2 if size % 2 == 0 else 1)
+        grads = []
+        for index in range(size):
+            grads.append(
+                lax.fori_loop(
+                    1,
+                    chips,
+                    lambda step, value, chunk=chunk, index=index: value
+                    + in_b[chunk, lax.rem(chip + step, chips), index].astype(f32),
+                    total[chunk, index],
+                )
+            )
+        soap_blocks(range(size), grads, chunk_ins, chunk_outs)
         for copy in stores(chunk):
             copy.start()
     for chunk in range(chunks):
@@ -1218,44 +1347,6 @@
         if chunk >= chunks - 2:
             for copy in stores(chunk):
                 copy.wait()
-
-
-def basis_kernel(
-    left_gram_ref, right_gram_ref, left_ref, right_ref, new_left_ref, new_right_ref, stat_ref,
-    inverse_ref, factor_ref
-):
-    order = left_gram_ref.shape[1]
-    count = left_gram_ref.shape[0] // order
-    spare = LANES - 2 * count
-
-    def enter(row, _):
-        rows = pl.ds(row, count, stride=order)
-        values = [left_gram_ref[rows, :], right_gram_ref[rows, :]]
-        if spare:
-            column = lax.broadcasted_iota(jnp.int32, (spare, order), 1)
-            values.append(jnp.where(column == row, 1.0, 0.0))
-        stat_ref[row] = jnp.concatenate(values, 0).T
-        return 0
-
-    lax.fori_loop(0, order, enter, 0)
-    inverse_factor_kernel(stat_ref, inverse_ref, factor_ref)
-
-    def leave(row, _):
-        rows = pl.ds(row, count, stride=order)
-        value = inverse_ref[row].T
-        new_left_ref[rows, :] = value[:count]
-        new_right_ref[rows, :] = value[count : 2 * count]
-        return 0
-
-    lax.fori_loop(0, order, leave, 0)
-
-    def solve(index, _):
-        rows = pl.ds(pl.multiple_of(index * order, order), order)
-        new_left_ref[rows, :] = product(left_ref[rows, :], new_left_ref[rows, :], 1, 1)
-        new_right_ref[rows, :] = product(right_ref[rows, :], new_right_ref[rows, :], 1, 1)
-        return 0
-
-    lax.fori_loop(0, count, solve, 0, unroll=2 if count % 2 == 0 else 1)
 
 
 def soap_update(blocks, owner, states):
@@ -1293,27 +1384,187 @@
             collective_id=1, has_side_effects=True, vmem_limit_bytes=60 * 2**20
         ),
     )(owner, blocks, *states)
-    new_master, new_copy, new_first, new_second, new_left_stat, new_right_stat = results[:6]
-    lanes = pltpu.VMEM((order, order, LANES), f32)
-    flat = [value.reshape(count * order, order) for value in results[8:] + results[6:8]]
-    new_left, new_right = pl.pallas_call(
-        basis_kernel,
-        out_shape=(jax.ShapeDtypeStruct(flat[0].shape, f32),) * 2,
-        in_specs=[vmem] * 4,
-        out_specs=(vmem, vmem),
-        scratch_shapes=[lanes, lanes, lanes],
-        compiler_params=pltpu.CompilerParams(vmem_limit_bytes=60 * 2**20),
-    )(*flat)
+    kept = list(results[:6])
+    new_left, new_right, *kept = new_bases(results[6:8], results[8:], kept)
+    new_master, new_copy, new_first, new_second, new_left_stat, new_right_stat = kept
     return [
         new_master,
         new_copy,
         new_first,
         new_second,
-        new_left.reshape(shape.shape),
-        new_right.reshape(shape.shape),
+        new_left,
+        new_right,
         new_left_stat,
         new_right_stat,
     ]
+
+
+LANES = 128
+
+
+def inverse_factor_kernel(stat_ref, inverse_ref, factor_ref):
+    order = stat_ref.shape[0]
+    tile = (8, LANES)
+    sub = lax.broadcasted_iota(jnp.int32, tile, 0)
+    groups = order // 8
+
+    def eliminate(source_ref, base, starts, first, count, accs):
+        width = len(starts)
+
+        def body(group, accs):
+            top = pl.multiple_of(group * 8, 8)
+            accs = [list(acc) for acc in accs]
+            for unit in range(8):
+                values = [source_ref[top + unit, pl.ds(start, 8), :] for start in starts]
+                for c in range(8):
+                    scale = jnp.broadcast_to(
+                        factor_ref[top + unit, pl.ds(base + c, 1), :], tile
+                    )
+                    for s in range(width):
+                        accs[s][c] = accs[s][c] - values[s] * scale
+            return tuple(tuple(acc) for acc in accs)
+
+        return lax.fori_loop(first, count, body, tuple(tuple(acc) for acc in accs))
+
+    def batches(first, last, run):
+        total = last - first
+
+        def at(group):
+            return pl.multiple_of(group * 8, 8)
+
+        def two(n, _):
+            run(first + 2 * n, [at(first + 2 * n), at(first + 2 * n + 1)])
+            return 0
+
+        lax.fori_loop(0, lax.div(total, 2), two, 0)
+
+        @pl.when(lax.rem(total, 2) == 1)
+        def _():
+            run(last - 1, [at(last - 1)])
+
+    def block(kb, _):
+        base = pl.multiple_of(kb * 8, 8)
+        accs = [stat_ref[base + c, pl.ds(base, 8), :] for c in range(8)]
+        accs = list(eliminate(factor_ref, base, [base], 0, kb, [accs])[0])
+        scale = []
+        coef = {}
+        for c in range(8):
+            scale.append(jnp.broadcast_to(lax.rsqrt(accs[c][c : c + 1, :]), tile))
+            accs[c] = accs[c] * scale[c]
+            for d in range(c + 1, 8):
+                coef[(c, d)] = jnp.broadcast_to(accs[c][d : d + 1, :], tile)
+                accs[d] = accs[d] - accs[c] * coef[(c, d)]
+        for c in range(8):
+            factor_ref[base + c, pl.ds(base, 8), :] = jnp.where(sub >= c, accs[c], 0.0)
+
+        def finish(accs, target_ref, start):
+            accs = list(accs)
+            for c in range(8):
+                for e in range(c):
+                    accs[c] = accs[c] - accs[e] * coef[(e, c)]
+                accs[c] = accs[c] * scale[c]
+                target_ref[base + c, pl.ds(start, 8), :] = accs[c]
+
+        def below(group, starts):
+            accs = [[stat_ref[base + c, pl.ds(s, 8), :] for c in range(8)] for s in starts]
+            accs = eliminate(factor_ref, base, starts, 0, kb, accs)
+            for acc, start in zip(accs, starts):
+                finish(acc, factor_ref, start)
+
+        def left(group, starts):
+            accs = [[jnp.zeros(tile, jnp.float32) for c in range(8)] for s in starts]
+            accs = eliminate(inverse_ref, base, starts, group, kb, accs)
+            for acc, start in zip(accs, starts):
+                finish(acc, inverse_ref, start)
+
+        def clear(group, _):
+            start = pl.multiple_of(group * 8, 8)
+            for c in range(8):
+                inverse_ref[base + c, pl.ds(start, 8), :] = jnp.zeros(tile, jnp.float32)
+            return 0
+
+        batches(kb + 1, groups, below)
+        batches(0, kb, left)
+        finish([jnp.where(sub == c, 1.0, 0.0) for c in range(8)], inverse_ref, base)
+        lax.fori_loop(kb + 1, groups, clear, 0)
+        return 0
+
+    lax.fori_loop(0, groups, block, 0)
+
+
+def basis_kernel(left_gram_ref, right_gram_ref, left_ref, right_ref, *refs):
+    number = (len(refs) - 7) // 3
+    kept, new_left_ref, new_right_ref = refs[:number], refs[number], refs[number + 1]
+    moved, refs = refs[number + 2 : 2 * number + 2], refs[2 * number + 2 :]
+    stat_ref, inverse_ref, factor_ref, in_sem, out_sem, *halts = refs
+    arriving = [
+        pltpu.make_async_copy(source, halt, in_sem.at[n])
+        for n, (source, halt) in enumerate(zip(kept, halts))
+    ]
+    leaving = [
+        pltpu.make_async_copy(halt, target, out_sem.at[n])
+        for n, (halt, target) in enumerate(zip(halts, moved))
+    ]
+    for copy in arriving:
+        copy.start()
+    order = left_gram_ref.shape[1]
+    count = left_gram_ref.shape[0] // order
+    spare = LANES - 2 * count
+
+    def enter(row, _):
+        rows = pl.ds(row, count, stride=order)
+        values = [left_gram_ref[rows, :], right_gram_ref[rows, :]]
+        if spare:
+            column = lax.broadcasted_iota(jnp.int32, (spare, order), 1)
+            values.append(jnp.where(column == row, 1.0, 0.0))
+        stat_ref[row] = jnp.concatenate(values, 0).T
+        return 0
+
+    lax.fori_loop(0, order, enter, 0, unroll=8)
+    for come, go in zip(arriving, leaving):
+        come.wait()
+        go.start()
+    inverse_factor_kernel(stat_ref, inverse_ref, factor_ref)
+
+    def leave(row, _):
+        rows = pl.ds(row, count, stride=order)
+        value = inverse_ref[row].T
+        new_left_ref[rows, :] = value[:count]
+        new_right_ref[rows, :] = value[count : 2 * count]
+        return 0
+
+    lax.fori_loop(0, order, leave, 0, unroll=8)
+
+    def solve(index, _):
+        rows = pl.ds(pl.multiple_of(index * order, order), order)
+        for basis_ref, target_ref in ((left_ref, new_left_ref), (right_ref, new_right_ref)):
+            target_ref[rows, :] = product_three(
+                split(basis_ref[rows, :]), split(target_ref[rows, :]), 1
+            )
+        return 0
+
+    lax.fori_loop(0, count, solve, 0, unroll=8 if count % 8 == 0 else 1)
+    for copy in leaving:
+        copy.wait()
+
+
+def new_bases(products, grams, kept):
+    count, order = products[0].shape[0], products[0].shape[-1]
+    vmem = pl.BlockSpec(memory_space=pltpu.VMEM)
+    anywhere = pl.BlockSpec(memory_space=pl.ANY)
+    lanes = pltpu.VMEM((order, order, LANES), f32)
+    flat = [value.reshape(count * order, order) for value in list(grams) + list(products)]
+    results = pl.pallas_call(
+        basis_kernel,
+        out_shape=[jax.ShapeDtypeStruct(value.shape, value.dtype) for value in flat[:2] + kept],
+        in_specs=[vmem] * 4 + [anywhere] * len(kept),
+        out_specs=[vmem] * 2 + [anywhere] * len(kept),
+        scratch_shapes=[lanes, lanes, lanes]
+        + [pltpu.SemaphoreType.DMA((len(kept),))] * 2
+        + [pltpu.VMEM(value.shape, value.dtype) for value in kept],
+        compiler_params=pltpu.CompilerParams(vmem_limit_bytes=60 * 2**20),
+    )(*flat, *kept)
+    return [value.reshape(products[0].shape) for value in results[:2]] + list(results[2:])
 
 
 def adam_small(grads, value, first, second):
@@ -1351,7 +1602,6 @@
     shards = lax.axis_size("blk")
     shard = lax.axis_index("blk")
     cols = image.shape[2]
-    copies = lax.all_gather(master.astype(bf16), "rows", axis=1, tiled=True)[0]
     slots = jnp.arange(owner.shape[0])
     place = jnp.sum(jnp.where(owner[None, :] == slots[:, None], slots[None, :], 0), 1)
     widths = (C1, C1, C1, C1, C0, C0)
@@ -1375,7 +1625,7 @@
     lab = jnp.pad(lab, ((0, 0), (0, 5), (0, 0)))
     skip = skip.reshape(2, cols, 2, C0).transpose(0, 2, 1, 3)
     blocks, sums = run_step(
-        copies, place.astype(jnp.int32), head_bias, image[0, 0], skip, lab, wide_rows, narrow_rows
+        master[0], place.astype(jnp.int32), head_bias, image[0, 0], skip, lab, wide_rows, narrow_rows
     )
     loss_sum, valid_count = sums[0, 6, 0], sums[0, 9, 0]
     grad_bias = sums[0, 7:9, 0]

time: 544 us -> 432 us (0.79); the launches traced: 544 us -> 425 us
  waiting for transfers between devices: 60.9 us -> 0 us
  Pallas kernels: 441 us -> 408 us
  between operations: 14.5 us -> 1.07 us
  local copies, waits for them, and re-layouts: 21.2 us -> 9.51 us
    all_gather x1 -> x0, waiting for transfers between devices: 60.9 us -> none  [local(): copies = lax.all_gather(master.astype(bf16), 'rows', axis=1, tiled=True)[0]]
    pallas_call x1, Pallas kernels: 87 us -> 54.7 us  [new_bases(): pl.pallas_call(basis_kernel, out_shape=[jax.ShapeDtypeStruct(value.shape,...]
    pallas_call x1, Pallas kernels: 91.5 us -> 73.6 us  [soap_update(): pl.pallas_call(functools.partial(collect_kernel, nr, size), out_shape=(sh...]
    pallas_call x1, Pallas kernels: 262 us -> 280 us  [run_step(): pl.pallas_call(functools.partial(step_kernel, nr, nb, cols), out_shape=(j...]
    unnamed x48 -> x20, local copies, waits for them, and re-layouts: 14.6 us -> 1.52 us
  transfers between devices with their start and end apart: 1 -> 0, of which waited for: 1 -> 0; matrix products, arithmetic and copies ran while one was open for 1% -> 0% of each run, Pallas kernels for 0% -> 0%
where the time goes in v4:
time: 432 us; the launch traced here: 425 us
  Pallas kernels  408 us (94%)
  local copies, waits for them, and re-layouts  9.51 us (2%)
  other arithmetic  5.94 us (1%)
    pallas_call x1, Pallas kernels, run_step(): pl.pallas_call(functools.partial(step_kernel, nr, nb, cols), out_shape=(j...  280 us
    pallas_call x1, Pallas kernels, soap_update(): pl.pallas_call(functools.partial(collect_kernel, nr, size), out_shape=(sh...  73.6 us
    pallas_call x1, Pallas kernels, new_bases(): pl.pallas_call(basis_kernel, out_shape=[jax.ShapeDtypeStruct(value.shape,...  54.7 us

profile of v4, /device:TPU:1, one launch (start us, length us, event | category | flops | bytes accessed | tf_op | source)
XLA Modules:
  0.0 424.6 jit_solution(16891486160358017542)
XLA Ops:
  0.7 1.4 select_reduce_fusion.place_ref
  2.1 1.4 copy.52
  3.5 0.8 copy.62
  4.3 0.7 convert_element_type.16
  5.0 0.1 stack.41
  5.2 0.7 convert_element_type.18
  6.1 0.7 multiply_multiply_fusion.1
  7.1 0.6 pad.15.lab_ref
  7.7 0.8 fusion.6
  8.5 0.6 select_maximum_fusion.1.wide_ref
  9.1 0.7 slice.46
  9.8 0.2 slice.47
  10.2 0.6 select_maximum_fusion.narrow_ref
  10.8 279.7 %shard_map.306 = (bf16[320,128,128]{2,1,0:T(8,128)(2,1)}, f32[4,16,256]{2,1,0:T(8,128)}) custom-call(f32[40,128,128]{2,1,0:T(8,128)} %bitcast.48, s32[320]{0:T(512)} %select_reduce_fusion.place_ref, f32[2]{0:T(128)} %bias_ref.1, bf16[96,512]{1,0:T(8,128)(2,1)} %bitcast.62, bf16[2,2,96,512]{3,2,1,0:T(8,128)(2,1)} %bitcast.60, f32[4,8,96]{2,1,0:T(8,128)} %pad.15.lab_ref, ...), custom_call_target="tpu_custom_call" | custom-call | tf_op jit(solution)/shard_map/pallas_call | solution.py:1061
  290.6 1.2 fusion.5
  291.8 73.6 %shard_map.307 = (f32[40,128,128]{2,1,0:T(8,128)}, bf16[40,128,128]{2,1,0:T(8,128)(2,1)}, f32[40,128,128]{2,1,0:T(8,128)}, f32[40,128,128]{2,1,0:T(8,128)}, f32[...) custom-call(s32[320]{0:T(512)} %refs_0_.1, ...), custom_call_target="tpu_custom_call" | custom-call | tf_op jit(solution)/shard_map/pallas_call | solution.py:1362
  365.4 54.7 %shard_map.308 = (f32[5120,128]{1,0:T(8,128)}, f32[5120,128]{1,0:T(8,128)}, f32[40,128,128]{2,1,0:T(8,128)}, bf16[40,128,128]{2,1,0:T(8,128)(2,1)}, f32[40,128,1...) custom-call(f32[5120,128]{1,0:T(8,128)} %bitcast.58, ...), custom_call_target="tpu_custom_call" | custom-call | tf_op jit(solution)/shard_map/pallas_call | solution.py:1557
  420.2 1.0 fusion.4
  421.2 0.8 slice_bitcast_fusion.1
  422.0 0.1 copy.59
  422.2 0.2 reshape.76
  422.4 0.6 multiply_subtract_fusion
  423.0 0.8 slice_reduce_fusion
  423.9 0.5 multiply_subtract_fusion.1
  (31 shorter events, 0.8 us)
Async XLA Ops:
  0.6 9.4 %copy-start = (f32[6144]{0:T(1024)S(1)}, f32[6144]{0:T(1024)}, u32[]{:S(2)}) copy-start(f32[6144]{0:T(1024)} %param.32) | copy-start | bytes 73732
  365.4 57.0 %copy-start.1 = (f32[6144]{0:T(1024)S(1)}, f32[6144]{0:T(1024)}, u32[]{:S(2)}) copy-start(f32[6144]{0:T(1024)} %param.34) | copy-start | bytes 73732
  365.4 57.0 %copy-start.2 = (f32[6144]{0:T(1024)S(1)}, f32[6144]{0:T(1024)}, u32[]{:S(2)}) copy-start(f32[6144]{0:T(1024)} %param.33) | copy-start | bytes 73732
  365.4 58.4 %copy-start.3 = (f32[2]{0:T(128)S(1)}, f32[2]{0:T(128)}, u32[]{:S(2)}) copy-start(f32[2]{0:T(128)} %bias_ref.1) | copy-start | bytes 28
  365.4 58.4 %copy-start.4 = (f32[2]{0:T(128)S(1)}, f32[2]{0:T(128)}, u32[]{:S(2)}) copy-start(f32[2]{0:T(128)} %param.37) | copy-start | bytes 28
  365.4 58.4 %copy-start.5 = (f32[2]{0:T(128)S(1)}, f32[2]{0:T(128)}, u32[]{:S(2)}) copy-start(f32[2]{0:T(128)} %param.36) | copy-start | bytes 28

commit v5 on v4

--- a/solution.py
+++ b/solution.py
@@ -284,7 +284,7 @@
             ).start()
             return 0
 
-        lax.fori_loop(1, nr, start, 0)
+        lax.fori_loop(1, nr, start, 0, unroll=nr <= 8)
 
     def reduce_finish(number, buffer):
         def wait(step, _):
@@ -301,8 +301,10 @@
             copy.wait_send()
             return 0
 
-        lax.fori_loop(1, nr, wait, 0)
-        return lax.fori_loop(1, nr, lambda k, total: total + buffer[k], buffer[0])
+        lax.fori_loop(1, nr, wait, 0, unroll=nr <= 8)
+        return lax.fori_loop(
+            1, nr, lambda k, total: total + buffer[k], buffer[0], unroll=nr <= 8
+        )
 
     def all_reduce(number, buffer):
         reduce_start(number, buffer)
@@ -423,8 +425,6 @@
                 skip.hop(1)
                 self.hand(x, 0)
                 self.hand(y, 1)
-                for k in range(2, nb):
-                    skip.hop(k)
                 self.hand(corner, 0)
                 self.hand(corner, 1)
                 rows = (r, x, y, corner)
@@ -452,8 +452,7 @@
                     return 0
 
                 lax.fori_loop(1, self.chips, pass_on, 0)
-                for k in range(1, nb):
-                    skip.hop(k)
+                skip.hop(1)
                 self.arrived(self.mate, 0)
                 self.move(2, self.mate, r, 0).wait_send()
                 lax.fori_loop(1, self.chips, close, 0)
@@ -577,8 +576,11 @@
         dz_high[3] = jnp.zeros_like(dz_high[3])
 
     gather.forward(moves)
-    for move in moves:
-        move.finish()
+    move_image.finish()
+    move_lab.finish()
+    middle = max(1, nb // 2)
+    for k in range(2, middle + 1):
+        move_skip.hop(k)
 
     def arrange(number, target):
         out, width, taps, first = layers[number]
@@ -647,6 +649,8 @@
     arrange(3, w_three)
     conv_low(z_two, w_two, lambda dy: a_one[dy], (1,))
     move.finish()
+    for k in range(middle + 1, nb):
+        move_skip.hop(k)
     conv_low(z_two, w_two, lambda dy: a_one[dy], (0, 2), True)
     norm_sums(reduce_two, z_two)
     total = all_reduce(1, reduce_two)
@@ -694,6 +698,7 @@
     every = ((0, 1, 2), (0, 1, 2))
     inner, outer = ((1, 2), (0, 1)), ((0,), (2,))
     move.begin()
+    move_skip.finish()
     conv_high(high_product(x_skip, C0, every), False)
     move.hops()
     conv_high(high_product(u_full, 0, inner), True)
@@ -1192,6 +1197,8 @@
     mate = r + 1 - 2 * core
     count = ins[0].shape[0]
     chunks = count // size
+    square = in_square(chips, size)
+    half = size // 2
 
     def device(chip, core):
         return {"rows": 2 * chip + core, "blk": b}
@@ -1211,7 +1218,6 @@
         return 0
 
     lax.fori_loop(1, chips, greet, 0)
-    pl.semaphore_wait(barrier, chips)
 
     def loads(chunk):
         return [
@@ -1240,6 +1246,10 @@
 
     def mine(to_chip, to_core, chunk, index):
         return grad_ref[owner_ref[(2 * to_chip + to_core) * count + chunk * size + index]]
+
+    def joined(to_chip, chunk, index):
+        value = mine(to_chip, core, chunk, index).astype(f32)
+        return value + in_a[chunk, to_chip, index].astype(f32)
 
     def send_a(chunk):
         return pltpu.make_async_remote_copy(
@@ -1251,102 +1261,186 @@
             device_id_type=MESH,
         )
 
-    def send_b(chunk, step):
-        other = lax.rem(chip + step, chips)
-        return pltpu.make_async_remote_copy(
-            src_ref=out_b.at[chunk, other],
-            dst_ref=in_b.at[chunk, chip],
-            send_sem=b_send.at[chunk, step],
-            recv_sem=b_recv.at[chunk, chip],
-            device_id=device(other, core),
-            device_id_type=MESH,
-        )
-
-    for copy in loads(0):
-        copy.start()
-    for chunk in range(chunks):
-
-        def fill(n, _, chunk=chunk):
+    def fill_a(chunk):
+        def fill(n, _):
             to_chip, index = lax.div(n, size), lax.rem(n, size)
             out_a[chunk, to_chip, index] = mine(to_chip, 1 - core, chunk, index)
             return 0
 
         lax.fori_loop(0, chips * size, fill, 0)
         send_a(chunk).start()
-    for chunk in range(chunks):
-        send_a(chunk).wait_recv()
-
-        def join(step, _, chunk=chunk):
+
+    class Straight:
+        def copy(self, chunk, step, source):
             other = lax.rem(chip + step, chips)
-
-            def each(index, _):
-                value = mine(other, core, chunk, index).astype(f32)
-                value = value + in_a[chunk, other, index].astype(f32)
-                out_b[chunk, other, index] = value.astype(bf16)
+            return pltpu.make_async_remote_copy(
+                src_ref=out_b.at[chunk, other],
+                dst_ref=in_b.at[chunk, source],
+                send_sem=b_send.at[chunk, step],
+                recv_sem=b_recv.at[chunk, source],
+                device_id=device(other, core),
+                device_id_type=MESH,
+            )
+
+        def first(self, chunk):
+            def join(step, _):
+                other = lax.rem(chip + step, chips)
+
+                def each(index, _):
+                    out_b[chunk, other, index] = joined(other, chunk, index).astype(bf16)
+                    return 0
+
+                lax.fori_loop(0, size, each, 0)
+                self.copy(chunk, step, chip).start()
                 return 0
 
-            lax.fori_loop(0, size, each, 0)
-            send_b(chunk, step).start()
+            lax.fori_loop(1, chips, join, 0)
+
+        def second(self, chunk):
+            pass
+
+        def arrive(self, chunk):
+            def wait(step, _):
+                self.copy(chunk, step, lax.rem(chip + step, chips)).wait_recv()
+                return 0
+
+            lax.fori_loop(1, chips, wait, 0)
+
+        def grad(self, chunk, index):
+            return lax.fori_loop(
+                1,
+                chips,
+                lambda step, value: value
+                + in_b[chunk, lax.rem(chip + step, chips), index].astype(f32),
+                total[chunk, index],
+            )
+
+        def close(self, chunk):
+            def wait(step, _):
+                self.copy(chunk, step, chip).wait_send()
+                return 0
+
+            lax.fori_loop(1, chips, wait, 0)
+
+    class Square:
+        def __init__(self):
+            self.x = chip + 1 - 2 * lax.rem(chip, 2)
+            self.y = chip + 2 - 4 * lax.div(chip, 2)
+            self.corner = 3 - chip
+
+        def one(self, chunk, way):
+            return pltpu.make_async_remote_copy(
+                src_ref=out_b.at[chunk, pl.ds(2 * way, 2)],
+                dst_ref=in_b.at[chunk, pl.ds(2 * way, 2)],
+                send_sem=b_send.at[chunk, way],
+                recv_sem=b_recv.at[chunk, way],
+                device_id=device((self.x, self.y)[way], core),
+                device_id_type=MESH,
+            )
+
+        def two(self, chunk, way):
+            return pltpu.make_async_remote_copy(
+                src_ref=out_b.at[chunk, 4 + way],
+                dst_ref=in_b.at[chunk, 4 + way],
+                send_sem=b_send.at[chunk, 2 + way],
+                recv_sem=b_recv.at[chunk, 2 + way],
+                device_id=device((self.y, self.x)[way], core),
+                device_id_type=MESH,
+            )
+
+        def first(self, chunk):
+            for way, near in enumerate((self.x, self.y)):
+
+                def each(index, _, way=way, near=near):
+                    slot = way * half + index
+                    out_b[chunk, 2 * way, index] = joined(near, chunk, slot).astype(bf16)
+                    value = joined(self.corner, chunk, slot)
+                    out_b[chunk, 2 * way + 1, index] = value.astype(bf16)
+                    return 0
+
+                lax.fori_loop(0, half, each, 0)
+                self.one(chunk, way).start()
+
+        def second(self, chunk):
+            for way, far in enumerate((self.y, self.x)):
+                self.one(chunk, way).wait_recv()
+
+                def each(index, _, way=way, far=far):
+                    value = joined(far, chunk, way * half + index)
+                    value = value + in_b[chunk, 2 * way + 1, index].astype(f32)
+                    out_b[chunk, 4 + way, index] = value.astype(bf16)
+                    return 0
+
+                lax.fori_loop(0, half, each, 0)
+                self.two(chunk, way).start()
+
+        def arrive(self, chunk):
+            for way in range(2):
+                self.two(chunk, way).wait_recv()
+
+        def grad(self, chunk, index):
+            way, place = index // half, index % half
+            value = total[chunk, index] + in_b[chunk, 2 * way, place].astype(f32)
+            return value + in_b[chunk, 4 + way, place].astype(f32)
+
+        def close(self, chunk):
+            for way in range(2):
+                self.one(chunk, way).wait_send()
+                self.two(chunk, way).wait_send()
+
+    plan = Square() if square else Straight()
+
+    def keep(chunk):
+        def each(index, _):
+            total[chunk, index] = joined(chip, chunk, index)
             return 0
 
-        lax.fori_loop(1, chips, join, 0)
-
-        def keep(index, _, chunk=chunk):
-            value = mine(chip, core, chunk, index).astype(f32)
-            total[chunk, index] = value + in_a[chunk, chip, index].astype(f32)
-            return 0
-
-        lax.fori_loop(0, size, keep, 0)
-    for chunk in range(chunks):
-        if chunk + 1 < chunks:
-            for copy in loads(chunk + 1):
-                copy.start()
+        lax.fori_loop(0, size, each, 0)
+
+    def work(chunk):
+        plan.arrive(chunk)
         for copy in loads(chunk):
             copy.wait()
         if chunk >= 2:
             for copy in stores(chunk - 2):
                 copy.wait()
-
-        def arrive(step, _, chunk=chunk):
-            other = lax.rem(chip + step, chips)
-            pltpu.make_async_remote_copy(
-                src_ref=out_b.at[chunk, other],
-                dst_ref=in_b.at[chunk, other],
-                send_sem=b_send.at[chunk, step],
-                recv_sem=b_recv.at[chunk, other],
-                device_id=device(other, core),
-                device_id_type=MESH,
-            ).wait_recv()
-            return 0
-
-        lax.fori_loop(1, chips, arrive, 0)
         slot = chunk % 2
         chunk_ins = [in_buffer.at[slot, number] for number in range(7)]
         chunk_outs = [out_buffer.at[slot, number] for number in range(9)]
         chunk_outs.insert(1, copy_buffer.at[slot])
-
-        grads = []
-        for index in range(size):
-            grads.append(
-                lax.fori_loop(
-                    1,
-                    chips,
-                    lambda step, value, chunk=chunk, index=index: value
-                    + in_b[chunk, lax.rem(chip + step, chips), index].astype(f32),
-                    total[chunk, index],
-                )
-            )
+        grads = [plan.grad(chunk, index) for index in range(size)]
         soap_blocks(range(size), grads, chunk_ins, chunk_outs)
         for copy in stores(chunk):
             copy.start()
+        if chunk + 2 < chunks:
+            for copy in loads(chunk + 2):
+                copy.start()
+
+    for chunk in range(min(2, chunks)):
+        for copy in loads(chunk):
+            copy.start()
+    pl.semaphore_wait(barrier, chips)
+    for chunk in range(chunks):
+        fill_a(chunk)
+    for chunk in range(chunks + 2):
+        if chunk < chunks:
+            send_a(chunk).wait_recv()
+            plan.first(chunk)
+            keep(chunk)
+        if 1 <= chunk <= chunks:
+            plan.second(chunk - 1)
+        if chunk >= 2:
+            work(chunk - 2)
     for chunk in range(chunks):
         send_a(chunk).wait_send()
-        lax.fori_loop(
-            1, chips, lambda step, _, chunk=chunk: (send_b(chunk, step).wait_send(), 0)[1], 0
-        )
+        plan.close(chunk)
         if chunk >= chunks - 2:
             for copy in stores(chunk):
                 copy.wait()
+
+
+def in_square(chips, size):
+    return chips == 4 and size % 2 == 0
 
 
 def soap_update(blocks, owner, states):
@@ -1359,24 +1453,26 @@
     shape = jax.ShapeDtypeStruct(states[0].shape, f32)
     dma = pltpu.SemaphoreType.DMA
     square = (order, order)
+    chips = nr // 2
+    parts = (6, size // 2) if in_square(chips, size) else (chips, size)
     results = pl.pallas_call(
         functools.partial(collect_kernel, nr, size),
         out_shape=(shape, jax.ShapeDtypeStruct(shape.shape, bf16)) + (shape,) * 8,
         in_specs=[pl.BlockSpec(memory_space=pltpu.SMEM), vmem] + [anywhere] * 7,
         out_specs=[anywhere] * 10,
         scratch_shapes=[
-            pltpu.VMEM((chunks, nr // 2, size) + square, bf16),
-            pltpu.VMEM((chunks, nr // 2, size) + square, bf16),
-            pltpu.VMEM((chunks, nr // 2, size) + square, bf16),
-            pltpu.VMEM((chunks, nr // 2, size) + square, bf16),
+            pltpu.VMEM((chunks, chips, size) + square, bf16),
+            pltpu.VMEM((chunks, chips, size) + square, bf16),
+            pltpu.VMEM((chunks,) + parts + square, bf16),
+            pltpu.VMEM((chunks,) + parts + square, bf16),
             pltpu.VMEM((chunks, size) + square, f32),
             pltpu.VMEM((2, 7, size) + square, f32),
             pltpu.VMEM((2, 9, size) + square, f32),
             pltpu.VMEM((2, size) + square, bf16),
             dma((chunks,)),
             dma((chunks,)),
-            dma((chunks, nr // 2)),
-            dma((chunks, nr // 2)),
+            dma((chunks, chips)),
+            dma((chunks, chips)),
             dma((2, 7)),
             dma((2, 10)),
         ],

time: 432 us -> 417 us (0.965)
  Pallas kernels: 408 us -> 393 us
    pallas_call x1, Pallas kernels: 73.6 us -> 61 us  [soap_update(): pl.pallas_call(functools.partial(collect_kernel, nr, size), out_shape=(sh...]
where the time goes in v5:
time: 417 us; the launch traced here: 410 us
  Pallas kernels  393 us (94%)
  local copies, waits for them, and re-layouts  9.51 us (2%)
  other arithmetic  5.94 us (1%)
    pallas_call x1, Pallas kernels, run_step(): pl.pallas_call(functools.partial(step_kernel, nr, nb, cols), out_shape=(j...  277 us
    pallas_call x1, Pallas kernels, soap_update(): pl.pallas_call(functools.partial(collect_kernel, nr, size), out_shape=(sh...  61 us
    pallas_call x1, Pallas kernels, new_bases(): pl.pallas_call(basis_kernel, out_shape=[jax.ShapeDtypeStruct(value.shape,...  54.7 us

profile of v5, /device:TPU:1, one launch (start us, length us, event | category | flops | bytes accessed | tf_op | source)
XLA Modules:
  0.0 409.6 jit_solution(9353695204664528190)
XLA Ops:
  0.7 1.4 select_reduce_fusion.place_ref
  2.1 1.4 copy.52
  3.5 0.8 copy.62
  4.3 0.7 convert_element_type.16
  5.2 0.7 convert_element_type.18
  5.9 0.1 stack.40
  6.1 0.7 multiply_multiply_fusion.1
  7.1 0.6 pad.15.lab_ref
  7.7 0.8 fusion.6
  8.5 0.6 select_maximum_fusion.1.wide_ref
  9.1 0.7 slice.46
  9.8 0.2 slice.47
  10.2 0.6 select_maximum_fusion.narrow_ref
  10.8 277.1 %shard_map.306 = (bf16[320,128,128]{2,1,0:T(8,128)(2,1)}, f32[4,16,256]{2,1,0:T(8,128)}) custom-call(f32[40,128,128]{2,1,0:T(8,128)} %bitcast.48, s32[320]{0:T(512)} %select_reduce_fusion.place_ref, f32[2]{0:T(128)} %bias_ref.1, bf16[96,512]{1,0:T(8,128)(2,1)} %bitcast.62, bf16[2,2,96,512]{3,2,1,0:T(8,128)(2,1)} %bitcast.60, f32[4,8,96]{2,1,0:T(8,128)} %pad.15.lab_ref, ...), custom_call_target="tpu_custom_call" | custom-call | tf_op jit(solution)/shard_map/pallas_call | solution.py:1066
  287.9 1.2 fusion.5
  289.2 61.0 %shard_map.307 = (f32[40,128,128]{2,1,0:T(8,128)}, bf16[40,128,128]{2,1,0:T(8,128)(2,1)}, f32[40,128,128]{2,1,0:T(8,128)}, f32[40,128,128]{2,1,0:T(8,128)}, f32[...) custom-call(s32[320]{0:T(512)} %refs_0_.1, ...), custom_call_target="tpu_custom_call" | custom-call | tf_op jit(solution)/shard_map/pallas_call | solution.py:1458
  350.2 54.7 %shard_map.308 = (f32[5120,128]{1,0:T(8,128)}, f32[5120,128]{1,0:T(8,128)}, f32[40,128,128]{2,1,0:T(8,128)}, bf16[40,128,128]{2,1,0:T(8,128)(2,1)}, f32[40,128,1...) custom-call(f32[5120,128]{1,0:T(8,128)} %bitcast.58, ...), custom_call_target="tpu_custom_call" | custom-call | tf_op jit(solution)/shard_map/pallas_call | solution.py:1653
  404.9 1.0 fusion.4
  406.0 0.8 slice_bitcast_fusion.1
  406.8 0.1 copy.59
  407.0 0.2 reshape.76
  407.2 0.6 multiply_subtract_fusion
  407.8 0.8 slice_reduce_fusion
  408.6 0.5 multiply_subtract_fusion.1
  (31 shorter events, 0.8 us)
Async XLA Ops:
  0.6 9.4 %copy-start = (f32[6144]{0:T(1024)S(1)}, f32[6144]{0:T(1024)}, u32[]{:S(2)}) copy-start(f32[6144]{0:T(1024)} %param.32) | copy-start | bytes 73732
  350.2 57.0 %copy-start.1 = (f32[6144]{0:T(1024)S(1)}, f32[6144]{0:T(1024)}, u32[]{:S(2)}) copy-start(f32[6144]{0:T(1024)} %param.34) | copy-start | bytes 73732
  350.2 57.0 %copy-start.2 = (f32[6144]{0:T(1024)S(1)}, f32[6144]{0:T(1024)}, u32[]{:S(2)}) copy-start(f32[6144]{0:T(1024)} %param.33) | copy-start | bytes 73732
  350.2 58.4 %copy-start.3 = (f32[2]{0:T(128)S(1)}, f32[2]{0:T(128)}, u32[]{:S(2)}) copy-start(f32[2]{0:T(128)} %bias_ref.1) | copy-start | bytes 28
  350.2 58.4 %copy-start.4 = (f32[2]{0:T(128)S(1)}, f32[2]{0:T(128)}, u32[]{:S(2)}) copy-start(f32[2]{0:T(128)} %param.37) | copy-start | bytes 28
  350.2 58.4 %copy-start.5 = (f32[2]{0:T(128)S(1)}, f32[2]{0:T(128)}, u32[]{:S(2)}) copy-start(f32[2]{0:T(128)} %param.36) | copy-start | bytes 28

commit v6 on v5

--- a/solution.py
+++ b/solution.py
@@ -63,8 +63,8 @@
     image_ref,
     skip_ref,
     lab_ref,
-    wide_ref,
-    narrow_ref,
+    params_ref,
+    head_ref,
     grad_ref,
     sums_ref,
     x_one,
@@ -598,9 +598,14 @@
         lax.fori_loop(0, out // TILE * taps * across, body, 0)
 
     arrange(0, w_one)
-    gain_one, shift_one = wide_ref[0:1, :], wide_ref[1:2, :]
-    gain_two, shift_two = wide_ref[2:3, :], wide_ref[3:4, :]
-    gain_three, shift_three = narrow_ref[0:1, :], narrow_ref[1:2, :]
+    def own_params(first, width):
+        start = first // TILE + b * (width // TILE)
+        return jnp.concatenate(
+            [params_ref[pl.ds(start + n, 1), :] for n in range(width // TILE)], 1
+        )
+
+    gain_one, shift_one, gain_two, shift_two = [own_params(n * C1, wide) for n in range(4)]
+    gain_three, shift_three = [own_params(4 * C1 + n * C0, slim) for n in range(2)]
     size_low, size_high = C1 // GROUPS, C0 // GROUPS
 
     def conv_low(z_ref, weight, source, lines=(0, 1, 2), more=False):
@@ -713,7 +718,7 @@
         a_three[part, 0, rows_of(image), :] = value
 
     norm_apply(total, z_three, inv_three, gain_three, shift_three, size_high, put_three)
-    head_low = narrow_ref[8:16, :].astype(bf16)
+    head_low = head_ref[...].astype(bf16)
     head = head_low.astype(f32)
     for part in range(4):
         for image in range(nb):
@@ -734,8 +739,8 @@
             tile = tile + logit[j, part * nb + image]
         first = tile[0:1, :] + bias_ref[0]
         second = tile[1:2, :] + bias_ref[1]
-        scale = x_lab[image, part, 0:1, :]
-        label = x_lab[image, part, 1:2, :]
+        label = x_lab[image, part, 0:1, :]
+        scale = x_lab[image, part, 1:2, :] * x_lab[image, part, 2:3, :] * 0.125
         largest = jnp.maximum(first, second)
         log_total = jnp.log(jnp.exp(first - largest) + jnp.exp(second - largest)) + largest
         picked = first * (1.0 - label) + second * label
@@ -1007,7 +1012,7 @@
     spread.finish()
 
 
-def run_step(master, place, bias, image, skip, lab, wide_rows, narrow_rows):
+def run_step(master, place, bias, image, skip, lab, params, head):
     nr, nb = lax.axis_size("rows"), lax.axis_size("blk")
     cols = image.shape[0]
     px = nb * cols
@@ -1075,12 +1080,144 @@
         compiler_params=pltpu.CompilerParams(
             collective_id=0, has_side_effects=True, vmem_limit_bytes=60 * 2**20
         ),
-    )(master, place, bias, image, skip, lab, wide_rows, narrow_rows)
+    )(master, place, bias, image, skip, lab, params, head)
+
+
+LANES = 128
+
+
+def inverse_factor_kernel(stat_ref, inverse_ref, factor_ref):
+    order = stat_ref.shape[0]
+    tile = (8, LANES)
+    sub = lax.broadcasted_iota(jnp.int32, tile, 0)
+    groups = order // 8
+
+    def eliminate(source_ref, base, starts, first, count, accs):
+        width = len(starts)
+
+        def body(group, accs):
+            top = pl.multiple_of(group * 8, 8)
+            accs = [list(acc) for acc in accs]
+            for unit in range(8):
+                values = [source_ref[top + unit, pl.ds(start, 8), :] for start in starts]
+                for c in range(8):
+                    scale = jnp.broadcast_to(
+                        factor_ref[top + unit, pl.ds(base + c, 1), :], tile
+                    )
+                    for s in range(width):
+                        accs[s][c] = accs[s][c] - values[s] * scale
+            return tuple(tuple(acc) for acc in accs)
+
+        return lax.fori_loop(first, count, body, tuple(tuple(acc) for acc in accs))
+
+    def batches(first, last, run):
+        total = last - first
+
+        def at(group):
+            return pl.multiple_of(group * 8, 8)
+
+        def two(n, _):
+            run(first + 2 * n, [at(first + 2 * n), at(first + 2 * n + 1)])
+            return 0
+
+        lax.fori_loop(0, lax.div(total, 2), two, 0)
+
+        @pl.when(lax.rem(total, 2) == 1)
+        def _():
+            run(last - 1, [at(last - 1)])
+
+    def block(kb, _):
+        base = pl.multiple_of(kb * 8, 8)
+        accs = [stat_ref[base + c, pl.ds(base, 8), :] for c in range(8)]
+        accs = list(eliminate(factor_ref, base, [base], 0, kb, [accs])[0])
+        scale = []
+        coef = {}
+        for c in range(8):
+            scale.append(jnp.broadcast_to(lax.rsqrt(accs[c][c : c + 1, :]), tile))
+            accs[c] = accs[c] * scale[c]
+            for d in range(c + 1, 8):
+                coef[(c, d)] = jnp.broadcast_to(accs[c][d : d + 1, :], tile)
+                accs[d] = accs[d] - accs[c] * coef[(c, d)]
+        for c in range(8):
+            factor_ref[base + c, pl.ds(base, 8), :] = jnp.where(sub >= c, accs[c], 0.0)
+
+        def finish(accs, target_ref, start):
+            accs = list(accs)
+            for c in range(8):
+                for e in range(c):
+                    accs[c] = accs[c] - accs[e] * coef[(e, c)]
+                accs[c] = accs[c] * scale[c]
+                target_ref[base + c, pl.ds(start, 8), :] = accs[c]
+
+        def below(group, starts):
+            accs = [[stat_ref[base + c, pl.ds(s, 8), :] for c in range(8)] for s in starts]
+            accs = eliminate(factor_ref, base, starts, 0, kb, accs)
+            for acc, start in zip(accs, starts):
+                finish(acc, factor_ref, start)
+
+        def left(group, starts):
+            accs = [[jnp.zeros(tile, jnp.float32) for c in range(8)] for s in starts]
+            accs = eliminate(inverse_ref, base, starts, group, kb, accs)
+            for acc, start in zip(accs, starts):
+                finish(acc, inverse_ref, start)
+
+        def clear(group, _):
+            start = pl.multiple_of(group * 8, 8)
+            for c in range(8):
+                inverse_ref[base + c, pl.ds(start, 8), :] = jnp.zeros(tile, jnp.float32)
+            return 0
+
+        batches(kb + 1, groups, below)
+        batches(0, kb, left)
+        finish([jnp.where(sub == c, 1.0, 0.0) for c in range(8)], inverse_ref, base)
+        lax.fori_loop(kb + 1, groups, clear, 0)
+        return 0
+
+    lax.fori_loop(0, groups, block, 0)
 
 
 def split(value):
     high = value.astype(bf16)
     return high, (value - high.astype(f32)).astype(bf16)
+
+
+def split_three(value):
+    high = value.astype(bf16)
+    rest = value - high.astype(f32)
+    middle = rest.astype(bf16)
+    return high, middle, (rest - middle.astype(f32)).astype(bf16)
+
+
+def diagonal(pair):
+    u, v = pair
+    empty = jnp.zeros_like(u)
+    return jnp.concatenate(
+        [jnp.concatenate([u, empty], 1), jnp.concatenate([empty, v], 1)], 0
+    )
+
+
+def pair_product(packed, pair):
+    a, b = split(packed)
+    u, v = [split(value) for value in pair]
+    c, d = diagonal((u[0], v[0])), diagonal((u[1], v[1]))
+    result = dot_nn(jnp.concatenate([a, a, b], 1), jnp.concatenate([c, d, c], 0))
+    order = packed.shape[1]
+    return result[:, :order], result[:, order:]
+
+
+def pair_cross(one, two):
+    a, b = [jnp.concatenate(half, 1) for half in zip(*[split(value) for value in one])]
+    c, d = [diagonal(half) for half in zip(*[split(value) for value in two])]
+    return dot_nt(jnp.concatenate([a, a, b], 1), jnp.concatenate([c, d, c], 1))
+
+
+def pair_square(pair):
+    thirds = list(zip(*[split_three(value) for value in pair]))
+    a, b, c = [jnp.concatenate(third, 1) for third in thirds]
+    d, e, f = [diagonal(third) for third in thirds]
+    return dot_nt(
+        jnp.concatenate([a, a, b, a, b, c], 1), jnp.concatenate([d, e, d, f, e, d], 1)
+    )
 
 
 def product_three(left, right, right_dim):
@@ -1093,19 +1230,6 @@
     )
 
 
-def square_six(value):
-    high = value.astype(bf16)
-    rest = value - high.astype(f32)
-    middle = rest.astype(bf16)
-    low = (rest - middle.astype(f32)).astype(bf16)
-    return lax.dot_general(
-        jnp.concatenate([high, high, middle, high, middle, low], 1),
-        jnp.concatenate([high, middle, high, low, middle, high], 1),
-        (((1,), (1,)), ((), ())),
-        preferred_element_type=f32,
-    )
-
-
 def soap_blocks(indices, grads, ins, outs):
     def every(function, *lists):
         return [function(*items) for items in zip(*lists)]
@@ -1125,7 +1249,8 @@
     def three(dim):
         return lambda one, two: product_three(one, two, dim)
 
-    half = every(three(0), every(lambda value: split(value.T), left), sides)
+    lefts_turned = every(lambda value: split(value.T), left)
+    half = every(three(0), lefts_turned, sides)
     left_outer = every(three(1), sides, sides)
     rotated = every(three(0), every(split, half), bases)
     right_outer = every(three(1), turned, turned)
@@ -1155,9 +1280,11 @@
         )
         store(target, stat)
         stats.append(every(split, stat))
-    moved = every(three(0), stats[0], lefts)
+    moved = every(three(0), lefts_turned, stats[0])
     update = every(three(1), every(split, half), bases)
-    moved_right = every(three(0), stats[1], bases)
+    moved_right = every(
+        lambda stat, basis: product_three(stat, basis, 0).T, stats[1], bases
+    )
     master = every(
         lambda old, new: old - soap_rate * (new + soap_decay * old), load(master_ref), update
     )
@@ -1165,14 +1292,17 @@
     store(outs[1], every(lambda value: value.astype(bf16), master))
     store(outs[6], moved)
     store(outs[7], moved_right)
-    store(outs[8], every(lambda value: square_six(value.T), moved))
-    store(outs[9], every(lambda value: square_six(value.T), moved_right))
+    middle = moved[0].shape[0] // 2
+    store(
+        outs[8],
+        every(lambda one, two: pair_square((one[:middle], two[:middle])), moved, moved_right),
+    )
 
 
 def collect_kernel(nr, size, *refs):
     (owner_ref, grad_ref), refs = refs[:2], refs[2:]
     ins, refs = refs[:7], refs[7:]
-    outs, refs = refs[:10], refs[10:]
+    outs, refs = refs[:9], refs[9:]
     (
         out_a,
         in_a,
@@ -1182,6 +1312,7 @@
         in_buffer,
         out_buffer,
         copy_buffer,
+        gram_buffer,
         a_send,
         a_recv,
         b_send,
@@ -1232,11 +1363,10 @@
     def stores(chunk):
         copies = []
         for number, ref in enumerate(outs):
-            source = (
-                copy_buffer.at[chunk % 2]
-                if number == 1
-                else out_buffer.at[chunk % 2, number - (number > 1)]
-            )
+            if number in (1, 8):
+                source = {1: copy_buffer, 8: gram_buffer}[number].at[chunk % 2]
+            else:
+                source = out_buffer.at[chunk % 2, number - (number > 1)]
             copies.append(
                 pltpu.make_async_copy(
                     source, ref.at[pl.ds(chunk * size, size)], out_sem.at[chunk % 2, number]
@@ -1406,8 +1536,9 @@
                 copy.wait()
         slot = chunk % 2
         chunk_ins = [in_buffer.at[slot, number] for number in range(7)]
-        chunk_outs = [out_buffer.at[slot, number] for number in range(9)]
+        chunk_outs = [out_buffer.at[slot, number] for number in range(7)]
         chunk_outs.insert(1, copy_buffer.at[slot])
+        chunk_outs.append(gram_buffer.at[slot])
         grads = [plan.grad(chunk, index) for index in range(size)]
         soap_blocks(range(size), grads, chunk_ins, chunk_outs)
         for copy in stores(chunk):
@@ -1457,9 +1588,10 @@
     parts = (6, size // 2) if in_square(chips, size) else (chips, size)
     results = pl.pallas_call(
         functools.partial(collect_kernel, nr, size),
-        out_shape=(shape, jax.ShapeDtypeStruct(shape.shape, bf16)) + (shape,) * 8,
+        out_shape=(shape, jax.ShapeDtypeStruct(shape.shape, bf16)) + (shape,) * 6
+        + (jax.ShapeDtypeStruct((count, order // 2, order), f32),),
         in_specs=[pl.BlockSpec(memory_space=pltpu.SMEM), vmem] + [anywhere] * 7,
-        out_specs=[anywhere] * 10,
+        out_specs=[anywhere] * 9,
         scratch_shapes=[
             pltpu.VMEM((chunks, chips, size) + square, bf16),
             pltpu.VMEM((chunks, chips, size) + square, bf16),
@@ -1467,21 +1599,22 @@
             pltpu.VMEM((chunks,) + parts + square, bf16),
             pltpu.VMEM((chunks, size) + square, f32),
             pltpu.VMEM((2, 7, size) + square, f32),
-            pltpu.VMEM((2, 9, size) + square, f32),
+            pltpu.VMEM((2, 7, size) + square, f32),
             pltpu.VMEM((2, size) + square, bf16),
+            pltpu.VMEM((2, size, order // 2, order), f32),
             dma((chunks,)),
             dma((chunks,)),
             dma((chunks, chips)),
             dma((chunks, chips)),
             dma((2, 7)),
-            dma((2, 10)),
+            dma((2, 9)),
         ],
         compiler_params=pltpu.CompilerParams(
             collective_id=1, has_side_effects=True, vmem_limit_bytes=60 * 2**20
         ),
     )(owner, blocks, *states)
     kept = list(results[:6])
-    new_left, new_right, *kept = new_bases(results[6:8], results[8:], kept)
+    new_left, new_right, *kept = new_bases(results[6:8], results[8], kept)
     new_master, new_copy, new_first, new_second, new_left_stat, new_right_stat = kept
     return [
         new_master,
@@ -1495,104 +1628,11 @@
     ]
 
 
-LANES = 128
-
-
-def inverse_factor_kernel(stat_ref, inverse_ref, factor_ref):
-    order = stat_ref.shape[0]
-    tile = (8, LANES)
-    sub = lax.broadcasted_iota(jnp.int32, tile, 0)
-    groups = order // 8
-
-    def eliminate(source_ref, base, starts, first, count, accs):
-        width = len(starts)
-
-        def body(group, accs):
-            top = pl.multiple_of(group * 8, 8)
-            accs = [list(acc) for acc in accs]
-            for unit in range(8):
-                values = [source_ref[top + unit, pl.ds(start, 8), :] for start in starts]
-                for c in range(8):
-                    scale = jnp.broadcast_to(
-                        factor_ref[top + unit, pl.ds(base + c, 1), :], tile
-                    )
-                    for s in range(width):
-                        accs[s][c] = accs[s][c] - values[s] * scale
-            return tuple(tuple(acc) for acc in accs)
-
-        return lax.fori_loop(first, count, body, tuple(tuple(acc) for acc in accs))
-
-    def batches(first, last, run):
-        total = last - first
-
-        def at(group):
-            return pl.multiple_of(group * 8, 8)
-
-        def two(n, _):
-            run(first + 2 * n, [at(first + 2 * n), at(first + 2 * n + 1)])
-            return 0
-
-        lax.fori_loop(0, lax.div(total, 2), two, 0)
-
-        @pl.when(lax.rem(total, 2) == 1)
-        def _():
-            run(last - 1, [at(last - 1)])
-
-    def block(kb, _):
-        base = pl.multiple_of(kb * 8, 8)
-        accs = [stat_ref[base + c, pl.ds(base, 8), :] for c in range(8)]
-        accs = list(eliminate(factor_ref, base, [base], 0, kb, [accs])[0])
-        scale = []
-        coef = {}
-        for c in range(8):
-            scale.append(jnp.broadcast_to(lax.rsqrt(accs[c][c : c + 1, :]), tile))
-            accs[c] = accs[c] * scale[c]
-            for d in range(c + 1, 8):
-                coef[(c, d)] = jnp.broadcast_to(accs[c][d : d + 1, :], tile)
-                accs[d] = accs[d] - accs[c] * coef[(c, d)]
-        for c in range(8):
-            factor_ref[base + c, pl.ds(base, 8), :] = jnp.where(sub >= c, accs[c], 0.0)
-
-        def finish(accs, target_ref, start):
-            accs = list(accs)
-            for c in range(8):
-                for e in range(c):
-                    accs[c] = accs[c] - accs[e] * coef[(e, c)]
-                accs[c] = accs[c] * scale[c]
-                target_ref[base + c, pl.ds(start, 8), :] = accs[c]
-
-        def below(group, starts):
-            accs = [[stat_ref[base + c, pl.ds(s, 8), :] for c in range(8)] for s in starts]
-            accs = eliminate(factor_ref, base, starts, 0, kb, accs)
-            for acc, start in zip(accs, starts):
-                finish(acc, factor_ref, start)
-
-        def left(group, starts):
-            accs = [[jnp.zeros(tile, jnp.float32) for c in range(8)] for s in starts]
-            accs = eliminate(inverse_ref, base, starts, group, kb, accs)
-            for acc, start in zip(accs, starts):
-                finish(acc, inverse_ref, start)
-
-        def clear(group, _):
-            start = pl.multiple_of(group * 8, 8)
-            for c in range(8):
-                inverse_ref[base + c, pl.ds(start, 8), :] = jnp.zeros(tile, jnp.float32)
-            return 0
-
-        batches(kb + 1, groups, below)
-        batches(0, kb, left)
-        finish([jnp.where(sub == c, 1.0, 0.0) for c in range(8)], inverse_ref, base)
-        lax.fori_loop(kb + 1, groups, clear, 0)
-        return 0
-
-    lax.fori_loop(0, groups, block, 0)
-
-
-def basis_kernel(left_gram_ref, right_gram_ref, left_ref, right_ref, *refs):
-    number = (len(refs) - 7) // 3
+def basis_kernel(gram_ref, left_ref, right_ref, *refs):
+    number = (len(refs) - 9) // 3
     kept, new_left_ref, new_right_ref = refs[:number], refs[number], refs[number + 1]
     moved, refs = refs[number + 2 : 2 * number + 2], refs[2 * number + 2 :]
-    stat_ref, inverse_ref, factor_ref, in_sem, out_sem, *halts = refs
+    stat_ref, inverse_ref, factor_ref, solve_ref, rest_ref, in_sem, out_sem, *halts = refs
     arriving = [
         pltpu.make_async_copy(source, halt, in_sem.at[n])
         for n, (source, halt) in enumerate(zip(kept, halts))
@@ -1603,64 +1643,97 @@
     ]
     for copy in arriving:
         copy.start()
-    order = left_gram_ref.shape[1]
-    count = left_gram_ref.shape[0] // order
-    spare = LANES - 2 * count
-
-    def enter(row, _):
-        rows = pl.ds(row, count, stride=order)
-        values = [left_gram_ref[rows, :], right_gram_ref[rows, :]]
-        if spare:
-            column = lax.broadcasted_iota(jnp.int32, (spare, order), 1)
-            values.append(jnp.where(column == row, 1.0, 0.0))
-        stat_ref[row] = jnp.concatenate(values, 0).T
+    count, order = left_ref.shape[0], left_ref.shape[1]
+    half = order // 2
+    width = next(size for size in (8, 5, 4, 2, 1) if count % size == 0)
+    column = lax.broadcasted_iota(jnp.int32, (half, order), 1)
+
+    def invert(source_ref):
+        def enter(row, _):
+            value = source_ref[pl.ds(row, count, stride=half), :]
+            if count < half:
+                spare = column[: half - count]
+                spare = (spare == row) | (spare == row + half)
+                value = jnp.concatenate([value, jnp.where(spare, 1.0, 0.0)], 0)
+            value = jnp.concatenate([value, pltpu.roll(value, half, 1)], 0)
+            stat_ref[row] = value.T[:half]
+            return 0
+
+        lax.fori_loop(0, half, enter, 0, unroll=8)
+        inverse_factor_kernel(stat_ref, inverse_ref, factor_ref)
+
+        def leave(row, _):
+            value = inverse_ref[row]
+            value = jnp.concatenate([value, value], 0).T
+            solve_ref[pl.ds(row, count, stride=half), :] = jnp.where(
+                column[:count] < half, value[:count], value[half : half + count]
+            )
+            return 0
+
+        lax.fori_loop(0, half, leave, 0, unroll=8)
+
+    def rows(index):
+        return pl.ds(pl.multiple_of(index * half, half), half)
+
+    def project(step, _):
+        blocks = [step * width + n for n in range(width)]
+        first = [(left_ref[n, :half], right_ref[n, :half]) for n in blocks]
+        second = [(left_ref[n, half:], right_ref[n, half:]) for n in blocks]
+        first = [pair_product(solve_ref[rows(n), :], pair) for n, pair in zip(blocks, first)]
+        cross = [pair_cross(one, two) for one, two in zip(second, first)]
+        shares = [pair_product(value, pair) for value, pair in zip(cross, first)]
+        second = [
+            (pair[0] - share[0], pair[1] - share[1]) for pair, share in zip(second, shares)
+        ]
+        squares = [pair_square(pair) for pair in second]
+        for n, one, two, value in zip(blocks, first, second, squares):
+            for side, ref in enumerate((new_left_ref, new_right_ref)):
+                ref[n, :half] = one[side]
+                ref[n, half:] = two[side]
+            rest_ref[rows(n), :] = value
         return 0
 
-    lax.fori_loop(0, order, enter, 0, unroll=8)
+    def complete(step, _):
+        blocks = [step * width + n for n in range(width)]
+        refs = (new_left_ref, new_right_ref)
+        second = [
+            pair_product(solve_ref[rows(n), :], [ref[n, half:] for ref in refs]) for n in blocks
+        ]
+        for n, pair in zip(blocks, second):
+            for ref, value in zip(refs, pair):
+                ref[n] = jnp.concatenate([ref[n, :half], value], 0).T
+        return 0
+
+    invert(gram_ref)
     for come, go in zip(arriving, leaving):
         come.wait()
         go.start()
-    inverse_factor_kernel(stat_ref, inverse_ref, factor_ref)
-
-    def leave(row, _):
-        rows = pl.ds(row, count, stride=order)
-        value = inverse_ref[row].T
-        new_left_ref[rows, :] = value[:count]
-        new_right_ref[rows, :] = value[count : 2 * count]
-        return 0
-
-    lax.fori_loop(0, order, leave, 0, unroll=8)
-
-    def solve(index, _):
-        rows = pl.ds(pl.multiple_of(index * order, order), order)
-        for basis_ref, target_ref in ((left_ref, new_left_ref), (right_ref, new_right_ref)):
-            target_ref[rows, :] = product_three(
-                split(basis_ref[rows, :]), split(target_ref[rows, :]), 1
-            )
-        return 0
-
-    lax.fori_loop(0, count, solve, 0, unroll=8 if count % 8 == 0 else 1)
+    lax.fori_loop(0, count // width, project, 0)
+    invert(rest_ref)
+    lax.fori_loop(0, count // width, complete, 0)
     for copy in leaving:
         copy.wait()
 
 
 def new_bases(products, grams, kept):
     count, order = products[0].shape[0], products[0].shape[-1]
+    half = order // 2
     vmem = pl.BlockSpec(memory_space=pltpu.VMEM)
     anywhere = pl.BlockSpec(memory_space=pl.ANY)
-    lanes = pltpu.VMEM((order, order, LANES), f32)
-    flat = [value.reshape(count * order, order) for value in list(grams) + list(products)]
-    results = pl.pallas_call(
+    lanes = pltpu.VMEM((half, half, LANES), f32)
+    flat = pltpu.VMEM((count * half, order), f32)
+    return pl.pallas_call(
         basis_kernel,
-        out_shape=[jax.ShapeDtypeStruct(value.shape, value.dtype) for value in flat[:2] + kept],
-        in_specs=[vmem] * 4 + [anywhere] * len(kept),
+        out_shape=[
+            jax.ShapeDtypeStruct(value.shape, value.dtype) for value in list(products) + kept
+        ],
+        in_specs=[vmem] * 3 + [anywhere] * len(kept),
         out_specs=[vmem] * 2 + [anywhere] * len(kept),
-        scratch_shapes=[lanes, lanes, lanes]
+        scratch_shapes=[lanes, lanes, lanes, flat, flat]
         + [pltpu.SemaphoreType.DMA((len(kept),))] * 2
         + [pltpu.VMEM(value.shape, value.dtype) for value in kept],
         compiler_params=pltpu.CompilerParams(vmem_limit_bytes=60 * 2**20),
-    )(*flat, *kept)
-    return [value.reshape(products[0].shape) for value in results[:2]] + list(results[2:])
+    )(grams.reshape(count * half, order), *products, *kept)
 
 
 def adam_small(grads, value, first, second):
@@ -1701,27 +1774,22 @@
     slots = jnp.arange(owner.shape[0])
     place = jnp.sum(jnp.where(owner[None, :] == slots[:, None], slots[None, :], 0), 1)
     widths = (C1, C1, C1, C1, C0, C0)
-    rows = []
-    offset = 0
-    for width in widths:
-        part = width // shards
-        rows.append(lax.dynamic_slice_in_dim(norm_params, offset + shard * part, part))
-        offset = offset + width
-    heads = norm_params[offset:].reshape(C0, 2)
+    heads = norm_params[sum(widths) :].reshape(C0, 2)
     part = C0 // shards
     heads = lax.dynamic_slice_in_dim(heads, shard * part, part).T
-    wide_rows = jnp.pad(jnp.stack(rows[:4]), ((0, 4), (0, 0)))
-    narrow_rows = jnp.concatenate(
-        [jnp.pad(jnp.stack(rows[4:]), ((0, 6), (0, 0))), jnp.pad(heads, ((0, 6), (0, 0)))]
-    )
-    valid_float = valid.astype(f32)
-    scales = valid_float * weight_map.astype(f32) * 0.125
-    lab = jnp.stack([scales, labels.astype(f32), valid_float]).reshape(3, 2, cols, 2)
-    lab = lab.transpose(1, 3, 0, 2).reshape(4, 3, cols)
-    lab = jnp.pad(lab, ((0, 0), (0, 5), (0, 0)))
+    heads = jnp.pad(heads, ((0, 6), (0, 0)))
+    lab = jnp.stack([labels, weight_map, valid]).astype(f32).reshape(3, 2, cols, 2)
+    lab = jnp.pad(lab.transpose(1, 3, 0, 2).reshape(4, 3, cols), ((0, 0), (0, 5), (0, 0)))
     skip = skip.reshape(2, cols, 2, C0).transpose(0, 2, 1, 3)
     blocks, sums = run_step(
-        master[0], place.astype(jnp.int32), head_bias, image[0, 0], skip, lab, wide_rows, narrow_rows
+        master[0],
+        place.astype(jnp.int32),
+        head_bias,
+        image[0, 0],
+        skip,
+        lab,
+        norm_params.reshape(-1, TILE),
+        heads,
     )
     loss_sum, valid_count = sums[0, 6, 0], sums[0, 9, 0]
     grad_bias = sums[0, 7:9, 0]

time: 417 us -> 399 us (0.957)
  Pallas kernels: 393 us -> 378 us
    pallas_call x1, Pallas kernels: 54.7 us -> 39.6 us  [new_bases(): pl.pallas_call(basis_kernel, out_shape=[jax.ShapeDtypeStruct(value.shape,...]
where the time goes in v6:
time: 399 us; the launch traced here: 392 us
  Pallas kernels  378 us (95%)
  local copies, waits for them, and re-layouts  11.3 us (3%)
    pallas_call x1, Pallas kernels, run_step(): pl.pallas_call(functools.partial(step_kernel, nr, nb, cols), out_shape=(j...  277 us
    pallas_call x1, Pallas kernels, soap_update(): pl.pallas_call(functools.partial(collect_kernel, nr, size), out_shape=(sh...  60.9 us
    pallas_call x1, Pallas kernels, new_bases(): pl.pallas_call(basis_kernel, out_shape=[jax.ShapeDtypeStruct(value.shape,...  39.6 us

profile of v6, /device:TPU:1, one launch (start us, length us, event | category | flops | bytes accessed | tf_op | source)
XLA Modules:
  0.0 392.2 jit_solution(12537138870000493145)
XLA Ops:
  0.7 0.7 slice.46
  1.4 0.2 slice.47
  1.6 0.6 pad.9.head_ref
  2.3 1.4 copy.52
  3.7 0.8 copy.62
  4.5 0.8 stack.15
  5.3 0.1 copy.54
  5.4 0.8 stack.16
  6.2 0.1 copy.55
  6.3 0.8 stack.17
  7.1 0.1 copy.56
  7.2 0.6 pad.8.lab_ref
  7.8 0.7 select_reduce_fusion.place_ref
  8.6 277.2 %shard_map.306 = (bf16[320,128,128]{2,1,0:T(8,128)(2,1)}, f32[4,16,256]{2,1,0:T(8,128)}) custom-call(f32[40,128,128]{2,1,0:T(8,128)} %bitcast.38, s32[320]{0:T(512)} %select_reduce_fusion.place_ref, f32[2]{0:T(128)} %bias_ref.1, bf16[96,512]{1,0:T(8,128)(2,1)} %bitcast.50, bf16[2,2,96,512]{3,2,1,0:T(8,128)(2,1)} %bitcast.46, f32[4,8,96]{2,1,0:T(8,128)} %pad.8.lab_ref, ...), custom_call_target="tpu_custom_call" | custom-call | tf_op jit(solution)/shard_map/pallas_call | solution.py:1071
  285.7 60.9 %shard_map.307 = (f32[40,128,128]{2,1,0:T(8,128)}, bf16[40,128,128]{2,1,0:T(8,128)(2,1)}, f32[40,128,128]{2,1,0:T(8,128)}, f32[40,128,128]{2,1,0:T(8,128)}, f32[...) custom-call(s32[320]{0:T(512)} %refs_0_.1, ...), custom_call_target="tpu_custom_call" | custom-call | tf_op jit(solution)/shard_map/pallas_call | solution.py:1589
  346.8 39.6 %shard_map.308 = (f32[40,128,128]{2,1,0:T(8,128)}, f32[40,128,128]{2,1,0:T(8,128)}, f32[40,128,128]{2,1,0:T(8,128)}, bf16[40,128,128]{2,1,0:T(8,128)(2,1)}, f32[...) custom-call(f32[2560,128]{1,0:T(8,128)} %bitcast.48, ...), custom_call_target="tpu_custom_call" | custom-call | tf_op jit(solution)/shard_map/pallas_call | solution.py:1725
  386.4 1.0 fusion.5
  387.4 0.8 slice_bitcast_fusion.1
  388.2 0.1 copy.59
  388.4 0.2 reshape.81
  388.6 0.6 multiply_subtract_fusion
  389.2 0.8 slice_reduce_fusion
  390.0 0.5 multiply_subtract_fusion.1
  390.6 1.2 fusion.6
  (26 shorter events, 0.2 us)
Async XLA Ops:
  0.6 7.2 %copy-start.3 = (s32[320]{0:T(512)S(1)}, s32[320]{0:T(512)}, u32[]{:S(2)}) copy-start(s32[320]{0:T(512)} %refs_0_.1) | copy-start | bytes 3844
  346.7 41.9 %copy-start = (f32[6144]{0:T(1024)S(1)}, f32[6144]{0:T(1024)}, u32[]{:S(2)}) copy-start(f32[6144]{0:T(1024)} %param.32) | copy-start | bytes 73732
  346.7 41.9 %copy-start.1 = (f32[6144]{0:T(1024)S(1)}, f32[6144]{0:T(1024)}, u32[]{:S(2)}) copy-start(f32[6144]{0:T(1024)} %param.34) | copy-start | bytes 73732
  346.7 41.9 %copy-start.2 = (f32[6144]{0:T(1024)S(1)}, f32[6144]{0:T(1024)}, u32[]{:S(2)}) copy-start(f32[6144]{0:T(1024)} %param.33) | copy-start | bytes 73732
  346.7 43.3 %copy-start.4 = (f32[2]{0:T(128)S(1)}, f32[2]{0:T(128)}, u32[]{:S(2)}) copy-start(f32[2]{0:T(128)} %bias_ref.1) | copy-start | bytes 28
  346.7 43.3 %copy-start.5 = (f32[2]{0:T(128)S(1)}, f32[2]{0:T(128)}, u32[]{:S(2)}) copy-start(f32[2]{0:T(128)} %param.37) | copy-start | bytes 28
  346.7 43.3 %copy-start.6 = (f32[2]{0:T(128)S(1)}, f32[2]{0:T(128)}, u32[]{:S(2)}) copy-start(f32[2]{0:T(128)} %param.36) | copy-start | bytes 28

commit v7 on v6

--- a/solution.py
+++ b/solution.py
@@ -65,8 +65,10 @@
     lab_ref,
     params_ref,
     head_ref,
+    blocks_ref,
+    sums_ref,
     grad_ref,
-    sums_ref,
+    local_sem,
     x_one,
     x_skip,
     x_lab,
@@ -97,6 +99,7 @@
     send_low,
     recv_low,
     logit,
+    grad_logit,
     reduce_wide,
     reduce_narrow,
     gather_send,
@@ -722,9 +725,8 @@
     head = head_low.astype(f32)
     for part in range(4):
         for image in range(nb):
-            logit[b, part * nb + image] = dot_nt(
-                head_low, a_three[part, 0, rows_of(image), :]
-            )
+            tile = dot_nt(head_low, a_three[part, 0, rows_of(image), :])
+            logit[b, part, 2 * image : 2 * image + 2, :] = tile[:2]
     spread = Spread(all_send.at[0], all_recv.at[0], lambda other: logit.at[b], lambda j: logit.at[j])
     spread.begin()
     spread.finish()
@@ -734,9 +736,10 @@
     level = lax.broadcasted_iota(jnp.int32, (8, cols), 0)
 
     def head_of(part, image):
-        tile = logit[0, part * nb + image]
+        two = slice(2 * image, 2 * image + 2)
+        tile = logit[0, part, two, :]
         for j in range(1, nb):
-            tile = tile + logit[j, part * nb + image]
+            tile = tile + logit[j, part, two, :]
         first = tile[0:1, :] + bias_ref[0]
         second = tile[1:2, :] + bias_ref[1]
         label = x_lab[image, part, 0:1, :]
@@ -757,7 +760,7 @@
             loss = loss + cost
             bias_grad = [bias_grad[0] + first, bias_grad[1] + second]
             tile = jnp.where(level == 0, first, jnp.where(level == 1, second, 0.0))
-            logit[0, part * nb + image] = tile
+            grad_logit[part * nb + image] = tile
             head_grad = head_grad + jnp.dot(
                 tile,
                 a_three[part, 0, rows_of(image), :].astype(f32),
@@ -767,7 +770,7 @@
 
     def grad_three(part, image):
         return lax.dot_general(
-            logit[0, part * nb + image],
+            grad_logit[part * nb + image],
             head,
             (((0,), (0,)), ((), ())),
             preferred_element_type=f32,
@@ -849,10 +852,32 @@
         shifted_high[row, 1, :, slim : 2 * slim] = odd
         shifted_high[row, 1, :, 2 * slim :] = even
 
+    def put_grad(first, across, value, rows, start):
+        for row, number in rows:
+            for k in range(value.shape[1] // TILE):
+                grad_ref[first + number * across + start + k] = value[
+                    row : row + TILE, k * TILE : (k + 1) * TILE
+                ].astype(bf16)
+
+    def weight_high(dy):
+        out, width, taps, first = layers[3]
+        rows = [(dx * slim, 3 * dy + dx) for dx in range(3)]
+        for half, source in enumerate((u_full, x_skip)):
+            total = 0.0
+            for e in range(2):
+                for f in range(2):
+                    value = source[e + dy, f].reshape(px, C0)
+                    total = total + dot_nn(turned_high[e, :, f * px : (f + 1) * px], value)
+            put_grad(first, width // TILE, total, rows, half * (C0 // TILE))
+
     begin, finish = edges(0, dz_high.at[2], dz_high.at[0], dz_high.at[1], dz_high.at[3])
     begin()
     widen_high(1)
     widen_high(2)
+    for e in range(2):
+        for f in range(2):
+            turned_high[e, :, f * px : (f + 1) * px] = shifted_high[1 + e, f].T
+    weight_high(0)
     finish()
     widen_high(0)
     widen_high(3)
@@ -881,26 +906,8 @@
         spread.begin()
         spreads.append(spread)
 
-    def put_grad(first, across, value, rows, start):
-        for row, number in rows:
-            for k in range(value.shape[1] // TILE):
-                grad_ref[first + number * across + start + k] = value[
-                    row : row + TILE, k * TILE : (k + 1) * TILE
-                ].astype(bf16)
-
-    out, width, taps, first = layers[3]
-    for e in range(2):
-        for f in range(2):
-            turned_high[e, :, f * px : (f + 1) * px] = shifted_high[1 + e, f].T
-    for dy in range(3):
-        rows = [(dx * slim, 3 * dy + dx) for dx in range(3)]
-        for half, source in enumerate((u_full, x_skip)):
-            total = 0.0
-            for e in range(2):
-                for f in range(2):
-                    value = source[e + dy, f].reshape(px, C0)
-                    total = total + dot_nn(turned_high[e, :, f * px : (f + 1) * px], value)
-            put_grad(first, width // TILE, total, rows, half * (C0 // TILE))
+    weight_high(1)
+    weight_high(2)
     for part in range(4):
         spreads[part].finish()
         total = dy_high[part]
@@ -965,11 +972,10 @@
         shifted_low[row, :, wide : 2 * wide] = value
         shifted_low[row, :, 2 * wide :] = shift_down(wider).astype(bf16)
 
-    def weight_low(number, source):
+    def weight_low(number, source, lines):
         out, width, taps, first = layers[number]
-        turned_low[...] = shifted_low[1].T
         chunk = 2 * TILE
-        for dy in range(3):
+        for dy in lines:
             rows = []
             for dx in range(3):
                 for ob in range(wide // TILE):
@@ -984,6 +990,8 @@
     begin, finish = edges(1, dz_low.at[1], dz_low.at[0], dz_low.at[1], dz_low.at[2])
     begin()
     widen_low(1)
+    turned_low[...] = shifted_low[1].T
+    weight_low(1, lambda dy, start, size: a_one[dy, :, start : start + size], (0,))
     finish()
     widen_low(0)
     widen_low(2)
@@ -998,7 +1006,13 @@
         return total
 
     finish_sum = input_low(2, product_two)
-    weight_low(1, lambda dy, start, size: a_one[dy, :, start : start + size])
+    weight_low(1, lambda dy, start, size: a_one[dy, :, start : start + size], (1, 2))
+    ready = pltpu.make_async_copy(
+        grad_ref.at[pl.ds(layers[1][3], grad_ref.shape[0] - layers[1][3])],
+        blocks_ref.at[pl.ds(layers[1][3], grad_ref.shape[0] - layers[1][3])],
+        local_sem.at[0],
+    )
+    ready.start()
     finish_sum()
     gain_grad, shift_grad = back_low(5, z_one, inv_one, gain_one, shift_one)
     sums_ref[b, 0:1, :] = gain_grad
@@ -1008,8 +1022,17 @@
     )
     spread.begin()
     widen_low(1)
-    weight_low(0, lambda dy, start, size: x_one[dy].reshape(px, C0)[:, start : start + size])
+    turned_low[...] = shifted_low[1].T
+    weight_low(
+        0, lambda dy, start, size: x_one[dy].reshape(px, C0)[:, start : start + size], (0, 1, 2)
+    )
+    last = pltpu.make_async_copy(
+        grad_ref.at[pl.ds(0, layers[1][3])], blocks_ref.at[pl.ds(0, layers[1][3])], local_sem.at[1]
+    )
+    last.start()
     spread.finish()
+    ready.wait()
+    last.wait()
 
 
 def run_step(master, place, bias, image, skip, lab, params, head):
@@ -1021,6 +1044,8 @@
     smem = pl.BlockSpec(memory_space=pltpu.SMEM)
     dma = pltpu.SemaphoreType.DMA
     scratch = [
+        pltpu.VMEM((place.shape[0],) + master.shape[1:], bf16),
+        dma((2,)),
         pltpu.VMEM((3, nb, cols, C0), bf16),
         pltpu.VMEM((4, 2, nb, cols, C0), bf16),
         pltpu.VMEM((nb, 4, 8, cols), f32),
@@ -1050,7 +1075,8 @@
         pltpu.VMEM((4, nb, px, slim), bf16),
         pltpu.VMEM((nb, px, wide), bf16),
         pltpu.VMEM((2, nb, px, wide), bf16),
-        pltpu.VMEM((nb, 4 * nb, 8, cols), f32),
+        pltpu.VMEM((nb, 4, 2 * nb, cols), f32),
+        pltpu.VMEM((4 * nb, 8, cols), f32),
         pltpu.VMEM((4, nr, 2 * nb + 8, wide), f32),
         pltpu.VMEM((2, nr, 2 * nb + 8, slim), f32),
         dma((3, nr, 2)),
@@ -1075,7 +1101,7 @@
             jax.ShapeDtypeStruct((nb, 16, wide), f32),
         ),
         in_specs=[vmem, smem, smem, vmem, vmem, vmem, vmem, vmem],
-        out_specs=(vmem, vmem),
+        out_specs=(pl.BlockSpec(memory_space=pl.ANY), vmem),
         scratch_shapes=scratch,
         compiler_params=pltpu.CompilerParams(
             collective_id=0, has_side_effects=True, vmem_limit_bytes=60 * 2**20
@@ -1300,7 +1326,7 @@
 
 
 def collect_kernel(nr, size, *refs):
-    (owner_ref, grad_ref), refs = refs[:2], refs[2:]
+    (owner_ref, blocks_ref), refs = refs[:2], refs[2:]
     ins, refs = refs[:7], refs[7:]
     outs, refs = refs[:9], refs[9:]
     (
@@ -1313,6 +1339,8 @@
         out_buffer,
         copy_buffer,
         gram_buffer,
+        grad_ref,
+        local_sem,
         a_send,
         a_recv,
         b_send,
@@ -1334,6 +1362,8 @@
     def device(chip, core):
         return {"rows": 2 * chip + core, "blk": b}
 
+    stage = pltpu.make_async_copy(blocks_ref, grad_ref, local_sem)
+    stage.start()
     barrier = pltpu.get_barrier_semaphore()
     pl.semaphore_signal(
         barrier, inc=1, device_id={"rows": mate, "blk": b}, device_id_type=MESH
@@ -1551,6 +1581,7 @@
         for copy in loads(chunk):
             copy.start()
     pl.semaphore_wait(barrier, chips)
+    stage.wait()
     for chunk in range(chunks):
         fill_a(chunk)
     for chunk in range(chunks + 2):
@@ -1590,7 +1621,7 @@
         functools.partial(collect_kernel, nr, size),
         out_shape=(shape, jax.ShapeDtypeStruct(shape.shape, bf16)) + (shape,) * 6
         + (jax.ShapeDtypeStruct((count, order // 2, order), f32),),
-        in_specs=[pl.BlockSpec(memory_space=pltpu.SMEM), vmem] + [anywhere] * 7,
+        in_specs=[pl.BlockSpec(memory_space=pltpu.SMEM)] + [anywhere] * 8,
         out_specs=[anywhere] * 9,
         scratch_shapes=[
             pltpu.VMEM((chunks, chips, size) + square, bf16),
@@ -1602,6 +1633,8 @@
             pltpu.VMEM((2, 7, size) + square, f32),
             pltpu.VMEM((2, size) + square, bf16),
             pltpu.VMEM((2, size, order // 2, order), f32),
+            pltpu.VMEM(blocks.shape, bf16),
+            dma(()),
             dma((chunks,)),
             dma((chunks,)),
             dma((chunks, chips)),

time: 399 us -> 392 us (0.982)
  Pallas kernels: 378 us -> 371 us
    pallas_call x1, Pallas kernels: 277 us -> 271 us  [run_step(): pl.pallas_call(functools.partial(step_kernel, nr, nb, cols), out_shape=(j...]
where the time goes in v7:
time: 392 us; the launch traced here: 385 us
  Pallas kernels  371 us (95%)
  local copies, waits for them, and re-layouts  11.3 us (3%)
    pallas_call x1, Pallas kernels, run_step(): pl.pallas_call(functools.partial(step_kernel, nr, nb, cols), out_shape=(j...  271 us
    pallas_call x1, Pallas kernels, soap_update(): pl.pallas_call(functools.partial(collect_kernel, nr, size), out_shape=(sh...  59.6 us
    pallas_call x1, Pallas kernels, new_bases(): pl.pallas_call(basis_kernel, out_shape=[jax.ShapeDtypeStruct(value.shape,...  39.6 us

profile of v7, /device:TPU:1, one launch (start us, length us, event | category | flops | bytes accessed | tf_op | source)
XLA Modules:
  0.0 385.2 jit_solution(5372037652313136110)
XLA Ops:
  0.7 0.7 slice.46
  1.4 0.2 slice.47
  1.6 0.6 pad.9.head_ref
  2.3 1.4 copy.52
  3.7 0.8 copy.62
  4.5 0.8 stack.15
  5.3 0.1 copy.54
  5.4 0.8 stack.16
  6.2 0.1 copy.55
  6.3 0.8 stack.17
  7.1 0.1 copy.56
  7.2 0.6 pad.8.lab_ref
  7.8 0.7 select_reduce_fusion.place_ref
  8.6 271.4 %shard_map.306 = (bf16[320,128,128]{2,1,0:T(8,128)(2,1)}, f32[4,16,256]{2,1,0:T(8,128)}) custom-call(f32[40,128,128]{2,1,0:T(8,128)} %bitcast.38, s32[320]{0:T(512)} %select_reduce_fusion.place_ref, f32[2]{0:T(128)} %bias_ref.1, bf16[96,512]{1,0:T(8,128)(2,1)} %bitcast.50, bf16[2,2,96,512]{3,2,1,0:T(8,128)(2,1)} %bitcast.46, f32[4,8,96]{2,1,0:T(8,128)} %pad.8.lab_ref, ...), custom_call_target="tpu_custom_call" | custom-call | tf_op jit(solution)/shard_map/pallas_call | solution.py:1097
  280.0 59.6 %shard_map.307 = (f32[40,128,128]{2,1,0:T(8,128)}, bf16[40,128,128]{2,1,0:T(8,128)(2,1)}, f32[40,128,128]{2,1,0:T(8,128)}, f32[40,128,128]{2,1,0:T(8,128)}, f32[...) custom-call(s32[320]{0:T(512)} %refs_0_.1, ...), custom_call_target="tpu_custom_call" | custom-call | tf_op jit(solution)/shard_map/pallas_call | solution.py:1620
  339.7 39.6 %shard_map.308 = (f32[40,128,128]{2,1,0:T(8,128)}, f32[40,128,128]{2,1,0:T(8,128)}, f32[40,128,128]{2,1,0:T(8,128)}, bf16[40,128,128]{2,1,0:T(8,128)(2,1)}, f32[...) custom-call(f32[2560,128]{1,0:T(8,128)} %bitcast.48, ...), custom_call_target="tpu_custom_call" | custom-call | tf_op jit(solution)/shard_map/pallas_call | solution.py:1758
  379.3 1.0 fusion.5
  380.3 0.8 slice_bitcast_fusion.1
  381.1 0.1 copy.59
  381.3 0.2 reshape.81
  381.5 0.6 multiply_subtract_fusion
  382.1 0.8 slice_reduce_fusion
  383.0 0.5 multiply_subtract_fusion.1
  383.5 1.2 fusion.6
  (26 shorter events, 0.2 us)
Async XLA Ops:
  0.6 7.2 %copy-start.3 = (s32[320]{0:T(512)S(1)}, s32[320]{0:T(512)}, u32[]{:S(2)}) copy-start(s32[320]{0:T(512)} %refs_0_.1) | copy-start | bytes 3844
  339.6 41.9 %copy-start = (f32[6144]{0:T(1024)S(1)}, f32[6144]{0:T(1024)}, u32[]{:S(2)}) copy-start(f32[6144]{0:T(1024)} %param.32) | copy-start | bytes 73732
  339.6 41.9 %copy-start.1 = (f32[6144]{0:T(1024)S(1)}, f32[6144]{0:T(1024)}, u32[]{:S(2)}) copy-start(f32[6144]{0:T(1024)} %param.34) | copy-start | bytes 73732
  339.6 41.9 %copy-start.2 = (f32[6144]{0:T(1024)S(1)}, f32[6144]{0:T(1024)}, u32[]{:S(2)}) copy-start(f32[6144]{0:T(1024)} %param.33) | copy-start | bytes 73732
  339.7 43.3 %copy-start.4 = (f32[2]{0:T(128)S(1)}, f32[2]{0:T(128)}, u32[]{:S(2)}) copy-start(f32[2]{0:T(128)} %bias_ref.1) | copy-start | bytes 28
  339.7 43.3 %copy-start.5 = (f32[2]{0:T(128)S(1)}, f32[2]{0:T(128)}, u32[]{:S(2)}) copy-start(f32[2]{0:T(128)} %param.37) | copy-start | bytes 28
  339.7 43.3 %copy-start.6 = (f32[2]{0:T(128)S(1)}, f32[2]{0:T(128)}, u32[]{:S(2)}) copy-start(f32[2]{0:T(128)} %param.36) | copy-start | bytes 28

commit v8 on v7

--- a/solution.py
+++ b/solution.py
@@ -62,9 +62,10 @@
     bias_ref,
     image_ref,
     skip_ref,
-    lab_ref,
+    labels_ref,
+    map_ref,
+    valid_ref,
     params_ref,
-    head_ref,
     blocks_ref,
     sums_ref,
     grad_ref,
@@ -542,8 +543,19 @@
     gather = Gather()
     gather.begin()
     x_one[1, b] = image_ref[...]
-    x_skip[1:3, :, b] = skip_ref[...]
-    x_lab[b] = lab_ref[...]
+
+    def pick(shape, dim, stride, start):
+        index = lax.broadcasted_iota(jnp.int32, shape, dim)
+        target = stride * lax.broadcasted_iota(jnp.int32, shape, 1 - dim) + start
+        return jnp.where(index == target, 1.0, 0.0).astype(bf16)
+
+    values = [ref[...].astype(f32) for ref in (labels_ref, map_ref, valid_ref)]
+    values = jnp.concatenate(values + [jnp.zeros_like(values[0])], 0).astype(bf16)
+    for f in range(2):
+        x_lab[b, f] = dot_nn(values, pick((2 * cols, cols), 0, 2, f))
+        for e in range(2):
+            value = dot_nn(pick((cols, 2 * cols), 1, 2, f), skip_ref[e])
+            x_skip[1 + e, f, b] = value.astype(bf16)
     move_image = Exchange(
         0,
         lambda j: x_one.at[1, j],
@@ -632,7 +644,9 @@
     count = 0.0
     for image in range(nb):
         for part in range(4):
-            count = count + jnp.sum(x_lab[image, part, 2:3, :], 1, keepdims=True)
+            line = 4 + part // 2
+            value = x_lab[image, part % 2, line : line + 1, :]
+            count = count + jnp.sum(value, 1, keepdims=True)
     reduce_one[r, 2 * nb : 2 * nb + 1, :] = jnp.broadcast_to(count, (1, wide))
     reduce_start(0, reduce_one)
     arrange(1, w_two)
@@ -721,8 +735,17 @@
         a_three[part, 0, rows_of(image), :] = value
 
     norm_apply(total, z_three, inv_three, gain_three, shift_three, size_high, put_three)
-    head_low = head_ref[...].astype(bf16)
-    head = head_low.astype(f32)
+    pairs = 2 * slim // TILE
+    start = (4 * C1 + 2 * C0) // TILE + b * pairs
+    head = []
+    for number in range(2):
+        total = 0.0
+        for n in range(pairs):
+            value = params_ref[pl.ds(start + n, 1), :].astype(bf16)
+            total = total + dot_nn(value, pick((TILE, slim), 0, 2, number - TILE * n))
+        head.append(total)
+    head = jnp.concatenate(head + [jnp.zeros((6, slim), f32)], 0)
+    head_low = head.astype(bf16)
     for part in range(4):
         for image in range(nb):
             tile = dot_nt(head_low, a_three[part, 0, rows_of(image), :])
@@ -742,8 +765,11 @@
             tile = tile + logit[j, part, two, :]
         first = tile[0:1, :] + bias_ref[0]
         second = tile[1:2, :] + bias_ref[1]
-        label = x_lab[image, part, 0:1, :]
-        scale = x_lab[image, part, 1:2, :] * x_lab[image, part, 2:3, :] * 0.125
+        e, f = part // 2, part % 2
+        label, level_map, counted = [
+            x_lab[image, f, line : line + 1, :] for line in (e, 2 + e, 4 + e)
+        ]
+        scale = counted * level_map * 0.125
         largest = jnp.maximum(first, second)
         log_total = jnp.log(jnp.exp(first - largest) + jnp.exp(second - largest)) + largest
         picked = first * (1.0 - label) + second * label
@@ -1035,7 +1061,7 @@
     last.wait()
 
 
-def run_step(master, place, bias, image, skip, lab, params, head):
+def run_step(master, place, bias, image, skip, labels, weight_map, valid, params):
     nr, nb = lax.axis_size("rows"), lax.axis_size("blk")
     cols = image.shape[0]
     px = nb * cols
@@ -1048,7 +1074,7 @@
         dma((2,)),
         pltpu.VMEM((3, nb, cols, C0), bf16),
         pltpu.VMEM((4, 2, nb, cols, C0), bf16),
-        pltpu.VMEM((nb, 4, 8, cols), f32),
+        pltpu.VMEM((nb, 2, 8, cols), f32),
         pltpu.VMEM((9 * wide, C0), bf16),
         pltpu.VMEM((9 * wide, C1), bf16),
         pltpu.VMEM((4 * slim, C1), bf16),
@@ -1100,13 +1126,13 @@
             jax.ShapeDtypeStruct((place.shape[0],) + master.shape[1:], bf16),
             jax.ShapeDtypeStruct((nb, 16, wide), f32),
         ),
-        in_specs=[vmem, smem, smem, vmem, vmem, vmem, vmem, vmem],
+        in_specs=[vmem, smem, smem] + [vmem] * 6,
         out_specs=(pl.BlockSpec(memory_space=pl.ANY), vmem),
         scratch_shapes=scratch,
         compiler_params=pltpu.CompilerParams(
             collective_id=0, has_side_effects=True, vmem_limit_bytes=60 * 2**20
         ),
-    )(master, place, bias, image, skip, lab, params, head)
+    )(master, place, bias, image, skip, labels, weight_map, valid, params)
 
 
 LANES = 128
@@ -1802,27 +1828,19 @@
     bias_second,
 ):
     shards = lax.axis_size("blk")
-    shard = lax.axis_index("blk")
-    cols = image.shape[2]
     slots = jnp.arange(owner.shape[0])
     place = jnp.sum(jnp.where(owner[None, :] == slots[:, None], slots[None, :], 0), 1)
-    widths = (C1, C1, C1, C1, C0, C0)
-    heads = norm_params[sum(widths) :].reshape(C0, 2)
     part = C0 // shards
-    heads = lax.dynamic_slice_in_dim(heads, shard * part, part).T
-    heads = jnp.pad(heads, ((0, 6), (0, 0)))
-    lab = jnp.stack([labels, weight_map, valid]).astype(f32).reshape(3, 2, cols, 2)
-    lab = jnp.pad(lab.transpose(1, 3, 0, 2).reshape(4, 3, cols), ((0, 0), (0, 5), (0, 0)))
-    skip = skip.reshape(2, cols, 2, C0).transpose(0, 2, 1, 3)
     blocks, sums = run_step(
         master[0],
         place.astype(jnp.int32),
         head_bias,
         image[0, 0],
-        skip,
-        lab,
+        skip[0],
+        labels[0],
+        weight_map[0],
+        valid[0],
         norm_params.reshape(-1, TILE),
-        heads,
     )
     loss_sum, valid_count = sums[0, 6, 0], sums[0, 9, 0]
     grad_bias = sums[0, 7:9, 0]

time: 392 us -> 385 us (0.982)
  local copies, waits for them, and re-layouts: 11.3 us -> 4.13 us
where the time goes in v8:
time: 385 us; the launch traced here: 379 us
  Pallas kernels  371 us (96%)
  local copies, waits for them, and re-layouts  4.13 us (1%)
    pallas_call x1, Pallas kernels, run_step(): pl.pallas_call(functools.partial(step_kernel, nr, nb, cols), out_shape=(j...  271 us
    pallas_call x1, Pallas kernels, soap_update(): pl.pallas_call(functools.partial(collect_kernel, nr, size), out_shape=(sh...  59.7 us
    pallas_call x1, Pallas kernels, new_bases(): pl.pallas_call(basis_kernel, out_shape=[jax.ShapeDtypeStruct(value.shape,...  39.6 us

profile of v8, /device:TPU:1, one launch (start us, length us, event | category | flops | bytes accessed | tf_op | source)
XLA Modules:
  0.0 378.7 jit_solution(2454317222047159194)
XLA Ops:
  0.6 1.4 select_reduce_fusion.place_ref
  2.1 271.4 %shard_map.306 = (bf16[320,128,128]{2,1,0:T(8,128)(2,1)}, f32[4,16,256]{2,1,0:T(8,128)}) custom-call(f32[40,128,128]{2,1,0:T(8,128)} %bitcast.34, s32[320]{0:T(512)} %select_reduce_fusion.place_ref, f32[2]{0:T(128)} %bias_ref.1, bf16[96,512]{1,0:T(8,128)(2,1)} %bitcast.45, bf16[2,192,512]{2,1,0:T(8,128)(2,1)} %bitcast.43, s32[2,192]{1,0:T(2,128)} %bitcast.52, ...), custom_call_target="tpu_custom_call" | custom-call | tf_op jit(solution)/shard_map/pallas_call | solution.py:1123
  273.5 59.7 %shard_map.307 = (f32[40,128,128]{2,1,0:T(8,128)}, bf16[40,128,128]{2,1,0:T(8,128)(2,1)}, f32[40,128,128]{2,1,0:T(8,128)}, f32[40,128,128]{2,1,0:T(8,128)}, f32[...) custom-call(s32[320]{0:T(512)} %refs_0_.1, ...), custom_call_target="tpu_custom_call" | custom-call | tf_op jit(solution)/shard_map/pallas_call | solution.py:1646
  333.2 0.0 copy-start
  333.2 0.0 copy-start.1
  333.2 0.0 copy-start.2
  333.2 0.0 copy-start.3
  333.2 0.0 copy-start.4
  333.2 0.0 copy-start.5
  333.2 39.6 %shard_map.308 = (f32[40,128,128]{2,1,0:T(8,128)}, f32[40,128,128]{2,1,0:T(8,128)}, f32[40,128,128]{2,1,0:T(8,128)}, bf16[40,128,128]{2,1,0:T(8,128)(2,1)}, f32[...) custom-call(f32[2560,128]{1,0:T(8,128)} %bitcast.42, ...), custom_call_target="tpu_custom_call" | custom-call | tf_op jit(solution)/shard_map/pallas_call | solution.py:1784
  372.8 0.9 fusion.4
  373.8 0.8 slice_bitcast_fusion.1
  374.7 0.1 copy.38
  374.8 0.2 reshape.44
  375.0 0.0 copy-done
  375.0 0.0 copy-done.1
  375.0 0.0 copy-done.2
  375.0 0.6 multiply_subtract_fusion
  375.7 0.8 slice_reduce_fusion
  376.5 0.0 copy-done.3
  376.5 0.0 copy-done.4
  376.5 0.0 copy-done.5
  376.5 0.5 multiply_subtract_fusion.1
  377.0 1.2 fusion.5
  (8 shorter events, 0.0 us)
Async XLA Ops:
  333.2 41.9 %copy-start = (f32[6144]{0:T(1024)S(1)}, f32[6144]{0:T(1024)}, u32[]{:S(2)}) copy-start(f32[6144]{0:T(1024)} %param.32) | copy-start | bytes 73732
  333.2 41.8 %copy-start.1 = (f32[6144]{0:T(1024)S(1)}, f32[6144]{0:T(1024)}, u32[]{:S(2)}) copy-start(f32[6144]{0:T(1024)} %param.34) | copy-start | bytes 73732
  333.2 41.8 %copy-start.2 = (f32[6144]{0:T(1024)S(1)}, f32[6144]{0:T(1024)}, u32[]{:S(2)}) copy-start(f32[6144]{0:T(1024)} %param.33) | copy-start | bytes 73732
  333.2 43.3 %copy-start.3 = (f32[2]{0:T(128)S(1)}, f32[2]{0:T(128)}, u32[]{:S(2)}) copy-start(f32[2]{0:T(128)} %bias_ref.1) | copy-start | bytes 28
  333.2 43.3 %copy-start.4 = (f32[2]{0:T(128)S(1)}, f32[2]{0:T(128)}, u32[]{:S(2)}) copy-start(f32[2]{0:T(128)} %param.37) | copy-start | bytes 28
  333.2 43.3 %copy-start.5 = (f32[2]{0:T(128)S(1)}, f32[2]{0:T(128)}, u32[]{:S(2)}) copy-start(f32[2]{0:T(128)} %param.36) | copy-start | bytes 28

commit v9 on v8

--- a/solution.py
+++ b/solution.py
@@ -668,14 +668,15 @@
     arrange(2, w_up)
     for k in range(2, nb):
         move.hop(k)
-    arrange(3, w_three)
     conv_low(z_two, w_two, lambda dy: a_one[dy], (1,))
     move.finish()
     for k in range(middle + 1, nb):
         move_skip.hop(k)
     conv_low(z_two, w_two, lambda dy: a_one[dy], (0, 2), True)
     norm_sums(reduce_two, z_two)
-    total = all_reduce(1, reduce_two)
+    reduce_start(1, reduce_two)
+    arrange(3, w_three)
+    total = reduce_finish(1, reduce_two)
 
     def put_two(part, image, value):
         a_two[rows_of(image), lanes(b, wide)] = value

time: 385 us -> 385 us (level)
  no operation moved by 1% of the time
where the time goes in v9:
time: 385 us; the launch traced here: 379 us
  Pallas kernels  371 us (96%)
  local copies, waits for them, and re-layouts  4.13 us (1%)
    pallas_call x1, Pallas kernels, run_step(): pl.pallas_call(functools.partial(step_kernel, nr, nb, cols), out_shape=(j...  271 us
    pallas_call x1, Pallas kernels, soap_update(): pl.pallas_call(functools.partial(collect_kernel, nr, size), out_shape=(sh...  59.5 us
    pallas_call x1, Pallas kernels, new_bases(): pl.pallas_call(basis_kernel, out_shape=[jax.ShapeDtypeStruct(value.shape,...  39.6 us

profile of v9, /device:TPU:1, one launch (start us, length us, event | category | flops | bytes accessed | tf_op | source)
XLA Modules:
  0.0 378.5 jit_solution(9195718806553152041)
XLA Ops:
  0.6 1.4 select_reduce_fusion.place_ref
  2.1 271.4 %shard_map.306 = (bf16[320,128,128]{2,1,0:T(8,128)(2,1)}, f32[4,16,256]{2,1,0:T(8,128)}) custom-call(f32[40,128,128]{2,1,0:T(8,128)} %bitcast.34, s32[320]{0:T(512)} %select_reduce_fusion.place_ref, f32[2]{0:T(128)} %bias_ref.1, bf16[96,512]{1,0:T(8,128)(2,1)} %bitcast.45, bf16[2,192,512]{2,1,0:T(8,128)(2,1)} %bitcast.43, s32[2,192]{1,0:T(2,128)} %bitcast.52, ...), custom_call_target="tpu_custom_call" | custom-call | tf_op jit(solution)/shard_map/pallas_call | solution.py:1124
  273.5 59.5 %shard_map.307 = (f32[40,128,128]{2,1,0:T(8,128)}, bf16[40,128,128]{2,1,0:T(8,128)(2,1)}, f32[40,128,128]{2,1,0:T(8,128)}, f32[40,128,128]{2,1,0:T(8,128)}, f32[...) custom-call(s32[320]{0:T(512)} %refs_0_.1, ...), custom_call_target="tpu_custom_call" | custom-call | tf_op jit(solution)/shard_map/pallas_call | solution.py:1647
  333.0 0.0 copy-start
  333.0 0.0 copy-start.1
  333.0 0.0 copy-start.2
  333.1 0.0 copy-start.3
  333.1 0.0 copy-start.4
  333.1 0.0 copy-start.5
  333.1 39.6 %shard_map.308 = (f32[40,128,128]{2,1,0:T(8,128)}, f32[40,128,128]{2,1,0:T(8,128)}, f32[40,128,128]{2,1,0:T(8,128)}, bf16[40,128,128]{2,1,0:T(8,128)(2,1)}, f32[...) custom-call(f32[2560,128]{1,0:T(8,128)} %bitcast.42, ...), custom_call_target="tpu_custom_call" | custom-call | tf_op jit(solution)/shard_map/pallas_call | solution.py:1785
  372.7 0.9 fusion.4
  373.7 0.8 slice_bitcast_fusion.1
  374.5 0.1 copy.38
  374.7 0.2 reshape.44
  374.9 0.0 copy-done
  374.9 0.0 copy-done.1
  374.9 0.0 copy-done.2
  374.9 0.6 multiply_subtract_fusion
  375.5 0.8 slice_reduce_fusion
  376.3 0.0 copy-done.3
  376.4 0.0 copy-done.4
  376.4 0.0 copy-done.5
  376.4 0.5 multiply_subtract_fusion.1
  376.9 1.2 fusion.5
  (8 shorter events, 0.0 us)
Async XLA Ops:
  333.0 41.9 %copy-start = (f32[6144]{0:T(1024)S(1)}, f32[6144]{0:T(1024)}, u32[]{:S(2)}) copy-start(f32[6144]{0:T(1024)} %param.32) | copy-start | bytes 73732
  333.0 41.8 %copy-start.1 = (f32[6144]{0:T(1024)S(1)}, f32[6144]{0:T(1024)}, u32[]{:S(2)}) copy-start(f32[6144]{0:T(1024)} %param.34) | copy-start | bytes 73732
  333.0 41.8 %copy-start.2 = (f32[6144]{0:T(1024)S(1)}, f32[6144]{0:T(1024)}, u32[]{:S(2)}) copy-start(f32[6144]{0:T(1024)} %param.33) | copy-start | bytes 73732
  333.1 43.3 %copy-start.3 = (f32[2]{0:T(128)S(1)}, f32[2]{0:T(128)}, u32[]{:S(2)}) copy-start(f32[2]{0:T(128)} %bias_ref.1) | copy-start | bytes 28
  333.1 43.3 %copy-start.4 = (f32[2]{0:T(128)S(1)}, f32[2]{0:T(128)}, u32[]{:S(2)}) copy-start(f32[2]{0:T(128)} %param.37) | copy-start | bytes 28
  333.1 43.3 %copy-start.5 = (f32[2]{0:T(128)S(1)}, f32[2]{0:T(128)}, u32[]{:S(2)}) copy-start(f32[2]{0:T(128)} %param.36) | copy-start | bytes 28
